TPU v7x, 1024 devices: a whole 8x8x8 slice. The times are simulated.
1024 devices in a mesh: fsdp: 128 (over z_lo, y, x), tensor: 8 (over z_hi, core).
Axes of the slice: x: 8, y: 8, z: 8 (z_hi: 4, z_lo: 2; z = z_hi * 2 + z_lo), core: 2. Of those that a mesh axis runs over, the one named last changes fastest.
Arguments:
- tokens: bfloat16 [16384, 16384], P('fsdp', 'tensor'), may hold values from -6 to 6
- seg_ids: int32 [128, 128], P('fsdp'), may hold values from 0 to 7, never falling along the last dimension, each value on 1 to 64 neighbouring positions
- key_weight: bfloat16 [512, 16384], P('fsdp', 'tensor'), may hold values from -0.046875 to 0.046875
- key_grad: bfloat16 [16384, 512], P('fsdp'), may hold values from -24 to 24
Outputs:
- keys: bfloat16 [16384, 512], P('fsdp')
- grad_tokens: bfloat16 [16384, 16384], P('fsdp', 'tensor')
- grad_key_weight: float32 [512, 16384], P('fsdp', 'tensor')
Inputs may be any that keep to these rules, and one draw needn't show every extreme that they name: `seg_ids`: within each window the ids never fall; each document spans 1 to 64 tokens, one exactly 64.
All inputs are finite; a program needn't handle non-finite values.
Results may differ from a plain program's by a relative error of at most 0.0041.
Values may be sent and summed in bfloat16 or wider, within the bound.
No kernel may reach another device: no remote copies, remote signals or barrier semaphores. Data moves between devices by JAX's collectives and lax.ppermute only.
A program may use at most 32 MiB of HBM per device.

v0:
```python
import jax
import jax.numpy as jnp
from jax import lax
from jax.sharding import PartitionSpec as P

HEAD = 128


def doc_positions(segments):
    width = segments.shape[0]
    index = jnp.arange(width, dtype=jnp.int32)
    change = jnp.concatenate([jnp.ones((1,), bool), segments[1:] != segments[:-1]])
    first = lax.cummax(jnp.where(change, index, 0))
    return index - first


def angles(positions, half):
    freq = 500000.0 ** (-2.0 * jnp.arange(half, dtype=jnp.float32) / (2 * half))
    turn = positions.astype(jnp.float32)[:, None] * freq[None, :]
    return (jnp.cos(turn)[:, None, :], jnp.sin(turn)[:, None, :])


def rotate(field, cosine, sine, sign):
    rows = field.shape[0]
    shaped = field.reshape(rows, -1, HEAD)
    first, second = (shaped[..., : HEAD // 2], shaped[..., HEAD // 2 :])
    out = jnp.concatenate(
        [first * cosine - sign * second * sine, second * cosine + sign * first * sine], axis=-1
    )
    return out.reshape(rows, -1)


def body(tokens, seg_ids, key_weight, key_grad):
    cosine, sine = angles(doc_positions(seg_ids[0]), HEAD // 2)
    weights = lax.all_gather(key_weight, "fsdp", axis=0, tiled=True)
    partial_value = lax.dot_general(
        tokens, weights, (((1,), (1,)), ((), ())), preferred_element_type=jnp.float32
    )
    kraw = lax.psum(partial_value, "tensor")
    keys = rotate(kraw, cosine, sine, 1.0).astype(jnp.bfloat16)
    kback = rotate(key_grad.astype(jnp.float32), cosine, sine, -1.0).astype(jnp.bfloat16)
    grad_tokens = jnp.dot(kback, weights, preferred_element_type=jnp.float32)
    grad_key_weight = lax.psum_scatter(
        lax.dot_general(
            kback, tokens, (((0,), (0,)), ((), ())), preferred_element_type=jnp.float32
        ),
        "fsdp",
        scatter_dimension=0,
        tiled=True,
    )
    return (keys, grad_tokens.astype(jnp.bfloat16), grad_key_weight)


def solution(mesh):
    placed = (P("fsdp", "tensor"), P("fsdp", None), P("fsdp", "tensor"), P("fsdp", None))
    return jax.shard_map(
        body,
        mesh=mesh,
        in_specs=placed,
        out_specs=(P("fsdp", None), P("fsdp", "tensor"), P("fsdp", "tensor")),
        check_vma=False,
    )
```

profile of v0, /device:TPU:128, one launch (start us, length us, event | category | flops | bytes accessed | tf_op | source)
XLA Modules:
  0.0 1917.1 jit_solution(10163622980492633496)
XLA Ops:
  7.2 0.0 copy-start
  7.2 0.0 all-gather.3.cloned.1.call-start
  7.2 0.7 all-gather.3.cloned.1.call-update
  7.9 0.0 all-reduce.4.cloned.1.call-start
  8.0 0.8 compare_bitcast_fusion
  8.8 0.1 add_select_fusion
  8.8 0.1 copy.9
  9.0 0.2 reduce-window.8
  9.1 0.1 reduce
  9.3 598.4 %all-gather.3.cloned.1.call-done = bf16[128,4,2048]{2,1,0:T(4,128)(2,1)} async-done(((bf16[1,4,2048]{2,1,0:T(4,128)(2,1)}), bf16[128,4,2048]{2,1,0:T(4,128)(2,1)}) %all-gather.3.cloned.1.call-update) | async-done | bytes 2097168 | tf_op jit(solution)/shard_map/all_gather | solution.py:35
  607.7 2.5 reshape.141
  610.2 0.0 copy-done
  610.2 0.0 copy-start.1
  610.3 0.8 fusion.5
  611.1 0.8 reshape.134
  611.9 0.0 all-reduce.4.cloned.1.call-update
  611.9 0.0 all-reduce.6.cloned.1.call-start
  612.0 0.0 copy-done.1
  612.0 0.1 reshape.139
  612.1 0.3 broadcast_multiply_fusion
  612.4 81.1 %all-reduce.4.cloned.1.call-done = f32[128,4,128]{2,1,0:T(4,128)} async-done(((f32[128,4,128]{2,1,0:T(4,128)}), f32[128,4,128]{2,1,0:T(4,128)}) %all-reduce.4.cloned.1.call-update) | async-done | bytes 262160 | tf_op jit(solution)/shard_map/psum | solution.py:39
  693.5 1.5 subtract_convert_fusion
  695.0 0.4 pad_maximum_fusion
  695.4 2.7 fusion
  698.1 0.0 all-reduce.6.cloned.1.call-update
  698.1 1.3 dynamic-slice
  700.1 0.7 copy.21
  700.7 1.2 convolution_convert_fusion
  702.0 1207.1 %all-reduce.6.cloned.1.call-done = f32[512,2048]{1,0:T(8,128)} async-done(((f32[512,2048]{1,0:T(8,128)}), f32[512,2048]{1,0:T(8,128)}) %all-reduce.6.cloned.1.call-update) | async-done | bytes 4194320
  1909.1 1.5 constant_dynamic-slice_fusion
  (2 shorter events, 0.0 us)
Async XLA Ops:
  7.2 603.1 %copy-start = (bf16[128,2048]{1,0:T(8,128)(2,1)S(1)}, bf16[128,2048]{1,0:T(8,128)(2,1)}, u32[]{:S(2)}) copy-start(bf16[128,2048]{1,0:T(8,128)(2,1)} %param.4) | copy-start | bytes 1572868
  7.2 600.5 %all-gather.3.cloned.1.call-start = ((), (), s32[]{:S(2)}) async-start(), calls=%async_computation.1 | async-start | bytes 2113536 | tf_op jit(solution)/shard_map/all_gather | solution.py:35
  7.9 685.6 %all-reduce.4.cloned.1.call-start = ((), (), s32[]{:S(2)}) async-start(), calls=%async_computation | async-start | bytes 524288 | tf_op jit(solution)/shard_map/psum | solution.py:39
  610.2 1.7 copy-start.1
  611.9 1297.2 %all-reduce.6.cloned.1.call-start = ((), (), s32[]{:S(2)}) async-start(), calls=%async_computation.2 | async-start | bytes 8388608
Sparse Core Ops, SparseCore 0:
  10.7 596.9 all-gather.2
  612.0 81.4 all-reduce.3
  698.2 1210.8 all-reduce.5
where the time goes:
time: 1920 us
  waiting for transfers between devices  1890 us (98%)
    unnamed x4, waiting for transfers between devices  1210 us
    all_gather x1, waiting for transfers between devices, body(): weights = lax.all_gather(key_weight, 'fsdp', axis=0, tiled=True)  598 us
    psum x1, waiting for transfers between devices, body(): kraw = lax.psum(partial_value, 'tensor')  81.1 us
  transfers between devices with their start and end apart: 3, of which 3 were waited for; matrix products, arithmetic and copies ran while one was open for 0% of the time, Pallas kernels for 0%

commit v1 on v0

v1 whole, which is shorter than its diff:
```python
import jax
import jax.numpy as jnp
from jax import lax
from jax.sharding import Mesh, PartitionSpec as P

HEAD = 128
SWAP = ((0, 1), (1, 0))


def doc_positions(segments):
    width = segments.shape[0]
    index = jnp.arange(width, dtype=jnp.int32)
    change = jnp.concatenate([jnp.ones((1,), bool), segments[1:] != segments[:-1]])
    first = lax.cummax(jnp.where(change, index, 0))
    return index - first


def angles(positions, half):
    freq = 500000.0 ** (-2.0 * jnp.arange(half, dtype=jnp.float32) / (2 * half))
    turn = positions.astype(jnp.float32)[:, None] * freq[None, :]
    return (jnp.cos(turn)[:, None, :], jnp.sin(turn)[:, None, :])


def rotate(field, cosine, sine, sign):
    rows = field.shape[0]
    shaped = field.reshape(rows, -1, HEAD)
    first, second = (shaped[..., : HEAD // 2], shaped[..., HEAD // 2 :])
    out = jnp.concatenate(
        [first * cosine - sign * second * sine, second * cosine + sign * first * sine], axis=-1
    )
    return out.reshape(rows, -1)


def dot(a, b, da, db):
    return lax.dot_general(a, b, (((da,), (db,)), ((), ())), preferred_element_type=jnp.float32)


def body(tokens, seg_ids, key_weight, key_grad):
    bf16 = jnp.bfloat16
    zl = lax.axis_index("zl")
    t = lax.axis_index("zh") * 2 + lax.axis_index("c")
    spread = jnp.broadcast_to(key_weight[None], (64, 4, 2048))
    gathered = lax.all_to_all(spread, ("y", "x"), 0, 0)
    tok_p = lax.ppermute(tokens, "zl", SWAP)

    cosine, sine = angles(doc_positions(seg_ids[0]), HEAD // 2)
    kback = rotate(key_grad.astype(jnp.float32), cosine, sine, -1.0).astype(bf16)
    left, right = kback[:, :256], kback[:, 256:]
    kb_p = lax.ppermute(jnp.where(zl == 0, right, left), "zl", SWAP)
    kb = jnp.where(zl == 0, left, right)

    partial = (dot(kb, tokens, 0, 0) + dot(kb_p, tok_p, 0, 0)).astype(bf16)
    gathered, partial = lax.optimization_barrier((gathered, partial))
    scattered = lax.all_to_all(partial.reshape(64, 4, 2048), ("y", "x"), 0, 0)

    weights = gathered.reshape(256, 2048)
    k_own = dot(tokens, weights, 1, 1).astype(bf16)
    k_par = dot(tok_p, weights, 1, 1).astype(bf16)
    ks = jnp.where(zl == 0, jnp.stack([k_own, k_par]), jnp.stack([k_par, k_own]))
    ks = lax.all_to_all(ks.reshape(16, 16, 256), ("zl", "zh", "c"), 0, 0)

    g_par = lax.ppermute(dot(kb_p, weights, 1, 0).astype(bf16), "zl", SWAP)
    grad_tokens = (dot(kb, weights, 1, 0) + g_par.astype(jnp.float32)).astype(bf16)

    kraw = jnp.sum(ks.reshape(2, 8, 16, 256).astype(jnp.float32), axis=1)
    kraw = kraw.transpose(1, 0, 2).reshape(16, 512)
    own_cos = lax.dynamic_slice_in_dim(cosine, t * 16, 16, 0)
    own_sin = lax.dynamic_slice_in_dim(sine, t * 16, 16, 0)
    keys = rotate(kraw, own_cos, own_sin, 1.0).astype(bf16)
    keys = lax.all_to_all(jnp.broadcast_to(keys[None], (8, 16, 512)), ("zh", "c"), 0, 0)
    keys = keys.reshape(128, 512)

    grad_key_weight = jnp.sum(scattered.astype(jnp.float32), axis=0)
    return keys, grad_tokens, grad_key_weight


def solution(mesh):
    fine = Mesh(mesh.devices.reshape(2, 8, 8, 4, 2), ("zl", "y", "x", "zh", "c"))
    fsdp, tensor = ("zl", "y", "x"), ("zh", "c")
    placed = (P(fsdp, tensor), P(fsdp, None), P(fsdp, tensor), P(fsdp, None))
    return jax.shard_map(
        body,
        mesh=fine,
        in_specs=placed,
        out_specs=(P(fsdp, None), P(fsdp, tensor), P(fsdp, tensor)),
        check_vma=False,
    )
```

time: 1920 us -> 131 us (0.07)
  the two profiles are of different devices: /device:TPU:128 before, /device:TPU:32 now
where the time goes in v1:
time: 131 us; the launch traced here: 130 us
  waiting for transfers between devices  64.3 us (49%)
  starting transfers between devices  50.8 us (39%)
  local copies, waits for them, and re-layouts  5.62 us (4%)
  matrix products  4.59 us (4%)
  other arithmetic  4.06 us (3%)
    all_to_all x1, waiting for transfers between devices, body(): gathered = lax.all_to_all(spread, ('y', 'x'), 0, 0)  20.9 us
    all_to_all x1, starting transfers between devices, body(): ks = lax.all_to_all(ks.reshape(16, 16, 256), ('zl', 'zh', 'c'), 0, 0)  15 us
    all_to_all x1, waiting for transfers between devices, body(): scattered = lax.all_to_all(partial.reshape(64, 4, 2048), ('y', 'x'), 0, 0)  14 us
    all_to_all x1, starting transfers between devices, body(): gathered = lax.all_to_all(spread, ('y', 'x'), 0, 0)  13.8 us
    ppermute x1, waiting for transfers between devices, body(): g_par = lax.ppermute(dot(kb_p, weights, 1, 0).astype(bf16), 'zl', SWAP)  10.9 us
    all_to_all x1, waiting for transfers between devices, body(): ks = lax.all_to_all(ks.reshape(16, 16, 256), ('zl', 'zh', 'c'), 0, 0)  8.89 us
    all_to_all x1, waiting for transfers between devices, body(): lax.all_to_all(jnp.broadcast_to(keys[None], (8, 16, 512)), ('zh', 'c'), 0...  7.79 us
    all_to_all x1, starting transfers between devices, body(): scattered = lax.all_to_all(partial.reshape(64, 4, 2048), ('y', 'x'), 0, 0)  5.95 us
  transfers between devices with their start and end apart: 7, of which 6 were waited for; matrix products, arithmetic and copies ran while one was open for 6% of the time, Pallas kernels for 0%

profile of v1, /device:TPU:32, one launch (start us, length us, event | category | flops | bytes accessed | tf_op | source)
XLA Modules:
  0.0 130.2 jit_solution(16063561989052701274)
XLA Ops:
  0.6 0.0 copy-start.3
  0.6 0.0 copy-start.2
  0.7 5.3 %collective-permute-start.1 = (bf16[128,2048]{1,0:T(8,128)(2,1)}, bf16[128,2048]{1,0:T(8,128)(2,1)S(1)}, u32[]{:S(2)}, u32[]{:S(2)}) collective-permute-start(bf16[128,2048]{1,0:T(8,128)(2,1)} %param.4), channel_id=1, source_target_pairs={{0,512},{512,0},{1,513},{513,1},{2,514},{514,2},{3,515},{515,3},{4... | collective-permute-start | bytes 1572872 | tf_op jit(solution)/shard_map/ppermute | solution.py:44
  6.0 2.2 %broadcast_in_dim.8 = bf16[64,4,2048]{2,1,0:T(4,128)(2,1)} broadcast(bf16[4,2048]{1,0:T(4,128)(2,1)} %param.6), dimensions={1,2} | broadcast | bytes 1064960 | tf_op jit(solution)/shard_map/broadcast_in_dim | solution.py:42
  8.2 0.0 copy-start.1
  8.2 13.8 %all-to-all-start = ((bf16[64,4,2048]{2,1,0:T(4,128)(2,1)}), bf16[64,4,2048]{2,1,0:T(4,128)(2,1)S(1)}, u32[]{:S(2)}, u32[]{:S(2)}) async-start(bf16[64,4,2048]{2,1,0:T(4,128)(2,1)} %broadcast_in_dim.8), calls=%async_computation | async-start | bytes 2097152 | tf_op jit(solution)/shard_map/all_to_all | solution.py:43
  22.0 0.0 copy-done.3
  22.0 0.1 compare_bitcast_fusion
  22.1 0.1 add_select_fusion
  22.2 0.1 copy.10
  22.3 0.0 copy-done.2
  22.3 0.1 reshape.165
  22.4 0.2 reduce-window.8
  22.5 0.1 reduce
  22.7 0.3 multiply_sine_fusion
  23.0 0.3 subtract_convert_fusion
  23.3 0.2 pad_maximum_fusion
  23.5 3.9 %collective-permute-start = (bf16[128,256]{1,0:T(8,128)(2,1)S(1)}, bf16[128,256]{1,0:T(8,128)(2,1)S(1)}, u32[]{:S(2)}, u32[]{:S(2)}) collective-permute-start(bf16[128,256]{1,0:T(8,128)(2,1)S(1)} %broadcast_select_fusion), channel_id=1, source_target_pairs={{0,512},{512,0},{1,513},{513,1},{2,514},{514,2},{3,515},{515,3},{4... | collective-permute-start | bytes 196616 | tf_op jit(solution)/shard_map/ppermute | solution.py:49
  27.5 0.0 copy-done.1
  27.5 0.5 fusion.4
  27.9 1.8 %collective-permute-done = bf16[128,256]{1,0:T(8,128)(2,1)S(1)} collective-permute-done((bf16[128,256]{1,0:T(8,128)(2,1)S(1)}, bf16[128,256]{1,0:T(8,128)(2,1)S(1)}, u32[]{:S(2)}, u32[]{:S(2)}) %collective-permute-start) | collective-permute-done | bytes 65568 | tf_op jit(solution)/shard_map/ppermute | solution.py:49
  29.7 0.0 collective-permute-done.1
  29.7 0.0 copy-start
  29.7 0.5 fusion
  30.2 0.3 copy-done
  30.5 20.9 %all-to-all-done = bf16[64,4,2048]{2,1,0:T(4,128)(2,1)S(1)} async-done(((bf16[64,4,2048]{2,1,0:T(4,128)(2,1)}), bf16[64,4,2048]{2,1,0:T(4,128)(2,1)S(1)}, u32[]{:S(2)}, u32[]{:S(2)}) %all-to-all-start) | async-done | bytes 1048608 | tf_op jit(solution)/shard_map/all_to_all | solution.py:43
  51.4 0.3 reshape.161
  51.7 1.5 %fusion.1 = bf16[1,128,256]{2,1,0:T(8,128)(2,1)S(1)} fusion(bf16[256,2048]{1,0:T(8,128)(2,1)S(1)} %reshape.161, bf16[128,2048]{1,0:T(8,128)(2,1)} %param.4), kind=kOutput, calls=%fused_computation.6 | convolution fusion | flops 134250496 | bytes 1638400 | tf_op jit(solution)/shard_map/dot_general | solution.py:35
  53.2 1.5 %fusion.2 = bf16[1,128,256]{2,1,0:T(8,128)(2,1)S(1)} fusion(bf16[256,2048]{1,0:T(8,128)(2,1)S(1)} %reshape.161, bf16[128,2048]{1,0:T(8,128)(2,1)} %copy-done), kind=kOutput, calls=%fused_computation.7 | convolution fusion | flops 134250496 | bytes 1638400 | tf_op jit(solution)/shard_map/dot_general | solution.py:35
  54.8 0.7 maximum_select_fusion
  55.4 15.0 %all-to-all-start.1 = ((bf16[16,16,256]{2,1,0:T(8,128)(2,1)}), bf16[16,16,256]{2,1,0:T(8,128)(2,1)S(1)}, u32[]{:S(2)}, u32[]{:S(2)}) async-start(bf16[16,16,256]{2,1,0:T(8,128)(2,1)} %bitcast.7), calls=%async_computation.1 | async-start | bytes 262144 | tf_op jit(solution)/shard_map/all_to_all | solution.py:60
  70.4 8.9 %all-to-all-done.1 = bf16[16,16,256]{2,1,0:T(8,128)(2,1)S(1)} async-done(((bf16[16,16,256]{2,1,0:T(8,128)(2,1)}), bf16[16,16,256]{2,1,0:T(8,128)(2,1)S(1)}, u32[]{:S(2)}, u32[]{:S(2)}) %all-to-all-start.1) | async-done | bytes 131104 | tf_op jit(solution)/shard_map/all_to_all | solution.py:60
  79.4 0.1 subtract_convert_fusion.1
  79.5 0.1 pad_maximum_fusion.1
  79.6 0.7 broadcast_in_dim.10
  80.3 3.4 %all-to-all-start.2 = ((bf16[8,16,512]{2,1,0:T(8,128)(2,1)}), bf16[8,16,512]{2,1,0:T(8,128)(2,1)S(1)}, u32[]{:S(2)}, u32[]{:S(2)}) async-start(bf16[8,16,512]{2,1,0:T(8,128)(2,1)} %broadcast_in_dim.10), calls=%async_computation.2 | async-start | bytes 262144 | tf_op jit(solution)/shard_map/all_to_all | solution.py:70
  83.7 1.2 reshape.163
  84.9 7.8 %all-to-all-done.2 = bf16[8,16,512]{2,1,0:T(8,128)(2,1)S(1)} async-done(((bf16[8,16,512]{2,1,0:T(8,128)(2,1)}), bf16[8,16,512]{2,1,0:T(8,128)(2,1)S(1)}, u32[]{:S(2)}, u32[]{:S(2)}) %all-to-all-start.2) | async-done | bytes 131104 | tf_op jit(solution)/shard_map/all_to_all | solution.py:70
  92.7 5.9 %all-to-all-start.3 = ((bf16[64,4,2048]{2,1,0:T(4,128)(2,1)}), bf16[64,4,2048]{2,1,0:T(4,128)(2,1)S(1)}, u32[]{:S(2)}, u32[]{:S(2)}) async-start(bf16[64,4,2048]{2,1,0:T(4,128)(2,1)} %reshape.163), calls=%async_computation.3 | async-start | bytes 2097152 | tf_op jit(solution)/shard_map/all_to_all | solution.py:54
  98.6 0.3 convolution_convert_fusion
  98.9 3.4 %collective-permute-start.2 = (bf16[128,2048]{1,0:T(8,128)(2,1)S(1)}, bf16[128,2048]{1,0:T(8,128)(2,1)S(1)}, u32[]{:S(2)}, u32[]{:S(2)}) collective-permute-start(bf16[128,2048]{1,0:T(8,128)(2,1)S(1)} %convolution_convert_fusion), channel_id=1, source_target_pairs={{0,512},{512,0},{1,513},{513,1},{2,514},{514,2},{3,515},{515,3},{4... | collective-permute-start | bytes 1572872 | tf_op jit(solution)/shard_map/ppermute | solution.py:62
  102.4 0.3 fusion.3
  102.7 10.9 %collective-permute-done.2 = bf16[128,2048]{1,0:T(8,128)(2,1)S(1)} collective-permute-done((bf16[128,2048]{1,0:T(8,128)(2,1)S(1)}, bf16[128,2048]{1,0:T(8,128)(2,1)S(1)}, u32[]{:S(2)}, u32[]{:S(2)}) %collective-permute-start.2) | collective-permute-done | bytes 524320 | tf_op jit(solution)/shard_map/ppermute | solution.py:62
  113.6 0.9 add_convert_fusion
  114.5 14.0 %all-to-all-done.3 = bf16[64,4,2048]{2,1,0:T(4,128)(2,1)S(1)} async-done(((bf16[64,4,2048]{2,1,0:T(4,128)(2,1)}), bf16[64,4,2048]{2,1,0:T(4,128)(2,1)S(1)}, u32[]{:S(2)}, u32[]{:S(2)}) %all-to-all-start.3) | async-done | bytes 1048608 | tf_op jit(solution)/shard_map/all_to_all | solution.py:54
  128.5 1.1 convert_reduce_fusion
  129.6 0.7 copy.19
  (9 shorter events, 0.1 us)
Async XLA Ops:
  0.6 21.4 %copy-start.3 = (s32[1,128]{1,0:T(1,128)S(1)}, s32[1,128]{1,0:T(1,128)}, u32[]{:S(2)}) copy-start(s32[1,128]{1,0:T(1,128)} %param.5) | copy-start | bytes 1540
  0.6 21.6 %copy-start.2 = (bf16[128,512]{1,0:T(8,128)(2,1)S(1)}, bf16[128,512]{1,0:T(8,128)(2,1)}, u32[]{:S(2)}) copy-start(bf16[128,512]{1,0:T(8,128)(2,1)} %param.7) | copy-start | bytes 393220
  0.7 29.0 %collective-permute-start.1 = (bf16[128,2048]{1,0:T(8,128)(2,1)}, bf16[128,2048]{1,0:T(8,128)(2,1)S(1)}, u32[]{:S(2)}, u32[]{:S(2)}) collective-permute-start(bf16[128,2048]{1,0:T(8,128)(2,1)} %param.4), channel_id=1, source_target_pairs={{0,512},{512,0},{1,513},{513,1},{2,514},{514,2},{3,515},{515,3},{4... | collective-permute-start | bytes 1572872 | tf_op jit(solution)/shard_map/ppermute | solution.py:44
  8.2 19.3 %copy-start.1 = (bf16[128,2048]{1,0:T(8,128)(2,1)S(1)}, bf16[128,2048]{1,0:T(8,128)(2,1)}, u32[]{:S(2)}) copy-start(bf16[128,2048]{1,0:T(8,128)(2,1)} %param.4) | copy-start | bytes 1572868
  8.2 43.2 %all-to-all-start = ((bf16[64,4,2048]{2,1,0:T(4,128)(2,1)}), bf16[64,4,2048]{2,1,0:T(4,128)(2,1)S(1)}, u32[]{:S(2)}, u32[]{:S(2)}) async-start(bf16[64,4,2048]{2,1,0:T(4,128)(2,1)} %broadcast_in_dim.8), calls=%async_computation | async-start | bytes 2097152 | tf_op jit(solution)/shard_map/all_to_all | solution.py:43
  23.5 6.2 %collective-permute-start = (bf16[128,256]{1,0:T(8,128)(2,1)S(1)}, bf16[128,256]{1,0:T(8,128)(2,1)S(1)}, u32[]{:S(2)}, u32[]{:S(2)}) collective-permute-start(bf16[128,256]{1,0:T(8,128)(2,1)S(1)} %broadcast_select_fusion), channel_id=1, source_target_pairs={{0,512},{512,0},{1,513},{513,1},{2,514},{514,2},{3,515},{515,3},{4... | collective-permute-start | bytes 196616 | tf_op jit(solution)/shard_map/ppermute | solution.py:49
  29.7 0.8 copy-start
  55.4 23.9 %all-to-all-start.1 = ((bf16[16,16,256]{2,1,0:T(8,128)(2,1)}), bf16[16,16,256]{2,1,0:T(8,128)(2,1)S(1)}, u32[]{:S(2)}, u32[]{:S(2)}) async-start(bf16[16,16,256]{2,1,0:T(8,128)(2,1)} %bitcast.7), calls=%async_computation.1 | async-start | bytes 262144 | tf_op jit(solution)/shard_map/all_to_all | solution.py:60
  80.3 12.4 %all-to-all-start.2 = ((bf16[8,16,512]{2,1,0:T(8,128)(2,1)}), bf16[8,16,512]{2,1,0:T(8,128)(2,1)S(1)}, u32[]{:S(2)}, u32[]{:S(2)}) async-start(bf16[8,16,512]{2,1,0:T(8,128)(2,1)} %broadcast_in_dim.10), calls=%async_computation.2 | async-start | bytes 262144 | tf_op jit(solution)/shard_map/all_to_all | solution.py:70
  92.7 35.8 %all-to-all-start.3 = ((bf16[64,4,2048]{2,1,0:T(4,128)(2,1)}), bf16[64,4,2048]{2,1,0:T(4,128)(2,1)S(1)}, u32[]{:S(2)}, u32[]{:S(2)}) async-start(bf16[64,4,2048]{2,1,0:T(4,128)(2,1)} %reshape.163), calls=%async_computation.3 | async-start | bytes 2097152 | tf_op jit(solution)/shard_map/all_to_all | solution.py:54
  98.9 14.6 %collective-permute-start.2 = (bf16[128,2048]{1,0:T(8,128)(2,1)S(1)}, bf16[128,2048]{1,0:T(8,128)(2,1)S(1)}, u32[]{:S(2)}, u32[]{:S(2)}) collective-permute-start(bf16[128,2048]{1,0:T(8,128)(2,1)S(1)} %convolution_convert_fusion), channel_id=1, source_target_pairs={{0,512},{512,0},{1,513},{513,1},{2,514},{514,2},{3,515},{515,3},{4... | collective-permute-start | bytes 1572872 | tf_op jit(solution)/shard_map/ppermute | solution.py:62

commit v2 on v1

v2 whole, which is shorter than its diff:
```python
import jax
import jax.numpy as jnp
from jax import lax
from jax.sharding import Mesh, PartitionSpec as P

HEAD = 128
SWAP = ((0, 1), (1, 0))


def doc_positions(segments):
    index = jnp.arange(segments.shape[0], dtype=jnp.int32)
    return index - jnp.sum((segments[None, :] < segments[:, None]).astype(jnp.int32), axis=1)


def angles(positions, half):
    freq = 500000.0 ** (-2.0 * jnp.arange(half, dtype=jnp.float32) / (2 * half))
    turn = positions.astype(jnp.float32)[:, None] * freq[None, :]
    return (jnp.cos(turn)[:, None, :], jnp.sin(turn)[:, None, :])


def rotate(field, cosine, sine, sign):
    rows = field.shape[0]
    shaped = field.reshape(rows, -1, HEAD)
    first, second = (shaped[..., : HEAD // 2], shaped[..., HEAD // 2 :])
    out = jnp.concatenate(
        [first * cosine - sign * second * sine, second * cosine + sign * first * sine], axis=-1
    )
    return out.reshape(rows, -1)


def dot(a, b, da, db):
    return lax.dot_general(a, b, (((da,), (db,)), ((), ())), preferred_element_type=jnp.float32)


def body(tokens, seg_ids, key_weight, key_grad):
    bf16, f32 = jnp.bfloat16, jnp.float32
    zl, core = lax.axis_index("zl"), lax.axis_index("c")
    spread = jnp.broadcast_to(key_weight[None], (64, 4, 2048))
    gathered = lax.all_to_all(spread, ("y", "x"), 0, 0)
    tok_p = lax.ppermute(tokens, "zl", SWAP)

    cosine, sine = angles(doc_positions(seg_ids[0]), HEAD // 2)
    kback = rotate(key_grad.astype(f32), cosine, sine, -1.0).astype(bf16)
    left, right = kback[:, :256], kback[:, 256:]
    kb_p = lax.ppermute(jnp.where(zl == 0, right, left), "zl", SWAP)
    kb = jnp.where(zl == 0, left, right)

    partial = (dot(kb, tokens, 0, 0) + dot(kb_p, tok_p, 0, 0)).astype(bf16)

    weights = gathered.reshape(256, 2048)
    k_own, k_par = dot(tokens, weights, 1, 1), dot(tok_p, weights, 1, 1)
    mine = core * 64
    other = 64 - mine
    cut = lambda field, at: lax.dynamic_slice_in_dim(field, at, 64, 0)
    keep = cut(k_own, mine)
    to_c, to_z, to_d = cut(k_own, other), cut(k_par, mine), cut(k_par, other)
    to_c, to_z, to_d = to_c.astype(bf16), to_z.astype(bf16), to_d.astype(bf16)
    to_c, to_z, to_d, partial = lax.optimization_barrier((to_c, to_z, to_d, partial))
    from_z = lax.ppermute(to_z, "zl", SWAP)
    from_d = lax.ppermute(to_d, ("zl", "c"), ((0, 3), (1, 2), (2, 1), (3, 0)))
    from_c = lax.ppermute(to_c, "c", SWAP)
    scattered = lax.all_to_all(partial.reshape(64, 4, 2048), ("y", "x"), 0, 0)

    g_par = lax.ppermute(dot(kb_p, weights, 1, 0).astype(bf16), "zl", SWAP)
    grad_tokens = (dot(kb, weights, 1, 0) + g_par.astype(f32)).astype(bf16)

    near = keep + from_c.astype(f32)
    far = from_z.astype(f32) + from_d.astype(f32)
    total = jnp.where(zl == 0, jnp.concatenate([near, far], 1), jnp.concatenate([far, near], 1))
    total_b = total.astype(bf16)
    one, three, two = (
        lax.ppermute(total_b, "zh", [(i, (i + step) % 4) for i in range(4)]).astype(f32)
        for step in (1, 3, 2)
    )
    total = (total_b.astype(f32) + two) + (one + three)
    own_cos, own_sin = cut(cosine, mine), cut(sine, mine)
    keys = rotate(total, own_cos, own_sin, 1.0).astype(bf16)
    others = lax.ppermute(keys, "c", SWAP)
    keys = jnp.where(core == 0, jnp.concatenate([keys, others]), jnp.concatenate([others, keys]))

    grad_key_weight = jnp.sum(scattered.astype(f32), axis=0)
    return keys, grad_tokens, grad_key_weight


def solution(mesh):
    fine = Mesh(mesh.devices.reshape(2, 8, 8, 4, 2), ("zl", "y", "x", "zh", "c"))
    fsdp, tensor = ("zl", "y", "x"), ("zh", "c")
    placed = (P(fsdp, tensor), P(fsdp, None), P(fsdp, tensor), P(fsdp, None))
    return jax.shard_map(
        body,
        mesh=fine,
        in_specs=placed,
        out_specs=(P(fsdp, None), P(fsdp, tensor), P(fsdp, tensor)),
        check_vma=False,
    )
```

time: 131 us -> 114 us (0.87)
  the two profiles are of different devices: /device:TPU:32 before, /device:TPU:1 now
where the time goes in v2:
time: 114 us; the launch traced here: 113 us
  starting transfers between devices  71.8 us (63%)
  waiting for transfers between devices  20.5 us (18%)
  other arithmetic  7.19 us (6%)
  local copies, waits for them, and re-layouts  6.89 us (6%)
  matrix products  5.66 us (5%)
    ppermute x3, starting transfers between devices, body(): lax.ppermute(total_b, 'zh', [(i, (i + step) % 4) for i in range(4)])  21.1 us
    all_to_all x1, starting transfers between devices, body(): gathered = lax.all_to_all(spread, ('y', 'x'), 0, 0)  14.3 us
    ppermute x1, starting transfers between devices, body(): from_z = lax.ppermute(to_z, 'zl', SWAP)  9.1 us
    ppermute x1, waiting for transfers between devices, body(): kb_p = lax.ppermute(jnp.where(zl == 0, right, left), 'zl', SWAP)  6.3 us
    all_to_all x1, starting transfers between devices, body(): scattered = lax.all_to_all(partial.reshape(64, 4, 2048), ('y', 'x'), 0, 0)  6.26 us
    all_to_all x1, waiting for transfers between devices, body(): gathered = lax.all_to_all(spread, ('y', 'x'), 0, 0)  6.15 us
    ppermute x1, waiting for transfers between devices, body(): g_par = lax.ppermute(dot(kb_p, weights, 1, 0).astype(bf16), 'zl', SWAP)  5.88 us
    dot_general x6, matrix products, dot(): lax.dot_general(a, b, (((da,), (db,)), ((), ())), preferred_element_type=...  5.66 us
  transfers between devices with their start and end apart: 12, of which 5 were waited for; matrix products, arithmetic and copies ran while one was open for 9% of the time, Pallas kernels for 0%

profile of v2, /device:TPU:1, one launch (start us, length us, event | category | flops | bytes accessed | tf_op | source)
XLA Modules:
  0.0 113.0 jit_solution(2353485353455493657)
XLA Ops:
  0.6 0.0 copy-start
  0.6 0.0 copy-start.4
  0.7 0.0 copy-start.5
  0.7 2.3 %broadcast_in_dim.2 = bf16[64,4,2048]{2,1,0:T(4,128)(2,1)} broadcast(bf16[4,2048]{1,0:T(4,128)(2,1)} %param.6), dimensions={1,2} | broadcast | bytes 1064960 | tf_op jit(solution)/shard_map/broadcast_in_dim | solution.py:38
  2.9 14.3 %all-to-all-start = ((bf16[64,4,2048]{2,1,0:T(4,128)(2,1)}), bf16[64,4,2048]{2,1,0:T(4,128)(2,1)}, u32[]{:S(2)}, u32[]{:S(2)}) async-start(bf16[64,4,2048]{2,1,0:T(4,128)(2,1)} %broadcast_in_dim.2), calls=%async_computation | async-start | bytes 2097152 | tf_op jit(solution)/shard_map/all_to_all | solution.py:39
  17.2 0.0 copy-done
  17.3 4.9 %collective-permute-start = (bf16[128,2048]{1,0:T(8,128)(2,1)S(1)}, bf16[128,2048]{1,0:T(8,128)(2,1)}, u32[]{:S(2)}, u32[]{:S(2)}) collective-permute-start(bf16[128,2048]{1,0:T(8,128)(2,1)S(1)} %copy-done), channel_id=1, source_target_pairs={{0,512},{512,0},{1,513},{513,1},{2,514},{514,2},{3,515},{515,3},{4... | collective-permute-start | bytes 1572872 | tf_op jit(solution)/shard_map/ppermute | solution.py:40
  22.2 0.0 copy-done.4
  22.2 0.1 reshape.96
  22.3 0.0 copy-done.5
  22.3 0.2 convert_reduce_fusion.1
  22.5 1.0 multiply_sine_fusion
  23.4 0.3 subtract_convert_fusion
  23.7 0.2 pad_maximum_fusion
  24.0 1.9 %collective-permute-start.1 = (bf16[128,256]{1,0:T(8,128)(2,1)S(1)}, bf16[128,256]{1,0:T(8,128)(2,1)S(1)}, u32[]{:S(2)}, u32[]{:S(2)}) collective-permute-start(bf16[128,256]{1,0:T(8,128)(2,1)S(1)} %broadcast_select_fusion), channel_id=1, source_target_pairs={{0,512},{512,0},{1,513},{513,1},{2,514},{514,2},{3,515},{515,3},{4... | collective-permute-start | bytes 196616 | tf_op jit(solution)/shard_map/ppermute | solution.py:45
  25.9 0.5 fusion.3
  26.4 6.3 %collective-permute-done.1 = bf16[128,256]{1,0:T(8,128)(2,1)S(1)} collective-permute-done((bf16[128,256]{1,0:T(8,128)(2,1)S(1)}, bf16[128,256]{1,0:T(8,128)(2,1)S(1)}, u32[]{:S(2)}, u32[]{:S(2)}) %collective-permute-start.1) | collective-permute-done | bytes 65568 | tf_op jit(solution)/shard_map/ppermute | solution.py:45
  32.7 0.0 collective-permute-done
  32.7 1.5 %fusion = bf16[256,2048]{1,0:T(8,128)(2,1)S(1)} fusion(f32[256,2048]{1,0:T(8,128)S(1)} %fusion.3, bf16[128,256]{1,0:T(8,128)(2,1)S(1)} %collective-permute-done.1, bf16[128,2048]{1,0:T(8,128)(2,1)} %collective-permute-done), kind=kOutput, calls=%fused_computation.1 | convolution fusion | flops 135266304 | bytes 3735552 | tf_op jit(solution)/shard_map/dot_general | solution.py:32
  34.2 6.1 %all-to-all-done = bf16[64,4,2048]{2,1,0:T(4,128)(2,1)} async-done(((bf16[64,4,2048]{2,1,0:T(4,128)(2,1)}), bf16[64,4,2048]{2,1,0:T(4,128)(2,1)}, u32[]{:S(2)}, u32[]{:S(2)}) %all-to-all-start) | async-done | bytes 1048608 | tf_op jit(solution)/shard_map/all_to_all | solution.py:39
  40.3 1.3 %reshape.90 = bf16[256,2048]{1,0:T(8,128)(2,1)S(1)} reshape(bf16[64,4,2048]{2,1,0:T(4,128)(2,1)} %all-to-all-done) | data formatting | bytes 2097152 | tf_op jit(solution)/shard_map/reshape | solution.py:50
  41.7 0.0 copy-start.1
  41.7 1.6 %fusion.4 = f32[128,256]{1,0:T(8,128)S(1)} fusion(bf16[128,2048]{1,0:T(8,128)(2,1)} %param.4, bf16[256,2048]{1,0:T(8,128)(2,1)S(1)} %reshape.90), kind=kOutput, calls=%fused_computation.34 | convolution fusion | flops 134217728 | bytes 1703936 | tf_op jit(solution)/shard_map/dot_general | solution.py:32
  43.2 0.6 dynamic-slice_convert_fusion.2
  43.9 1.5 %fusion.5 = bf16[128,256]{1,0:T(8,128)(2,1)S(1)} fusion(bf16[128,2048]{1,0:T(8,128)(2,1)} %collective-permute-done, bf16[256,2048]{1,0:T(8,128)(2,1)S(1)} %reshape.90), kind=kOutput, calls=%fused_computation.35 | convolution fusion | flops 134217728 | bytes 1638400 | tf_op jit(solution)/shard_map/dot_general | solution.py:32
  45.4 0.6 dynamic-slice_convert_fusion
  46.0 9.1 %collective-permute-start.3 = (bf16[64,256]{1,0:T(8,128)(2,1)}, bf16[64,256]{1,0:T(8,128)(2,1)}, u32[]{:S(2)}, u32[]{:S(2)}) collective-permute-start(bf16[64,256]{1,0:T(8,128)(2,1)} %get-tuple-element.8), channel_id=1, source_target_pairs={{0,512},{512,0},{1,513},{513,1},{2,514},{514,2},{3,515},{515,3},{4... | collective-permute-start | bytes 98312 | tf_op jit(solution)/shard_map/ppermute | solution.py:59
  55.1 5.1 %collective-permute-start.4 = (bf16[64,256]{1,0:T(8,128)(2,1)}, bf16[64,256]{1,0:T(8,128)(2,1)}, u32[]{:S(2)}, u32[]{:S(2)}) collective-permute-start(bf16[64,256]{1,0:T(8,128)(2,1)} %get-tuple-element.9), channel_id=1, source_target_pairs={{0,513},{1,512},{512,1},{513,0},{2,515},{3,514},{514,3},{515,2},{4... | collective-permute-start | bytes 98312 | tf_op jit(solution)/shard_map/ppermute | solution.py:60
  60.3 0.0 copy-done.1
  60.3 0.6 constant_dynamic-slice_fusion
  60.9 2.3 %collective-permute-start.2 = (bf16[64,256]{1,0:T(8,128)(2,1)}, bf16[64,256]{1,0:T(8,128)(2,1)}, u32[]{:S(2)}, u32[]{:S(2)}) collective-permute-start(bf16[64,256]{1,0:T(8,128)(2,1)} %dynamic-slice_convert_fusion.2), channel_id=1, source_target_pairs={{0,1},{1,0},{2,3},{3,2},{4,5},{5,4},{6,7},{7,6},{8,9},{9,8},{10,11... | collective-permute-start | bytes 98312 | tf_op jit(solution)/shard_map/ppermute | solution.py:61
  63.2 1.2 %reshape.94 = bf16[64,4,2048]{2,1,0:T(4,128)(2,1)} reshape(bf16[256,2048]{1,0:T(8,128)(2,1)S(1)} %fusion) | data formatting | bytes 2097152 | tf_op jit(solution)/shard_map/reshape | solution.py:62
  64.4 0.0 copy-start.2
  64.4 0.0 copy-start.3
  64.4 6.3 %all-to-all-start.1 = ((bf16[64,4,2048]{2,1,0:T(4,128)(2,1)}), bf16[64,4,2048]{2,1,0:T(4,128)(2,1)S(1)}, u32[]{:S(2)}, u32[]{:S(2)}) async-start(bf16[64,4,2048]{2,1,0:T(4,128)(2,1)} %reshape.94), calls=%async_computation.1 | async-start | bytes 2097152 | tf_op jit(solution)/shard_map/all_to_all | solution.py:62
  70.7 0.0 collective-permute-done.3
  70.7 0.0 collective-permute-done.4
  70.7 0.8 convert_add_fusion
  71.5 0.0 collective-permute-done.2
  71.5 0.8 convert_add_fusion.1
  72.3 15.2 %collective-permute-start.7 = (bf16[64,512]{1,0:T(8,128)(2,1)S(1)}, bf16[64,512]{1,0:T(8,128)(2,1)S(1)}, u32[]{:S(2)}, u32[]{:S(2)}) collective-permute-start(bf16[64,512]{1,0:T(8,128)(2,1)S(1)} %fusion.1), channel_id=1, source_target_pairs={{0,6},{2,0},{4,2},{6,4},{1,7},{3,1},{5,3},{7,5},{8,14},{10,8},{12,... | collective-permute-start | bytes 196616 | tf_op jit(solution)/shard_map/ppermute | solution.py:72
  87.5 1.9 %collective-permute-start.6 = (bf16[64,512]{1,0:T(8,128)(2,1)S(1)}, bf16[64,512]{1,0:T(8,128)(2,1)S(1)}, u32[]{:S(2)}, u32[]{:S(2)}) collective-permute-start(bf16[64,512]{1,0:T(8,128)(2,1)S(1)} %fusion.1), channel_id=1, source_target_pairs={{0,2},{2,4},{4,6},{6,0},{1,3},{3,5},{5,7},{7,1},{8,10},{10,12},{12... | collective-permute-start | bytes 196616 | tf_op jit(solution)/shard_map/ppermute | solution.py:72
  89.4 4.0 %collective-permute-start.5 = (bf16[64,512]{1,0:T(8,128)(2,1)S(1)}, bf16[64,512]{1,0:T(8,128)(2,1)S(1)}, u32[]{:S(2)}, u32[]{:S(2)}) collective-permute-start(bf16[64,512]{1,0:T(8,128)(2,1)S(1)} %fusion.1), channel_id=1, source_target_pairs={{0,4},{2,6},{4,0},{6,2},{1,5},{3,7},{5,1},{7,3},{8,12},{10,14},{12... | collective-permute-start | bytes 196616 | tf_op jit(solution)/shard_map/ppermute | solution.py:72
  93.4 0.3 convolution_convert_fusion
  93.8 3.3 %collective-permute-start.9 = (bf16[128,2048]{1,0:T(8,128)(2,1)S(1)}, bf16[128,2048]{1,0:T(8,128)(2,1)}, u32[]{:S(2)}, u32[]{:S(2)}) collective-permute-start(bf16[128,2048]{1,0:T(8,128)(2,1)S(1)} %convolution_convert_fusion), channel_id=1, source_target_pairs={{0,512},{512,0},{1,513},{513,1},{2,514},{514,2},{3,515},{515,3},{4... | collective-permute-start | bytes 1572872 | tf_op jit(solution)/shard_map/ppermute | solution.py:64
  97.0 0.0 collective-permute-done.7
  97.0 0.0 collective-permute-done.6
  97.1 1.6 %collective-permute-done.5 = bf16[64,512]{1,0:T(8,128)(2,1)S(1)} collective-permute-done((bf16[64,512]{1,0:T(8,128)(2,1)S(1)}, bf16[64,512]{1,0:T(8,128)(2,1)S(1)}, u32[]{:S(2)}, u32[]{:S(2)}) %collective-permute-start.5) | collective-permute-done | bytes 65568 | tf_op jit(solution)/shard_map/ppermute | solution.py:72
  98.8 0.0 copy-done.2
  98.8 0.0 copy-done.3
  98.8 0.2 subtract_convert_fusion.1
  99.0 0.1 pad_maximum_fusion.1
  99.1 3.5 %collective-permute-start.8 = (bf16[64,512]{1,0:T(8,128)(2,1)S(1)}, bf16[64,512]{1,0:T(8,128)(2,1)S(1)}, u32[]{:S(2)}, u32[]{:S(2)}) collective-permute-start(bf16[64,512]{1,0:T(8,128)(2,1)S(1)} %bitcast.24), channel_id=1, source_target_pairs={{0,1},{1,0},{2,3},{3,2},{4,5},{5,4},{6,7},{7,6},{8,9},{9,8},{10,11... | collective-permute-start | bytes 196616 | tf_op jit(solution)/shard_map/ppermute | solution.py:78
  102.6 0.3 fusion.2
  102.9 0.6 collective-permute-done.8
  103.5 0.7 maximum_select_fusion.1
  104.1 5.9 %collective-permute-done.9 = bf16[128,2048]{1,0:T(8,128)(2,1)} collective-permute-done((bf16[128,2048]{1,0:T(8,128)(2,1)S(1)}, bf16[128,2048]{1,0:T(8,128)(2,1)}, u32[]{:S(2)}, u32[]{:S(2)}) %collective-permute-start.9) | collective-permute-done | bytes 524320 | tf_op jit(solution)/shard_map/ppermute | solution.py:64
  110.0 1.9 %add_convert_fusion = bf16[128,2048]{1,0:T(8,128)(2,1)} fusion(f32[128,2048]{1,0:T(8,128)S(1)} %fusion.2, bf16[128,2048]{1,0:T(8,128)(2,1)} %collective-permute-done.9), kind=kLoop, calls=%fused_computation.4 | loop fusion | flops 786432 | bytes 2097152 | tf_op jit(solution)/shard_map/convert_element_type | solution.py:65
  112.0 0.0 all-to-all-done.1
  112.0 1.1 convert_reduce_fusion
  (8 shorter events, 0.2 us)
Async XLA Ops:
  0.6 16.6 %copy-start = (bf16[128,2048]{1,0:T(8,128)(2,1)S(1)}, bf16[128,2048]{1,0:T(8,128)(2,1)}, u32[]{:S(2)}) copy-start(bf16[128,2048]{1,0:T(8,128)(2,1)} %param.4) | copy-start | bytes 1572868
  0.6 21.5 %copy-start.4 = (bf16[128,512]{1,0:T(8,128)(2,1)S(1)}, bf16[128,512]{1,0:T(8,128)(2,1)}, u32[]{:S(2)}) copy-start(bf16[128,512]{1,0:T(8,128)(2,1)} %param.7) | copy-start | bytes 393220
  0.7 21.6 %copy-start.5 = (s32[1,128]{1,0:T(1,128)S(1)}, s32[1,128]{1,0:T(1,128)}, u32[]{:S(2)}) copy-start(s32[1,128]{1,0:T(1,128)} %param.5) | copy-start | bytes 1540
  2.9 37.4 %all-to-all-start = ((bf16[64,4,2048]{2,1,0:T(4,128)(2,1)}), bf16[64,4,2048]{2,1,0:T(4,128)(2,1)}, u32[]{:S(2)}, u32[]{:S(2)}) async-start(bf16[64,4,2048]{2,1,0:T(4,128)(2,1)} %broadcast_in_dim.2), calls=%async_computation | async-start | bytes 2097152 | tf_op jit(solution)/shard_map/all_to_all | solution.py:39
  17.3 15.4 %collective-permute-start = (bf16[128,2048]{1,0:T(8,128)(2,1)S(1)}, bf16[128,2048]{1,0:T(8,128)(2,1)}, u32[]{:S(2)}, u32[]{:S(2)}) collective-permute-start(bf16[128,2048]{1,0:T(8,128)(2,1)S(1)} %copy-done), channel_id=1, source_target_pairs={{0,512},{512,0},{1,513},{513,1},{2,514},{514,2},{3,515},{515,3},{4... | collective-permute-start | bytes 1572872 | tf_op jit(solution)/shard_map/ppermute | solution.py:40
  24.0 8.7 %collective-permute-start.1 = (bf16[128,256]{1,0:T(8,128)(2,1)S(1)}, bf16[128,256]{1,0:T(8,128)(2,1)S(1)}, u32[]{:S(2)}, u32[]{:S(2)}) collective-permute-start(bf16[128,256]{1,0:T(8,128)(2,1)S(1)} %broadcast_select_fusion), channel_id=1, source_target_pairs={{0,512},{512,0},{1,513},{513,1},{2,514},{514,2},{3,515},{515,3},{4... | collective-permute-start | bytes 196616 | tf_op jit(solution)/shard_map/ppermute | solution.py:45
  41.7 18.6 %copy-start.1 = (f32[128,64]{1,0:T(8,128)S(1)}, f32[128,64]{1,0:T(8,128)}, u32[]{:S(2)}) copy-start(f32[128,64]{1,0:T(8,128)} %get-tuple-element.17) | copy-start | bytes 98308
  46.0 24.7 %collective-permute-start.3 = (bf16[64,256]{1,0:T(8,128)(2,1)}, bf16[64,256]{1,0:T(8,128)(2,1)}, u32[]{:S(2)}, u32[]{:S(2)}) collective-permute-start(bf16[64,256]{1,0:T(8,128)(2,1)} %get-tuple-element.8), channel_id=1, source_target_pairs={{0,512},{512,0},{1,513},{513,1},{2,514},{514,2},{3,515},{515,3},{4... | collective-permute-start | bytes 98312 | tf_op jit(solution)/shard_map/ppermute | solution.py:59
  55.1 15.6 %collective-permute-start.4 = (bf16[64,256]{1,0:T(8,128)(2,1)}, bf16[64,256]{1,0:T(8,128)(2,1)}, u32[]{:S(2)}, u32[]{:S(2)}) collective-permute-start(bf16[64,256]{1,0:T(8,128)(2,1)} %get-tuple-element.9), channel_id=1, source_target_pairs={{0,513},{1,512},{512,1},{513,0},{2,515},{3,514},{514,3},{515,2},{4... | collective-permute-start | bytes 98312 | tf_op jit(solution)/shard_map/ppermute | solution.py:60
  60.9 10.6 %collective-permute-start.2 = (bf16[64,256]{1,0:T(8,128)(2,1)}, bf16[64,256]{1,0:T(8,128)(2,1)}, u32[]{:S(2)}, u32[]{:S(2)}) collective-permute-start(bf16[64,256]{1,0:T(8,128)(2,1)} %dynamic-slice_convert_fusion.2), channel_id=1, source_target_pairs={{0,1},{1,0},{2,3},{3,2},{4,5},{5,4},{6,7},{7,6},{8,9},{9,8},{10,11... | collective-permute-start | bytes 98312 | tf_op jit(solution)/shard_map/ppermute | solution.py:61
  64.4 34.3 %copy-start.2 = (f32[64,64]{1,0:T(8,128)S(1)}, f32[64,64]{1,0:T(8,128)}, u32[]{:S(2)}) copy-start(f32[64,64]{1,0:T(8,128)} %get-tuple-element.20) | copy-start | bytes 49156
  64.4 34.4 %copy-start.3 = (f32[64,64]{1,0:T(8,128)S(1)}, f32[64,64]{1,0:T(8,128)}, u32[]{:S(2)}) copy-start(f32[64,64]{1,0:T(8,128)} %get-tuple-element.21) | copy-start | bytes 49156
  64.4 47.5 %all-to-all-start.1 = ((bf16[64,4,2048]{2,1,0:T(4,128)(2,1)}), bf16[64,4,2048]{2,1,0:T(4,128)(2,1)S(1)}, u32[]{:S(2)}, u32[]{:S(2)}) async-start(bf16[64,4,2048]{2,1,0:T(4,128)(2,1)} %reshape.94), calls=%async_computation.1 | async-start | bytes 2097152 | tf_op jit(solution)/shard_map/all_to_all | solution.py:62
  72.3 24.7 %collective-permute-start.7 = (bf16[64,512]{1,0:T(8,128)(2,1)S(1)}, bf16[64,512]{1,0:T(8,128)(2,1)S(1)}, u32[]{:S(2)}, u32[]{:S(2)}) collective-permute-start(bf16[64,512]{1,0:T(8,128)(2,1)S(1)} %fusion.1), channel_id=1, source_target_pairs={{0,6},{2,0},{4,2},{6,4},{1,7},{3,1},{5,3},{7,5},{8,14},{10,8},{12,... | collective-permute-start | bytes 196616 | tf_op jit(solution)/shard_map/ppermute | solution.py:72
  87.5 9.5 %collective-permute-start.6 = (bf16[64,512]{1,0:T(8,128)(2,1)S(1)}, bf16[64,512]{1,0:T(8,128)(2,1)S(1)}, u32[]{:S(2)}, u32[]{:S(2)}) collective-permute-start(bf16[64,512]{1,0:T(8,128)(2,1)S(1)} %fusion.1), channel_id=1, source_target_pairs={{0,2},{2,4},{4,6},{6,0},{1,3},{3,5},{5,7},{7,1},{8,10},{10,12},{12... | collective-permute-start | bytes 196616 | tf_op jit(solution)/shard_map/ppermute | solution.py:72
  89.4 9.2 %collective-permute-start.5 = (bf16[64,512]{1,0:T(8,128)(2,1)S(1)}, bf16[64,512]{1,0:T(8,128)(2,1)S(1)}, u32[]{:S(2)}, u32[]{:S(2)}) collective-permute-start(bf16[64,512]{1,0:T(8,128)(2,1)S(1)} %fusion.1), channel_id=1, source_target_pairs={{0,4},{2,6},{4,0},{6,2},{1,5},{3,7},{5,1},{7,3},{8,12},{10,14},{12... | collective-permute-start | bytes 196616 | tf_op jit(solution)/shard_map/ppermute | solution.py:72
  93.8 16.3 %collective-permute-start.9 = (bf16[128,2048]{1,0:T(8,128)(2,1)S(1)}, bf16[128,2048]{1,0:T(8,128)(2,1)}, u32[]{:S(2)}, u32[]{:S(2)}) collective-permute-start(bf16[128,2048]{1,0:T(8,128)(2,1)S(1)} %convolution_convert_fusion), channel_id=1, source_target_pairs={{0,512},{512,0},{1,513},{513,1},{2,514},{514,2},{3,515},{515,3},{4... | collective-permute-start | bytes 1572872 | tf_op jit(solution)/shard_map/ppermute | solution.py:64
  99.1 4.4 %collective-permute-start.8 = (bf16[64,512]{1,0:T(8,128)(2,1)S(1)}, bf16[64,512]{1,0:T(8,128)(2,1)S(1)}, u32[]{:S(2)}, u32[]{:S(2)}) collective-permute-start(bf16[64,512]{1,0:T(8,128)(2,1)S(1)} %bitcast.24), channel_id=1, source_target_pairs={{0,1},{1,0},{2,3},{3,2},{4,5},{5,4},{6,7},{7,6},{8,9},{9,8},{10,11... | collective-permute-start | bytes 196616 | tf_op jit(solution)/shard_map/ppermute | solution.py:78

commit v3 on v2

v3 whole, which is shorter than its diff:
```python
import jax
import jax.numpy as jnp
from jax import lax
from jax.experimental import pallas as pl
from jax.experimental.pallas import tpu as pltpu
from jax.sharding import Mesh, PartitionSpec as P

HEAD = 128
SWAP = ((0, 1), (1, 0))


def doc_positions(segments):
    index = jnp.arange(segments.shape[0], dtype=jnp.int32)
    return index - jnp.sum((segments[None, :] < segments[:, None]).astype(jnp.int32), axis=1)


def angles(positions, half):
    freq = 500000.0 ** (-2.0 * jnp.arange(half, dtype=jnp.float32) / (2 * half))
    turn = positions.astype(jnp.float32)[:, None] * freq[None, :]
    return (jnp.cos(turn)[:, None, :], jnp.sin(turn)[:, None, :])


def rotate(field, cosine, sine, sign):
    rows = field.shape[0]
    shaped = field.reshape(rows, -1, HEAD)
    first, second = (shaped[..., : HEAD // 2], shaped[..., HEAD // 2 :])
    out = jnp.concatenate(
        [first * cosine - sign * second * sine, second * cosine + sign * first * sine], axis=-1
    )
    return out.reshape(rows, -1)


def dot(a, b, da, db):
    return lax.dot_general(a, b, (((da,), (db,)), ((), ())), preferred_element_type=jnp.float32)


def kraw_kernel(tok_ref, par_ref, w_ref, keep_ref, send_ref):
    mine = pl.multiple_of(lax.axis_index("c") * 64, 64)
    other = pl.multiple_of(64 - mine, 64)
    halves = [ref[pl.ds(at, 64), :] for at in (mine, other) for ref in (tok_ref, par_ref)]
    out = dot(jnp.concatenate(halves, axis=0), w_ref[...], 1, 1)
    keep_ref[...] = out[:128]
    send_ref[...] = out[128:].astype(jnp.bfloat16)


def merge_kernel(keep_ref, c_ref, own_ref, far_ref):
    out = (keep_ref[...] + c_ref[...].astype(jnp.float32)).astype(jnp.bfloat16)
    own_ref[...] = out[:64]
    far_ref[...] = out[64:]


def grad_kernel(kb_ref, w_ref, add_ref, out_ref):
    out = dot(kb_ref[...], w_ref[...], 1, 0) + add_ref[...].astype(jnp.float32)
    out_ref[...] = out.astype(jnp.bfloat16)


def whole(kernel, outs, n_in, name):
    vmem = pl.BlockSpec(memory_space=pltpu.VMEM)
    return pl.pallas_call(
        kernel,
        out_shape=outs,
        in_specs=[vmem] * n_in,
        out_specs=jax.tree.map(lambda _: vmem, outs),
        compiler_params=pltpu.CompilerParams(vmem_limit_bytes=32 << 20),
        name=name,
    )


def body(tokens, seg_ids, key_weight, key_grad):
    bf16, f32 = jnp.bfloat16, jnp.float32
    shape = jax.ShapeDtypeStruct
    zl, core = lax.axis_index("zl"), lax.axis_index("c")
    spread = jnp.broadcast_to(key_weight[None], (64, 4, 2048))
    gathered = lax.all_to_all(spread, ("y", "x"), 0, 0)
    tok_p = lax.ppermute(tokens, "zl", SWAP)

    cosine, sine = angles(doc_positions(seg_ids[0]), HEAD // 2)
    kback = rotate(key_grad.astype(f32), cosine, sine, -1.0).astype(bf16)
    left, right = kback[:, :256], kback[:, 256:]
    kb_p = lax.ppermute(jnp.where(zl == 0, right, left), "zl", SWAP)
    kb = jnp.where(zl == 0, left, right)

    partial = (dot(kb, tokens, 0, 0) + dot(kb_p, tok_p, 0, 0)).astype(bf16).reshape(64, 4, 2048)

    weights = gathered.reshape(256, 2048)
    keep, to_c = whole(kraw_kernel, (shape((128, 256), f32), shape((128, 256), bf16)), 3, "kraw")(
        tokens, tok_p, weights
    )
    g_send = dot(kb_p, weights, 1, 0).astype(bf16)
    to_c, partial = lax.optimization_barrier((to_c, partial))
    from_c = lax.ppermute(to_c, "c", SWAP)
    half = shape((64, 256), bf16)
    own, to_z = whole(merge_kernel, (half, half), 2, "merge")(keep, from_c)
    from_z = lax.ppermute(to_z, "zl", SWAP)
    g_par = lax.ppermute(g_send, "zl", SWAP)
    scattered = lax.all_to_all(partial, ("y", "x"), 0, 0)

    total_b = jnp.where(
        zl == 0, jnp.concatenate([own, from_z], 1), jnp.concatenate([from_z, own], 1)
    )
    one, three, two = (
        lax.ppermute(total_b, "zh", [(i, (i + step) % 4) for i in range(4)])
        for step in (1, 3, 2)
    )
    one, three, two, g_par = lax.optimization_barrier((one, three, two, g_par))
    total = (total_b.astype(f32) + two.astype(f32)) + (one.astype(f32) + three.astype(f32))
    own_cos = lax.dynamic_slice_in_dim(cosine, core * 64, 64, 0)
    own_sin = lax.dynamic_slice_in_dim(sine, core * 64, 64, 0)
    keys = rotate(total, own_cos, own_sin, 1.0).astype(bf16)
    others = lax.ppermute(keys, "c", SWAP)
    keys = jnp.where(core == 0, jnp.concatenate([keys, others]), jnp.concatenate([others, keys]))

    grad_tokens = whole(grad_kernel, shape((128, 2048), bf16), 3, "grad")(kb, weights, g_par)
    grad_key_weight = jnp.sum(scattered.astype(f32), axis=0)
    return keys, grad_tokens, grad_key_weight


def solution(mesh):
    fine = Mesh(mesh.devices.reshape(2, 8, 8, 4, 2), ("zl", "y", "x", "zh", "c"))
    fsdp, tensor = ("zl", "y", "x"), ("zh", "c")
    placed = (P(fsdp, tensor), P(fsdp, None), P(fsdp, tensor), P(fsdp, None))
    return jax.shard_map(
        body,
        mesh=fine,
        in_specs=placed,
        out_specs=(P(fsdp, None), P(fsdp, tensor), P(fsdp, tensor)),
        check_vma=False,
    )
```

time: 114 us -> 106 us (0.930)
  matrix products: 5.66 us -> 2.01 us
  other arithmetic: 7.19 us -> 3.69 us
  local copies, waits for them, and re-layouts: 6.89 us -> 3.96 us
  waiting for transfers between devices: 20.5 us -> 22.6 us
  Pallas kernels: 0 us -> 1.6 us
    ppermute x1, starting transfers between devices: 9.1 us -> 1.92 us  [body(): from_z = lax.ppermute(to_z, 'zl', SWAP)]
    ppermute x2 -> x1, waiting for transfers between devices: 5.88 us -> 0.01 us  [body(): g_par = lax.ppermute(g_send, 'zl', SWAP)]
    ppermute x1, waiting for transfers between devices: 0.01 us -> 4.09 us  [body(): from_z = lax.ppermute(to_z, 'zl', SWAP)]
    dot_general x6 -> x3, matrix products: 5.66 us -> 2.01 us  [dot(): lax.dot_general(a, b, (((da,), (db,)), ((), ())), preferred_element_type=...]
    all_to_all x1, starting transfers between devices: 6.26 us -> 9.86 us  [body(): scattered = lax.all_to_all(partial, ('y', 'x'), 0, 0)]
    ppermute x3, waiting for transfers between devices: 1.61 us -> 4.9 us  [body(): lax.ppermute(total_b, 'zh', [(i, (i + step) % 4) for i in range(4)])]
    ppermute x1, starting transfers between devices: 3.48 us -> 6.02 us  [body(): others = lax.ppermute(keys, 'c', SWAP)]
    convert_element_type x2 -> x0, other arithmetic: 1.96 us -> none  [the longest x1 1.94 us: body(): grad_tokens = (dot(kb, weights, 1, 0) + g_par.astype(f32)).astype(bf16)]
  transfers between devices with their start and end apart: 12 -> 11, of which waited for: 5 -> 5; matrix products, arithmetic and copies ran while one was open for 9% -> 6% of each run, Pallas kernels for 0% -> 1%
where the time goes in v3:
time: 106 us
  starting transfers between devices  70.8 us (67%)
  waiting for transfers between devices  22.6 us (21%)
  local copies, waits for them, and re-layouts  3.96 us (4%)
  other arithmetic  3.69 us (3%)
  matrix products  2.01 us (2%)
  Pallas kernels  1.6 us (2%)
    ppermute x3, starting transfers between devices, body(): lax.ppermute(total_b, 'zh', [(i, (i + step) % 4) for i in range(4)])  21.1 us
    all_to_all x1, starting transfers between devices, body(): gathered = lax.all_to_all(spread, ('y', 'x'), 0, 0)  14 us
    all_to_all x1, starting transfers between devices, body(): scattered = lax.all_to_all(partial, ('y', 'x'), 0, 0)  9.86 us
    ppermute x1, waiting for transfers between devices, body(): kb_p = lax.ppermute(jnp.where(zl == 0, right, left), 'zl', SWAP)  6.91 us
    ppermute x1, starting transfers between devices, body(): g_par = lax.ppermute(g_send, 'zl', SWAP)  6.83 us
    ppermute x1, starting transfers between devices, body(): others = lax.ppermute(keys, 'c', SWAP)  6.02 us
    all_to_all x1, waiting for transfers between devices, body(): gathered = lax.all_to_all(spread, ('y', 'x'), 0, 0)  5.79 us
    ppermute x1, starting transfers between devices, body(): tok_p = lax.ppermute(tokens, 'zl', SWAP)  4.91 us
  transfers between devices with their start and end apart: 11, of which 5 were waited for; matrix products, arithmetic and copies ran while one was open for 6% of the time, Pallas kernels for 1%

profile of v3, /device:TPU:1, one launch (start us, length us, event | category | flops | bytes accessed | tf_op | source)
XLA Modules:
  0.0 105.6 jit_solution(10514658514175922442)
XLA Ops:
  0.6 0.0 copy-start
  0.6 0.0 copy-start.2
  0.7 0.0 copy-start.3
  0.7 2.3 %broadcast_in_dim.2 = bf16[64,4,2048]{2,1,0:T(4,128)(2,1)} broadcast(bf16[4,2048]{1,0:T(4,128)(2,1)} %param.6), dimensions={1,2} | broadcast | bytes 1064960 | tf_op jit(solution)/shard_map/broadcast_in_dim | solution.py:73
  2.9 14.0 %all-to-all-start = ((bf16[64,4,2048]{2,1,0:T(4,128)(2,1)}), bf16[64,4,2048]{2,1,0:T(4,128)(2,1)S(1)}, u32[]{:S(2)}, u32[]{:S(2)}) async-start(bf16[64,4,2048]{2,1,0:T(4,128)(2,1)} %broadcast_in_dim.2), calls=%async_computation | async-start | bytes 2097152 | tf_op jit(solution)/shard_map/all_to_all | solution.py:74
  17.0 0.0 copy-done
  17.0 4.9 %collective-permute-start = (bf16[128,2048]{1,0:T(8,128)(2,1)S(1)}, bf16[128,2048]{1,0:T(8,128)(2,1)S(1)}, u32[]{:S(2)}, u32[]{:S(2)}) collective-permute-start(bf16[128,2048]{1,0:T(8,128)(2,1)S(1)} %copy-done), channel_id=1, source_target_pairs={{0,512},{512,0},{1,513},{513,1},{2,514},{514,2},{3,515},{515,3},{4... | collective-permute-start | bytes 1572872 | tf_op jit(solution)/shard_map/ppermute | solution.py:75
  21.9 0.0 copy-done.2
  21.9 0.1 reshape.96
  22.0 0.0 copy-done.3
  22.0 0.2 convert_reduce_fusion.1
  22.2 1.0 multiply_sine_fusion
  23.2 0.3 subtract_convert_fusion
  23.5 0.2 pad_maximum_fusion
  23.7 1.9 %collective-permute-start.1 = (bf16[128,256]{1,0:T(8,128)(2,1)S(1)}, bf16[128,256]{1,0:T(8,128)(2,1)S(1)}, u32[]{:S(2)}, u32[]{:S(2)}) collective-permute-start(bf16[128,256]{1,0:T(8,128)(2,1)S(1)} %get-tuple-element.27), channel_id=1, source_target_pairs={{0,512},{512,0},{1,513},{513,1},{2,514},{514,2},{3,515},{515,3},{4... | collective-permute-start | bytes 196616 | tf_op jit(solution)/shard_map/ppermute | solution.py:80
  25.6 0.5 fusion.1
  26.1 6.9 %collective-permute-done.1 = bf16[128,256]{1,0:T(8,128)(2,1)S(1)} collective-permute-done((bf16[128,256]{1,0:T(8,128)(2,1)S(1)}, bf16[128,256]{1,0:T(8,128)(2,1)S(1)}, u32[]{:S(2)}, u32[]{:S(2)}) %collective-permute-start.1) | collective-permute-done | bytes 65568 | tf_op jit(solution)/shard_map/ppermute | solution.py:80
  33.0 0.0 collective-permute-done.par_ref
  33.0 0.5 fusion
  33.5 1.2 %reshape.93 = bf16[64,4,2048]{2,1,0:T(4,128)(2,1)} reshape(bf16[256,2048]{1,0:T(8,128)(2,1)S(1)} %fusion) | data formatting | bytes 2097152 | tf_op jit(solution)/shard_map/reshape | solution.py:83
  34.7 5.8 %all-to-all-done = bf16[64,4,2048]{2,1,0:T(4,128)(2,1)S(1)} async-done(((bf16[64,4,2048]{2,1,0:T(4,128)(2,1)}), bf16[64,4,2048]{2,1,0:T(4,128)(2,1)S(1)}, u32[]{:S(2)}, u32[]{:S(2)}) %all-to-all-start) | async-done | bytes 1048608 | tf_op jit(solution)/shard_map/all_to_all | solution.py:74
  40.5 0.3 reshape.90.w_ref
  40.8 0.5 kraw.1
  41.2 0.0 copy-start.1
  41.2 9.9 %all-to-all-start.1 = ((bf16[64,4,2048]{2,1,0:T(4,128)(2,1)}), bf16[64,4,2048]{2,1,0:T(4,128)(2,1)S(1)}, u32[]{:S(2)}, u32[]{:S(2)}) async-start(bf16[64,4,2048]{2,1,0:T(4,128)(2,1)} %reshape.93), calls=%async_computation.1 | async-start | bytes 2097152 | tf_op jit(solution)/shard_map/all_to_all | solution.py:96
  51.1 1.1 %convolution_convert_fusion = bf16[128,2048]{1,0:T(8,128)(2,1)} fusion(bf16[128,256]{1,0:T(8,128)(2,1)S(1)} %collective-permute-done.1, bf16[256,2048]{1,0:T(8,128)(2,1)S(1)} %reshape.90.w_ref), kind=kOutput, calls=%fused_computation.2 | convolution fusion | flops 134479872 | bytes 1638400 | tf_op jit(solution)/shard_map/dot_general | solution.py:34
  52.2 6.8 %collective-permute-start.7 = (bf16[128,2048]{1,0:T(8,128)(2,1)}, bf16[128,2048]{1,0:T(8,128)(2,1)S(1)}, u32[]{:S(2)}, u32[]{:S(2)}) collective-permute-start(bf16[128,2048]{1,0:T(8,128)(2,1)} %convolution_convert_fusion), channel_id=1, source_target_pairs={{0,512},{512,0},{1,513},{513,1},{2,514},{514,2},{3,515},{515,3},{4... | collective-permute-start | bytes 1572872 | tf_op jit(solution)/shard_map/ppermute | solution.py:95
  59.0 4.2 %collective-permute-start.2 = (bf16[128,256]{1,0:T(8,128)(2,1)S(1)}, bf16[128,256]{1,0:T(8,128)(2,1)S(1)}, u32[]{:S(2)}, u32[]{:S(2)}) collective-permute-start(bf16[128,256]{1,0:T(8,128)(2,1)S(1)} %get-tuple-element.15), channel_id=1, source_target_pairs={{0,1},{1,0},{2,3},{3,2},{4,5},{5,4},{6,7},{7,6},{8,9},{9,8},{10,11... | collective-permute-start | bytes 196616 | tf_op jit(solution)/shard_map/ppermute | solution.py:91
  63.2 0.9 collective-permute-done.2.c_ref
  64.1 1.9 %collective-permute-start.3 = (bf16[64,256]{1,0:T(8,128)(2,1)S(1)}, bf16[64,256]{1,0:T(8,128)(2,1)S(1)}, u32[]{:S(2)}, u32[]{:S(2)}) collective-permute-start(bf16[64,256]{1,0:T(8,128)(2,1)S(1)} %get-tuple-element.17), channel_id=1, source_target_pairs={{0,512},{512,0},{1,513},{513,1},{2,514},{514,2},{3,515},{515,3},{4... | collective-permute-start | bytes 98312 | tf_op jit(solution)/shard_map/ppermute | solution.py:94
  66.1 4.1 %collective-permute-done.3 = bf16[64,256]{1,0:T(8,128)(2,1)S(1)} collective-permute-done((bf16[64,256]{1,0:T(8,128)(2,1)S(1)}, bf16[64,256]{1,0:T(8,128)(2,1)S(1)}, u32[]{:S(2)}, u32[]{:S(2)}) %collective-permute-start.3) | collective-permute-done | bytes 32800 | tf_op jit(solution)/shard_map/ppermute | solution.py:94
  70.2 7.6 %collective-permute-start.4 = (bf16[64,512]{1,0:T(8,128)(2,1)S(1)}, bf16[64,512]{1,0:T(8,128)(2,1)S(1)}, u32[]{:S(2)}, u32[]{:S(2)}) collective-permute-start(bf16[64,512]{1,0:T(8,128)(2,1)S(1)} %maximum_select_fusion.1), channel_id=1, source_target_pairs={{0,2},{2,4},{4,6},{6,0},{1,3},{3,5},{5,7},{7,1},{8,10},{10,12},{12... | collective-permute-start | bytes 196616 | tf_op jit(solution)/shard_map/ppermute | solution.py:102
  77.8 9.5 %collective-permute-start.5 = (bf16[64,512]{1,0:T(8,128)(2,1)S(1)}, bf16[64,512]{1,0:T(8,128)(2,1)S(1)}, u32[]{:S(2)}, u32[]{:S(2)}) collective-permute-start(bf16[64,512]{1,0:T(8,128)(2,1)S(1)} %maximum_select_fusion.1), channel_id=1, source_target_pairs={{0,6},{2,0},{4,2},{6,4},{1,7},{3,1},{5,3},{7,5},{8,14},{10,8},{12,... | collective-permute-start | bytes 196616 | tf_op jit(solution)/shard_map/ppermute | solution.py:102
  87.3 4.0 %collective-permute-start.6 = (bf16[64,512]{1,0:T(8,128)(2,1)S(1)}, bf16[64,512]{1,0:T(8,128)(2,1)S(1)}, u32[]{:S(2)}, u32[]{:S(2)}) collective-permute-start(bf16[64,512]{1,0:T(8,128)(2,1)S(1)} %maximum_select_fusion.1), channel_id=1, source_target_pairs={{0,4},{2,6},{4,0},{6,2},{1,5},{3,7},{5,1},{7,3},{8,12},{10,14},{12... | collective-permute-start | bytes 196616 | tf_op jit(solution)/shard_map/ppermute | solution.py:102
  91.3 0.0 copy-done.1
  91.4 0.0 collective-permute-done.4
  91.4 0.0 collective-permute-done.5
  91.4 4.9 %collective-permute-done.6 = bf16[64,512]{1,0:T(8,128)(2,1)S(1)} collective-permute-done((bf16[64,512]{1,0:T(8,128)(2,1)S(1)}, bf16[64,512]{1,0:T(8,128)(2,1)S(1)}, u32[]{:S(2)}, u32[]{:S(2)}) %collective-permute-start.6) | collective-permute-done | bytes 65568 | tf_op jit(solution)/shard_map/ppermute | solution.py:102
  96.3 0.0 collective-permute-done.7.add_ref
  96.4 0.2 subtract_convert_fusion.1
  96.6 0.1 pad_maximum_fusion.1
  96.7 6.0 %collective-permute-start.8 = (bf16[64,512]{1,0:T(8,128)(2,1)S(1)}, bf16[64,512]{1,0:T(8,128)(2,1)S(1)}, u32[]{:S(2)}, u32[]{:S(2)}) collective-permute-start(bf16[64,512]{1,0:T(8,128)(2,1)S(1)} %bitcast.18), channel_id=1, source_target_pairs={{0,1},{1,0},{2,3},{3,2},{4,5},{5,4},{6,7},{7,6},{8,9},{9,8},{10,11... | collective-permute-start | bytes 196616 | tf_op jit(solution)/shard_map/ppermute | solution.py:110
  102.7 1.1 %grad.1 = bf16[128,2048]{1,0:T(8,128)(2,1)} custom-call(bf16[128,256]{1,0:T(8,128)(2,1)S(1)} %get-tuple-element.28.kb_ref, bf16[256,2048]{1,0:T(8,128)(2,1)S(1)} %reshape.90.w_ref, bf16[128,2048]{1,0:T(8,128)(2,1)S(1)} %collective-permute-done.7.add_ref), custom_call_target="tpu_custom_call" | custom-call | tf_op jit(solution)/shard_map/grad/pallas_call | solution.py:113
  103.8 0.0 collective-permute-done.8
  103.8 0.7 maximum_select_fusion
  104.5 0.0 all-to-all-done.1
  104.5 1.1 %convert_reduce_fusion = f32[4,2048]{1,0:T(4,128)} fusion(bf16[64,4,2048]{2,1,0:T(4,128)(2,1)S(1)} %all-to-all-done.1), kind=kLoop, calls=%fused_computation.3 | loop fusion | flops 1040384 | bytes 1081344 | tf_op jit(solution)/shard_map/reduce_sum | solution.py:114
  (10 shorter events, 0.2 us)
Async XLA Ops:
  0.6 16.3 %copy-start = (bf16[128,2048]{1,0:T(8,128)(2,1)S(1)}, bf16[128,2048]{1,0:T(8,128)(2,1)}, u32[]{:S(2)}) copy-start(bf16[128,2048]{1,0:T(8,128)(2,1)} %tok_ref.1) | copy-start | bytes 1572868
  0.6 21.3 %copy-start.2 = (bf16[128,512]{1,0:T(8,128)(2,1)S(1)}, bf16[128,512]{1,0:T(8,128)(2,1)}, u32[]{:S(2)}) copy-start(bf16[128,512]{1,0:T(8,128)(2,1)} %param.7) | copy-start | bytes 393220
  0.7 21.4 %copy-start.3 = (s32[1,128]{1,0:T(1,128)S(1)}, s32[1,128]{1,0:T(1,128)}, u32[]{:S(2)}) copy-start(s32[1,128]{1,0:T(1,128)} %param.5) | copy-start | bytes 1540
  2.9 37.6 %all-to-all-start = ((bf16[64,4,2048]{2,1,0:T(4,128)(2,1)}), bf16[64,4,2048]{2,1,0:T(4,128)(2,1)S(1)}, u32[]{:S(2)}, u32[]{:S(2)}) async-start(bf16[64,4,2048]{2,1,0:T(4,128)(2,1)} %broadcast_in_dim.2), calls=%async_computation | async-start | bytes 2097152 | tf_op jit(solution)/shard_map/all_to_all | solution.py:74
  17.0 16.0 %collective-permute-start = (bf16[128,2048]{1,0:T(8,128)(2,1)S(1)}, bf16[128,2048]{1,0:T(8,128)(2,1)S(1)}, u32[]{:S(2)}, u32[]{:S(2)}) collective-permute-start(bf16[128,2048]{1,0:T(8,128)(2,1)S(1)} %copy-done), channel_id=1, source_target_pairs={{0,512},{512,0},{1,513},{513,1},{2,514},{514,2},{3,515},{515,3},{4... | collective-permute-start | bytes 1572872 | tf_op jit(solution)/shard_map/ppermute | solution.py:75
  23.7 9.3 %collective-permute-start.1 = (bf16[128,256]{1,0:T(8,128)(2,1)S(1)}, bf16[128,256]{1,0:T(8,128)(2,1)S(1)}, u32[]{:S(2)}, u32[]{:S(2)}) collective-permute-start(bf16[128,256]{1,0:T(8,128)(2,1)S(1)} %get-tuple-element.27), channel_id=1, source_target_pairs={{0,512},{512,0},{1,513},{513,1},{2,514},{514,2},{3,515},{515,3},{4... | collective-permute-start | bytes 196616 | tf_op jit(solution)/shard_map/ppermute | solution.py:80
  41.2 50.1 %copy-start.1 = (f32[128,64]{1,0:T(8,128)S(1)}, f32[128,64]{1,0:T(8,128)}, u32[]{:S(2)}) copy-start(f32[128,64]{1,0:T(8,128)} %get-tuple-element.29) | copy-start | bytes 98308
  41.2 63.3 %all-to-all-start.1 = ((bf16[64,4,2048]{2,1,0:T(4,128)(2,1)}), bf16[64,4,2048]{2,1,0:T(4,128)(2,1)S(1)}, u32[]{:S(2)}, u32[]{:S(2)}) async-start(bf16[64,4,2048]{2,1,0:T(4,128)(2,1)} %reshape.93), calls=%async_computation.1 | async-start | bytes 2097152 | tf_op jit(solution)/shard_map/all_to_all | solution.py:96
  52.2 44.1 %collective-permute-start.7 = (bf16[128,2048]{1,0:T(8,128)(2,1)}, bf16[128,2048]{1,0:T(8,128)(2,1)S(1)}, u32[]{:S(2)}, u32[]{:S(2)}) collective-permute-start(bf16[128,2048]{1,0:T(8,128)(2,1)} %convolution_convert_fusion), channel_id=1, source_target_pairs={{0,512},{512,0},{1,513},{513,1},{2,514},{514,2},{3,515},{515,3},{4... | collective-permute-start | bytes 1572872 | tf_op jit(solution)/shard_map/ppermute | solution.py:95
  59.0 5.1 %collective-permute-start.2 = (bf16[128,256]{1,0:T(8,128)(2,1)S(1)}, bf16[128,256]{1,0:T(8,128)(2,1)S(1)}, u32[]{:S(2)}, u32[]{:S(2)}) collective-permute-start(bf16[128,256]{1,0:T(8,128)(2,1)S(1)} %get-tuple-element.15), channel_id=1, source_target_pairs={{0,1},{1,0},{2,3},{3,2},{4,5},{5,4},{6,7},{7,6},{8,9},{9,8},{10,11... | collective-permute-start | bytes 196616 | tf_op jit(solution)/shard_map/ppermute | solution.py:91
  64.1 6.0 %collective-permute-start.3 = (bf16[64,256]{1,0:T(8,128)(2,1)S(1)}, bf16[64,256]{1,0:T(8,128)(2,1)S(1)}, u32[]{:S(2)}, u32[]{:S(2)}) collective-permute-start(bf16[64,256]{1,0:T(8,128)(2,1)S(1)} %get-tuple-element.17), channel_id=1, source_target_pairs={{0,512},{512,0},{1,513},{513,1},{2,514},{514,2},{3,515},{515,3},{4... | collective-permute-start | bytes 98312 | tf_op jit(solution)/shard_map/ppermute | solution.py:94
  70.2 21.2 %collective-permute-start.4 = (bf16[64,512]{1,0:T(8,128)(2,1)S(1)}, bf16[64,512]{1,0:T(8,128)(2,1)S(1)}, u32[]{:S(2)}, u32[]{:S(2)}) collective-permute-start(bf16[64,512]{1,0:T(8,128)(2,1)S(1)} %maximum_select_fusion.1), channel_id=1, source_target_pairs={{0,2},{2,4},{4,6},{6,0},{1,3},{3,5},{5,7},{7,1},{8,10},{10,12},{12... | collective-permute-start | bytes 196616 | tf_op jit(solution)/shard_map/ppermute | solution.py:102
  77.8 13.6 %collective-permute-start.5 = (bf16[64,512]{1,0:T(8,128)(2,1)S(1)}, bf16[64,512]{1,0:T(8,128)(2,1)S(1)}, u32[]{:S(2)}, u32[]{:S(2)}) collective-permute-start(bf16[64,512]{1,0:T(8,128)(2,1)S(1)} %maximum_select_fusion.1), channel_id=1, source_target_pairs={{0,6},{2,0},{4,2},{6,4},{1,7},{3,1},{5,3},{7,5},{8,14},{10,8},{12,... | collective-permute-start | bytes 196616 | tf_op jit(solution)/shard_map/ppermute | solution.py:102
  87.3 8.9 %collective-permute-start.6 = (bf16[64,512]{1,0:T(8,128)(2,1)S(1)}, bf16[64,512]{1,0:T(8,128)(2,1)S(1)}, u32[]{:S(2)}, u32[]{:S(2)}) collective-permute-start(bf16[64,512]{1,0:T(8,128)(2,1)S(1)} %maximum_select_fusion.1), channel_id=1, source_target_pairs={{0,4},{2,6},{4,0},{6,2},{1,5},{3,7},{5,1},{7,3},{8,12},{10,14},{12... | collective-permute-start | bytes 196616 | tf_op jit(solution)/shard_map/ppermute | solution.py:102
  96.7 7.1 %collective-permute-start.8 = (bf16[64,512]{1,0:T(8,128)(2,1)S(1)}, bf16[64,512]{1,0:T(8,128)(2,1)S(1)}, u32[]{:S(2)}, u32[]{:S(2)}) collective-permute-start(bf16[64,512]{1,0:T(8,128)(2,1)S(1)} %bitcast.18), channel_id=1, source_target_pairs={{0,1},{1,0},{2,3},{3,2},{4,5},{5,4},{6,7},{7,6},{8,9},{9,8},{10,11... | collective-permute-start | bytes 196616 | tf_op jit(solution)/shard_map/ppermute | solution.py:110

commit v4 on v3

--- a/solution.py
+++ b/solution.py
@@ -32,6 +32,10 @@
 
 def dot(a, b, da, db):
     return lax.dot_general(a, b, (((da,), (db,)), ((), ())), preferred_element_type=jnp.float32)
+
+
+def spread_kernel(w_ref, out_ref):
+    out_ref[...] = jnp.broadcast_to(w_ref[...][None], out_ref.shape)
 
 
 def kraw_kernel(tok_ref, par_ref, w_ref, keep_ref, send_ref):
@@ -70,7 +74,7 @@
     bf16, f32 = jnp.bfloat16, jnp.float32
     shape = jax.ShapeDtypeStruct
     zl, core = lax.axis_index("zl"), lax.axis_index("c")
-    spread = jnp.broadcast_to(key_weight[None], (64, 4, 2048))
+    spread = whole(spread_kernel, shape((64, 4, 2048), bf16), 1, "spread")(key_weight)
     gathered = lax.all_to_all(spread, ("y", "x"), 0, 0)
     tok_p = lax.ppermute(tokens, "zl", SWAP)
 
@@ -86,23 +90,22 @@
     keep, to_c = whole(kraw_kernel, (shape((128, 256), f32), shape((128, 256), bf16)), 3, "kraw")(
         tokens, tok_p, weights
     )
-    g_send = dot(kb_p, weights, 1, 0).astype(bf16)
     to_c, partial = lax.optimization_barrier((to_c, partial))
     from_c = lax.ppermute(to_c, "c", SWAP)
     half = shape((64, 256), bf16)
     own, to_z = whole(merge_kernel, (half, half), 2, "merge")(keep, from_c)
     from_z = lax.ppermute(to_z, "zl", SWAP)
-    g_par = lax.ppermute(g_send, "zl", SWAP)
     scattered = lax.all_to_all(partial, ("y", "x"), 0, 0)
 
     total_b = jnp.where(
         zl == 0, jnp.concatenate([own, from_z], 1), jnp.concatenate([from_z, own], 1)
     )
+    total_b, kb_p = lax.optimization_barrier((total_b, kb_p))
+    g_par = lax.ppermute(dot(kb_p, weights, 1, 0).astype(bf16), "zl", SWAP)
     one, three, two = (
         lax.ppermute(total_b, "zh", [(i, (i + step) % 4) for i in range(4)])
         for step in (1, 3, 2)
     )
-    one, three, two, g_par = lax.optimization_barrier((one, three, two, g_par))
     total = (total_b.astype(f32) + two.astype(f32)) + (one.astype(f32) + three.astype(f32))
     own_cos = lax.dynamic_slice_in_dim(cosine, core * 64, 64, 0)
     own_sin = lax.dynamic_slice_in_dim(sine, core * 64, 64, 0)

time: 106 us -> 104 us (0.981)
  local copies, waits for them, and re-layouts: 3.96 us -> 2.47 us
  Pallas kernels: 1.6 us -> 2.7 us
    ppermute x1, waiting for transfers between devices: 0.01 us -> 5.34 us  [body(): g_par = lax.ppermute(dot(kb_p, weights, 1, 0).astype(bf16), 'zl', SWAP)]
    ppermute x3, waiting for transfers between devices: 4.9 us -> 0.28 us  [body(): lax.ppermute(total_b, 'zh', [(i, (i + step) % 4) for i in range(4)])]
    ppermute x1, starting transfers between devices: 6.83 us -> 3.36 us  [body(): g_par = lax.ppermute(dot(kb_p, weights, 1, 0).astype(bf16), 'zl', SWAP)]
    ppermute x1, starting transfers between devices: 1.92 us -> 4.95 us  [body(): from_z = lax.ppermute(to_z, 'zl', SWAP)]
    ppermute x1, waiting for transfers between devices: 4.09 us -> 1.55 us  [body(): from_z = lax.ppermute(to_z, 'zl', SWAP)]
    broadcast_in_dim x1 -> x0, local copies, waits for them, and re-layouts: 2.27 us -> none  [body(): spread = jnp.broadcast_to(key_weight[None], (64, 4, 2048))]
    ppermute x1, starting transfers between devices: 4.19 us -> 5.8 us  [body(): from_c = lax.ppermute(to_c, 'c', SWAP)]
    pallas_call x0 -> x1, Pallas kernels: none -> 1.11 us  [body(): whole(spread_kernel, shape((64, 4, 2048), bf16), 1, 'spread')(key_weight)]
  transfers between devices with their start and end apart: 11 -> 11, of which waited for: 5 -> 7; matrix products, arithmetic and copies ran while one was open for 6% -> 5% of each run, Pallas kernels for 1% -> 1%
where the time goes in v4:
time: 104 us
  starting transfers between devices  71 us (68%)
  waiting for transfers between devices  21.6 us (21%)
  other arithmetic  3.69 us (4%)
  Pallas kernels  2.7 us (3%)
  local copies, waits for them, and re-layouts  2.47 us (2%)
  matrix products  1.22 us (1%)
    ppermute x3, starting transfers between devices, body(): lax.ppermute(total_b, 'zh', [(i, (i + step) % 4) for i in range(4)])  21.1 us
    all_to_all x1, starting transfers between devices, body(): gathered = lax.all_to_all(spread, ('y', 'x'), 0, 0)  14 us
    all_to_all x1, starting transfers between devices, body(): scattered = lax.all_to_all(partial, ('y', 'x'), 0, 0)  9.86 us
    ppermute x1, waiting for transfers between devices, body(): kb_p = lax.ppermute(jnp.where(zl == 0, right, left), 'zl', SWAP)  6.91 us
    ppermute x1, starting transfers between devices, body(): from_c = lax.ppermute(to_c, 'c', SWAP)  5.8 us
    all_to_all x1, waiting for transfers between devices, body(): gathered = lax.all_to_all(spread, ('y', 'x'), 0, 0)  5.78 us
    ppermute x1, waiting for transfers between devices, body(): g_par = lax.ppermute(dot(kb_p, weights, 1, 0).astype(bf16), 'zl', SWAP)  5.34 us
    ppermute x1, starting transfers between devices, body(): others = lax.ppermute(keys, 'c', SWAP)  5.05 us
  transfers between devices with their start and end apart: 11, of which 7 were waited for; matrix products, arithmetic and copies ran while one was open for 5% of the time, Pallas kernels for 1%

profile of v4, /device:TPU:1, one launch (start us, length us, event | category | flops | bytes accessed | tf_op | source)
XLA Modules:
  0.0 103.6 jit_solution(17153601866305573475)
XLA Ops:
  0.6 0.0 copy-start
  0.6 0.0 copy-start.1
  0.7 0.8 copy-done.1
  1.4 0.0 copy-start.3
  1.4 0.0 copy-start.4
  1.4 1.1 %spread.1 = bf16[64,4,2048]{2,1,0:T(4,128)(2,1)} custom-call(bf16[4,2048]{1,0:T(4,128)(2,1)S(1)} %copy-done.1), custom_call_target="tpu_custom_call" | custom-call | tf_op jit(solution)/shard_map/spread/pallas_call | solution.py:77
  2.5 14.0 %all-to-all-start = ((bf16[64,4,2048]{2,1,0:T(4,128)(2,1)}), bf16[64,4,2048]{2,1,0:T(4,128)(2,1)S(1)}, u32[]{:S(2)}, u32[]{:S(2)}) async-start(bf16[64,4,2048]{2,1,0:T(4,128)(2,1)} %spread.1), calls=%async_computation | async-start | bytes 2097152 | tf_op jit(solution)/shard_map/all_to_all | solution.py:78
  16.6 0.0 copy-done
  16.6 4.9 %collective-permute-start = (bf16[128,2048]{1,0:T(8,128)(2,1)S(1)}, bf16[128,2048]{1,0:T(8,128)(2,1)S(1)}, u32[]{:S(2)}, u32[]{:S(2)}) collective-permute-start(bf16[128,2048]{1,0:T(8,128)(2,1)S(1)} %copy-done), channel_id=1, source_target_pairs={{0,512},{512,0},{1,513},{513,1},{2,514},{514,2},{3,515},{515,3},{4... | collective-permute-start | bytes 1572872 | tf_op jit(solution)/shard_map/ppermute | solution.py:79
  21.5 0.0 copy-done.3
  21.5 0.1 reshape.95
  21.6 0.0 copy-done.4
  21.6 0.2 convert_reduce_fusion.1
  21.8 1.0 multiply_sine_fusion
  22.8 0.3 subtract_convert_fusion
  23.0 0.2 pad_maximum_fusion
  23.3 1.9 %collective-permute-start.1 = (bf16[128,256]{1,0:T(8,128)(2,1)S(1)}, bf16[128,256]{1,0:T(8,128)(2,1)S(1)}, u32[]{:S(2)}, u32[]{:S(2)}) collective-permute-start(bf16[128,256]{1,0:T(8,128)(2,1)S(1)} %get-tuple-element.23), channel_id=1, source_target_pairs={{0,512},{512,0},{1,513},{513,1},{2,514},{514,2},{3,515},{515,3},{4... | collective-permute-start | bytes 196616 | tf_op jit(solution)/shard_map/ppermute | solution.py:84
  25.2 0.5 fusion.1
  25.7 6.9 %collective-permute-done.1 = bf16[128,256]{1,0:T(8,128)(2,1)S(1)} collective-permute-done((bf16[128,256]{1,0:T(8,128)(2,1)S(1)}, bf16[128,256]{1,0:T(8,128)(2,1)S(1)}, u32[]{:S(2)}, u32[]{:S(2)}) %collective-permute-start.1) | collective-permute-done | bytes 65568 | tf_op jit(solution)/shard_map/ppermute | solution.py:84
  32.6 0.0 collective-permute-done.par_ref
  32.6 0.5 fusion
  33.1 1.2 %reshape.92 = bf16[64,4,2048]{2,1,0:T(4,128)(2,1)} reshape(bf16[256,2048]{1,0:T(8,128)(2,1)S(1)} %fusion) | data formatting | bytes 2097152 | tf_op jit(solution)/shard_map/reshape | solution.py:87
  34.3 5.8 %all-to-all-done = bf16[64,4,2048]{2,1,0:T(4,128)(2,1)S(1)} async-done(((bf16[64,4,2048]{2,1,0:T(4,128)(2,1)}), bf16[64,4,2048]{2,1,0:T(4,128)(2,1)S(1)}, u32[]{:S(2)}, u32[]{:S(2)}) %all-to-all-start) | async-done | bytes 1048608 | tf_op jit(solution)/shard_map/all_to_all | solution.py:78
  40.1 0.3 reshape.89.w_ref
  40.3 0.5 kraw.1
  40.8 0.0 copy-start.2
  40.8 9.9 %all-to-all-start.1 = ((bf16[64,4,2048]{2,1,0:T(4,128)(2,1)}), bf16[64,4,2048]{2,1,0:T(4,128)(2,1)S(1)}, u32[]{:S(2)}, u32[]{:S(2)}) async-start(bf16[64,4,2048]{2,1,0:T(4,128)(2,1)} %reshape.92), calls=%async_computation.1 | async-start | bytes 2097152 | tf_op jit(solution)/shard_map/all_to_all | solution.py:98
  50.7 5.8 %collective-permute-start.2 = (bf16[128,256]{1,0:T(8,128)(2,1)S(1)}, bf16[128,256]{1,0:T(8,128)(2,1)S(1)}, u32[]{:S(2)}, u32[]{:S(2)}) collective-permute-start(bf16[128,256]{1,0:T(8,128)(2,1)S(1)} %get-tuple-element.13), channel_id=1, source_target_pairs={{0,1},{1,0},{2,3},{3,2},{4,5},{5,4},{6,7},{7,6},{8,9},{9,8},{10,11... | collective-permute-start | bytes 196616 | tf_op jit(solution)/shard_map/ppermute | solution.py:94
  56.5 0.9 collective-permute-done.2.c_ref
  57.4 4.9 %collective-permute-start.3 = (bf16[64,256]{1,0:T(8,128)(2,1)S(1)}, bf16[64,256]{1,0:T(8,128)(2,1)S(1)}, u32[]{:S(2)}, u32[]{:S(2)}) collective-permute-start(bf16[64,256]{1,0:T(8,128)(2,1)S(1)} %get-tuple-element.15), channel_id=1, source_target_pairs={{0,512},{512,0},{1,513},{513,1},{2,514},{514,2},{3,515},{515,3},{4... | collective-permute-start | bytes 98312 | tf_op jit(solution)/shard_map/ppermute | solution.py:97
  62.4 0.0 copy-done.2
  62.4 1.6 %collective-permute-done.3 = bf16[64,256]{1,0:T(8,128)(2,1)S(1)} collective-permute-done((bf16[64,256]{1,0:T(8,128)(2,1)S(1)}, bf16[64,256]{1,0:T(8,128)(2,1)S(1)}, u32[]{:S(2)}, u32[]{:S(2)}) %collective-permute-start.3) | collective-permute-done | bytes 32800 | tf_op jit(solution)/shard_map/ppermute | solution.py:97
  64.0 13.4 %collective-permute-start.4 = (bf16[64,512]{1,0:T(8,128)(2,1)S(1)}, bf16[64,512]{1,0:T(8,128)(2,1)S(1)}, u32[]{:S(2)}, u32[]{:S(2)}) collective-permute-start(bf16[64,512]{1,0:T(8,128)(2,1)S(1)} %maximum_select_fusion.1), channel_id=1, source_target_pairs={{0,4},{2,6},{4,0},{6,2},{1,5},{3,7},{5,1},{7,3},{8,12},{10,14},{12... | collective-permute-start | bytes 196616 | tf_op jit(solution)/shard_map/ppermute | solution.py:106
  77.3 5.8 %collective-permute-start.5 = (bf16[64,512]{1,0:T(8,128)(2,1)S(1)}, bf16[64,512]{1,0:T(8,128)(2,1)S(1)}, u32[]{:S(2)}, u32[]{:S(2)}) collective-permute-start(bf16[64,512]{1,0:T(8,128)(2,1)S(1)} %maximum_select_fusion.1), channel_id=1, source_target_pairs={{0,2},{2,4},{4,6},{6,0},{1,3},{3,5},{5,7},{7,1},{8,10},{10,12},{12... | collective-permute-start | bytes 196616 | tf_op jit(solution)/shard_map/ppermute | solution.py:106
  83.2 1.9 %collective-permute-start.6 = (bf16[64,512]{1,0:T(8,128)(2,1)S(1)}, bf16[64,512]{1,0:T(8,128)(2,1)S(1)}, u32[]{:S(2)}, u32[]{:S(2)}) collective-permute-start(bf16[64,512]{1,0:T(8,128)(2,1)S(1)} %maximum_select_fusion.1), channel_id=1, source_target_pairs={{0,6},{2,0},{4,2},{6,4},{1,7},{3,1},{5,3},{7,5},{8,14},{10,8},{12,... | collective-permute-start | bytes 196616 | tf_op jit(solution)/shard_map/ppermute | solution.py:106
  85.1 0.3 convolution_convert_fusion
  85.4 3.4 %collective-permute-start.8 = (bf16[128,2048]{1,0:T(8,128)(2,1)S(1)}, bf16[128,2048]{1,0:T(8,128)(2,1)S(1)}, u32[]{:S(2)}, u32[]{:S(2)}) collective-permute-start(bf16[128,2048]{1,0:T(8,128)(2,1)S(1)} %convolution_convert_fusion), channel_id=1, source_target_pairs={{0,512},{512,0},{1,513},{513,1},{2,514},{514,2},{3,515},{515,3},{4... | collective-permute-start | bytes 1572872 | tf_op jit(solution)/shard_map/ppermute | solution.py:104
  88.8 0.0 collective-permute-done.4
  88.8 0.0 collective-permute-done.5
  88.8 0.3 collective-permute-done.6
  89.2 0.2 subtract_convert_fusion.1
  89.4 0.1 pad_maximum_fusion.1
  89.5 5.1 %collective-permute-start.7 = (bf16[64,512]{1,0:T(8,128)(2,1)S(1)}, bf16[64,512]{1,0:T(8,128)(2,1)S(1)}, u32[]{:S(2)}, u32[]{:S(2)}) collective-permute-start(bf16[64,512]{1,0:T(8,128)(2,1)S(1)} %bitcast.18), channel_id=1, source_target_pairs={{0,1},{1,0},{2,3},{3,2},{4,5},{5,4},{6,7},{7,6},{8,9},{9,8},{10,11... | collective-permute-start | bytes 196616 | tf_op jit(solution)/shard_map/ppermute | solution.py:113
  94.6 0.9 collective-permute-done.7
  95.4 0.7 maximum_select_fusion
  96.1 5.3 %collective-permute-done.8.add_ref = bf16[128,2048]{1,0:T(8,128)(2,1)S(1)} collective-permute-done((bf16[128,2048]{1,0:T(8,128)(2,1)S(1)}, bf16[128,2048]{1,0:T(8,128)(2,1)S(1)}, u32[]{:S(2)}, u32[]{:S(2)}) %collective-permute-start.8) | collective-permute-done | bytes 524320 | tf_op jit(solution)/shard_map/ppermute | solution.py:104
  101.5 1.1 %grad.1 = bf16[128,2048]{1,0:T(8,128)(2,1)} custom-call(bf16[128,256]{1,0:T(8,128)(2,1)S(1)} %get-tuple-element.24.kb_ref, bf16[256,2048]{1,0:T(8,128)(2,1)S(1)} %reshape.89.w_ref, bf16[128,2048]{1,0:T(8,128)(2,1)S(1)} %collective-permute-done.8.add_ref), custom_call_target="tpu_custom_call" | custom-call | tf_op jit(solution)/shard_map/grad/pallas_call | solution.py:116
  102.6 0.0 all-to-all-done.1
  102.6 1.1 %convert_reduce_fusion = f32[4,2048]{1,0:T(4,128)} fusion(bf16[64,4,2048]{2,1,0:T(4,128)(2,1)S(1)} %all-to-all-done.1), kind=kLoop, calls=%fused_computation.3 | loop fusion | flops 1040384 | bytes 1081344 | tf_op jit(solution)/shard_map/reduce_sum | solution.py:117
  (10 shorter events, 0.2 us)
Async XLA Ops:
  0.6 15.9 %copy-start = (bf16[128,2048]{1,0:T(8,128)(2,1)S(1)}, bf16[128,2048]{1,0:T(8,128)(2,1)}, u32[]{:S(2)}) copy-start(bf16[128,2048]{1,0:T(8,128)(2,1)} %tok_ref.1) | copy-start | bytes 1572868
  0.6 0.8 copy-start.1
  1.4 20.1 %copy-start.3 = (bf16[128,512]{1,0:T(8,128)(2,1)S(1)}, bf16[128,512]{1,0:T(8,128)(2,1)}, u32[]{:S(2)}) copy-start(bf16[128,512]{1,0:T(8,128)(2,1)} %param.7) | copy-start | bytes 393220
  1.4 20.2 %copy-start.4 = (s32[1,128]{1,0:T(1,128)S(1)}, s32[1,128]{1,0:T(1,128)}, u32[]{:S(2)}) copy-start(s32[1,128]{1,0:T(1,128)} %param.5) | copy-start | bytes 1540
  2.5 37.6 %all-to-all-start = ((bf16[64,4,2048]{2,1,0:T(4,128)(2,1)}), bf16[64,4,2048]{2,1,0:T(4,128)(2,1)S(1)}, u32[]{:S(2)}, u32[]{:S(2)}) async-start(bf16[64,4,2048]{2,1,0:T(4,128)(2,1)} %spread.1), calls=%async_computation | async-start | bytes 2097152 | tf_op jit(solution)/shard_map/all_to_all | solution.py:78
  16.6 16.0 %collective-permute-start = (bf16[128,2048]{1,0:T(8,128)(2,1)S(1)}, bf16[128,2048]{1,0:T(8,128)(2,1)S(1)}, u32[]{:S(2)}, u32[]{:S(2)}) collective-permute-start(bf16[128,2048]{1,0:T(8,128)(2,1)S(1)} %copy-done), channel_id=1, source_target_pairs={{0,512},{512,0},{1,513},{513,1},{2,514},{514,2},{3,515},{515,3},{4... | collective-permute-start | bytes 1572872 | tf_op jit(solution)/shard_map/ppermute | solution.py:79
  23.3 9.3 %collective-permute-start.1 = (bf16[128,256]{1,0:T(8,128)(2,1)S(1)}, bf16[128,256]{1,0:T(8,128)(2,1)S(1)}, u32[]{:S(2)}, u32[]{:S(2)}) collective-permute-start(bf16[128,256]{1,0:T(8,128)(2,1)S(1)} %get-tuple-element.23), channel_id=1, source_target_pairs={{0,512},{512,0},{1,513},{513,1},{2,514},{514,2},{3,515},{515,3},{4... | collective-permute-start | bytes 196616 | tf_op jit(solution)/shard_map/ppermute | solution.py:84
  40.8 21.5 %copy-start.2 = (f32[128,64]{1,0:T(8,128)S(1)}, f32[128,64]{1,0:T(8,128)}, u32[]{:S(2)}) copy-start(f32[128,64]{1,0:T(8,128)} %get-tuple-element.25) | copy-start | bytes 98308
  40.8 61.7 %all-to-all-start.1 = ((bf16[64,4,2048]{2,1,0:T(4,128)(2,1)}), bf16[64,4,2048]{2,1,0:T(4,128)(2,1)S(1)}, u32[]{:S(2)}, u32[]{:S(2)}) async-start(bf16[64,4,2048]{2,1,0:T(4,128)(2,1)} %reshape.92), calls=%async_computation.1 | async-start | bytes 2097152 | tf_op jit(solution)/shard_map/all_to_all | solution.py:98
  50.7 6.7 %collective-permute-start.2 = (bf16[128,256]{1,0:T(8,128)(2,1)S(1)}, bf16[128,256]{1,0:T(8,128)(2,1)S(1)}, u32[]{:S(2)}, u32[]{:S(2)}) collective-permute-start(bf16[128,256]{1,0:T(8,128)(2,1)S(1)} %get-tuple-element.13), channel_id=1, source_target_pairs={{0,1},{1,0},{2,3},{3,2},{4,5},{5,4},{6,7},{7,6},{8,9},{9,8},{10,11... | collective-permute-start | bytes 196616 | tf_op jit(solution)/shard_map/ppermute | solution.py:94
  57.4 6.5 %collective-permute-start.3 = (bf16[64,256]{1,0:T(8,128)(2,1)S(1)}, bf16[64,256]{1,0:T(8,128)(2,1)S(1)}, u32[]{:S(2)}, u32[]{:S(2)}) collective-permute-start(bf16[64,256]{1,0:T(8,128)(2,1)S(1)} %get-tuple-element.15), channel_id=1, source_target_pairs={{0,512},{512,0},{1,513},{513,1},{2,514},{514,2},{3,515},{515,3},{4... | collective-permute-start | bytes 98312 | tf_op jit(solution)/shard_map/ppermute | solution.py:97
  64.0 24.8 %collective-permute-start.4 = (bf16[64,512]{1,0:T(8,128)(2,1)S(1)}, bf16[64,512]{1,0:T(8,128)(2,1)S(1)}, u32[]{:S(2)}, u32[]{:S(2)}) collective-permute-start(bf16[64,512]{1,0:T(8,128)(2,1)S(1)} %maximum_select_fusion.1), channel_id=1, source_target_pairs={{0,4},{2,6},{4,0},{6,2},{1,5},{3,7},{5,1},{7,3},{8,12},{10,14},{12... | collective-permute-start | bytes 196616 | tf_op jit(solution)/shard_map/ppermute | solution.py:106
  77.3 11.5 %collective-permute-start.5 = (bf16[64,512]{1,0:T(8,128)(2,1)S(1)}, bf16[64,512]{1,0:T(8,128)(2,1)S(1)}, u32[]{:S(2)}, u32[]{:S(2)}) collective-permute-start(bf16[64,512]{1,0:T(8,128)(2,1)S(1)} %maximum_select_fusion.1), channel_id=1, source_target_pairs={{0,2},{2,4},{4,6},{6,0},{1,3},{3,5},{5,7},{7,1},{8,10},{10,12},{12... | collective-permute-start | bytes 196616 | tf_op jit(solution)/shard_map/ppermute | solution.py:106
  83.2 5.9 %collective-permute-start.6 = (bf16[64,512]{1,0:T(8,128)(2,1)S(1)}, bf16[64,512]{1,0:T(8,128)(2,1)S(1)}, u32[]{:S(2)}, u32[]{:S(2)}) collective-permute-start(bf16[64,512]{1,0:T(8,128)(2,1)S(1)} %maximum_select_fusion.1), channel_id=1, source_target_pairs={{0,6},{2,0},{4,2},{6,4},{1,7},{3,1},{5,3},{7,5},{8,14},{10,8},{12,... | collective-permute-start | bytes 196616 | tf_op jit(solution)/shard_map/ppermute | solution.py:106
  85.4 16.0 %collective-permute-start.8 = (bf16[128,2048]{1,0:T(8,128)(2,1)S(1)}, bf16[128,2048]{1,0:T(8,128)(2,1)S(1)}, u32[]{:S(2)}, u32[]{:S(2)}) collective-permute-start(bf16[128,2048]{1,0:T(8,128)(2,1)S(1)} %convolution_convert_fusion), channel_id=1, source_target_pairs={{0,512},{512,0},{1,513},{513,1},{2,514},{514,2},{3,515},{515,3},{4... | collective-permute-start | bytes 1572872 | tf_op jit(solution)/shard_map/ppermute | solution.py:104
  89.5 5.9 %collective-permute-start.7 = (bf16[64,512]{1,0:T(8,128)(2,1)S(1)}, bf16[64,512]{1,0:T(8,128)(2,1)S(1)}, u32[]{:S(2)}, u32[]{:S(2)}) collective-permute-start(bf16[64,512]{1,0:T(8,128)(2,1)S(1)} %bitcast.18), channel_id=1, source_target_pairs={{0,1},{1,0},{2,3},{3,2},{4,5},{5,4},{6,7},{7,6},{8,9},{9,8},{10,11... | collective-permute-start | bytes 196616 | tf_op jit(solution)/shard_map/ppermute | solution.py:113

commit v5 on v4

--- a/solution.py
+++ b/solution.py
@@ -48,7 +48,8 @@
 
 
 def merge_kernel(keep_ref, c_ref, own_ref, far_ref):
-    out = (keep_ref[...] + c_ref[...].astype(jnp.float32)).astype(jnp.bfloat16)
+    theirs = c_ref[1 - lax.axis_index("c")].astype(jnp.float32)
+    out = (keep_ref[...] + theirs).astype(jnp.bfloat16)
     own_ref[...] = out[:64]
     far_ref[...] = out[64:]
 
@@ -91,27 +92,24 @@
         tokens, tok_p, weights
     )
     to_c, partial = lax.optimization_barrier((to_c, partial))
-    from_c = lax.ppermute(to_c, "c", SWAP)
+    from_c = lax.all_gather(to_c, "c")
     half = shape((64, 256), bf16)
     own, to_z = whole(merge_kernel, (half, half), 2, "merge")(keep, from_c)
-    from_z = lax.ppermute(to_z, "zl", SWAP)
+    from_z = lax.all_gather(to_z, "zl")
     scattered = lax.all_to_all(partial, ("y", "x"), 0, 0)
 
     total_b = jnp.where(
-        zl == 0, jnp.concatenate([own, from_z], 1), jnp.concatenate([from_z, own], 1)
+        zl == 0, jnp.concatenate([own, from_z[1]], 1), jnp.concatenate([from_z[0], own], 1)
     )
     total_b, kb_p = lax.optimization_barrier((total_b, kb_p))
     g_par = lax.ppermute(dot(kb_p, weights, 1, 0).astype(bf16), "zl", SWAP)
-    one, three, two = (
-        lax.ppermute(total_b, "zh", [(i, (i + step) % 4) for i in range(4)])
-        for step in (1, 3, 2)
-    )
-    total = (total_b.astype(f32) + two.astype(f32)) + (one.astype(f32) + three.astype(f32))
+    every = lax.all_gather(total_b, "zh")
+    every, g_par = lax.optimization_barrier((every, g_par))
+    total = jnp.sum(every.astype(f32), axis=0)
     own_cos = lax.dynamic_slice_in_dim(cosine, core * 64, 64, 0)
     own_sin = lax.dynamic_slice_in_dim(sine, core * 64, 64, 0)
     keys = rotate(total, own_cos, own_sin, 1.0).astype(bf16)
-    others = lax.ppermute(keys, "c", SWAP)
-    keys = jnp.where(core == 0, jnp.concatenate([keys, others]), jnp.concatenate([others, keys]))
+    keys = lax.all_gather(keys, "c", axis=0, tiled=True)
 
     grad_tokens = whole(grad_kernel, shape((128, 2048), bf16), 3, "grad")(kb, weights, g_par)
     grad_key_weight = jnp.sum(scattered.astype(f32), axis=0)

time: 104 us -> 107 us (1.029)
  blocking collectives: 0 us -> 47.9 us
  starting transfers between devices: 71 us -> 34.1 us
  waiting for transfers between devices: 21.6 us -> 12.7 us
    all_gather x0 -> x4, blocking collectives: none -> 47.9 us  [the longest x1 31.7 us: body(): every = lax.all_gather(total_b, 'zh')]
    ppermute x6 -> x0, starting transfers between devices: 36.9 us -> none  [the longest x3 21.1 us: body(): lax.ppermute(total_b, 'zh', [(i, (i + step) % 4) for i in range(4)])]
    ppermute x1, waiting for transfers between devices: 5.34 us -> 0.01 us  [body(): g_par = lax.ppermute(dot(kb_p, weights, 1, 0).astype(bf16), 'zl', SWAP)]
    ppermute x6 -> x0, waiting for transfers between devices: 3.58 us -> none  [the longest x1 1.55 us: body(): from_z = lax.ppermute(to_z, 'zl', SWAP)]
  transfers between devices with their start and end apart: 11 -> 5, of which waited for: 7 -> 2; matrix products, arithmetic and copies ran while one was open for 5% -> 5% of each run, Pallas kernels for 1% -> 1%
where the time goes in v5:
time: 107 us; the launch traced here: 106 us
  blocking collectives  47.9 us (45%)
  starting transfers between devices  34.1 us (32%)
  waiting for transfers between devices  12.7 us (12%)
  local copies, waits for them, and re-layouts  3.1 us (3%)
  other arithmetic  3.01 us (3%)
  Pallas kernels  2.7 us (3%)
  matrix products  2.01 us (2%)
    all_gather x1, blocking collectives, body(): every = lax.all_gather(total_b, 'zh')  31.7 us
    all_to_all x1, starting transfers between devices, body(): gathered = lax.all_to_all(spread, ('y', 'x'), 0, 0)  14 us
    all_to_all x1, starting transfers between devices, body(): scattered = lax.all_to_all(partial, ('y', 'x'), 0, 0)  9.85 us
    ppermute x1, waiting for transfers between devices, body(): kb_p = lax.ppermute(jnp.where(zl == 0, right, left), 'zl', SWAP)  6.91 us
    all_to_all x1, waiting for transfers between devices, body(): gathered = lax.all_to_all(spread, ('y', 'x'), 0, 0)  5.81 us
    all_gather x1, blocking collectives, body(): keys = lax.all_gather(keys, 'c', axis=0, tiled=True)  5.52 us
    all_gather x1, blocking collectives, body(): from_c = lax.all_gather(to_c, 'c')  5.44 us
    all_gather x1, blocking collectives, body(): from_z = lax.all_gather(to_z, 'zl')  5.29 us
  transfers between devices with their start and end apart: 5, of which 2 were waited for; matrix products, arithmetic and copies ran while one was open for 5% of the time, Pallas kernels for 1%

profile of v5, /device:TPU:1, one launch (start us, length us, event | category | flops | bytes accessed | tf_op | source)
XLA Modules:
  0.0 106.4 jit_solution(1871432989327273228)
XLA Ops:
  0.6 0.0 copy-start
  0.6 0.0 copy-start.1
  0.7 0.8 copy-done.1
  1.4 0.0 copy-start.3
  1.4 0.0 copy-start.4
  1.4 1.1 %spread.1 = bf16[64,4,2048]{2,1,0:T(4,128)(2,1)} custom-call(bf16[4,2048]{1,0:T(4,128)(2,1)S(1)} %copy-done.1), custom_call_target="tpu_custom_call" | custom-call | tf_op jit(solution)/shard_map/spread/pallas_call | solution.py:78
  2.5 14.0 %all-to-all-start = ((bf16[64,4,2048]{2,1,0:T(4,128)(2,1)}), bf16[64,4,2048]{2,1,0:T(4,128)(2,1)S(1)}, u32[]{:S(2)}, u32[]{:S(2)}) async-start(bf16[64,4,2048]{2,1,0:T(4,128)(2,1)} %spread.1), calls=%async_computation | async-start | bytes 2097152 | tf_op jit(solution)/shard_map/all_to_all | solution.py:79
  16.6 0.0 copy-done
  16.6 4.9 %collective-permute-start = (bf16[128,2048]{1,0:T(8,128)(2,1)S(1)}, bf16[128,2048]{1,0:T(8,128)(2,1)S(1)}, u32[]{:S(2)}, u32[]{:S(2)}) collective-permute-start(bf16[128,2048]{1,0:T(8,128)(2,1)S(1)} %copy-done), channel_id=1, source_target_pairs={{0,512},{512,0},{1,513},{513,1},{2,514},{514,2},{3,515},{515,3},{4... | collective-permute-start | bytes 1572872 | tf_op jit(solution)/shard_map/ppermute | solution.py:80
  21.5 0.0 copy-done.3
  21.5 0.1 reshape.95
  21.6 0.0 copy-done.4
  21.6 0.2 convert_reduce_fusion.2
  21.8 1.0 multiply_sine_fusion
  22.8 0.3 subtract_convert_fusion
  23.0 0.2 pad_maximum_fusion
  23.3 1.9 %collective-permute-start.1 = (bf16[128,256]{1,0:T(8,128)(2,1)S(1)}, bf16[128,256]{1,0:T(8,128)(2,1)S(1)}, u32[]{:S(2)}, u32[]{:S(2)}) collective-permute-start(bf16[128,256]{1,0:T(8,128)(2,1)S(1)} %get-tuple-element.27), channel_id=1, source_target_pairs={{0,512},{512,0},{1,513},{513,1},{2,514},{514,2},{3,515},{515,3},{4... | collective-permute-start | bytes 196616 | tf_op jit(solution)/shard_map/ppermute | solution.py:85
  25.2 0.5 fusion.2
  25.7 6.9 %collective-permute-done.1 = bf16[128,256]{1,0:T(8,128)(2,1)S(1)} collective-permute-done((bf16[128,256]{1,0:T(8,128)(2,1)S(1)}, bf16[128,256]{1,0:T(8,128)(2,1)S(1)}, u32[]{:S(2)}, u32[]{:S(2)}) %collective-permute-start.1) | collective-permute-done | bytes 65568 | tf_op jit(solution)/shard_map/ppermute | solution.py:85
  32.6 0.0 collective-permute-done.par_ref
  32.6 0.5 fusion
  33.0 1.2 %reshape.92 = bf16[64,4,2048]{2,1,0:T(4,128)(2,1)} reshape(bf16[256,2048]{1,0:T(8,128)(2,1)S(1)} %fusion) | data formatting | bytes 2097152 | tf_op jit(solution)/shard_map/reshape | solution.py:88
  34.3 5.8 %all-to-all-done = bf16[64,4,2048]{2,1,0:T(4,128)(2,1)S(1)} async-done(((bf16[64,4,2048]{2,1,0:T(4,128)(2,1)}), bf16[64,4,2048]{2,1,0:T(4,128)(2,1)S(1)}, u32[]{:S(2)}, u32[]{:S(2)}) %all-to-all-start) | async-done | bytes 1048608 | tf_op jit(solution)/shard_map/all_to_all | solution.py:79
  40.1 0.3 reshape.89.w_ref
  40.3 0.5 kraw.1
  40.8 0.0 copy-start.2
  40.8 9.9 %all-to-all-start.1 = ((bf16[64,4,2048]{2,1,0:T(4,128)(2,1)}), bf16[64,4,2048]{2,1,0:T(4,128)(2,1)S(1)}, u32[]{:S(2)}, u32[]{:S(2)}) async-start(bf16[64,4,2048]{2,1,0:T(4,128)(2,1)} %reshape.92), calls=%async_computation.1 | async-start | bytes 2097152 | tf_op jit(solution)/shard_map/all_to_all | solution.py:99
  50.7 5.4 %all-gather = bf16[256,256]{1,0:T(8,128)(2,1)S(1)} all-gather(bf16[128,256]{1,0:T(8,128)(2,1)S(1)} %get-tuple-element.15), channel_id=2, replica_groups=mesh['zl'=2,'y'=8,'x'=8,'zh'=4,'c'=2] {'c'}, dimensions={0}, use_global_device_ids=true | all-gather | bytes 196608 | tf_op jit(solution)/shard_map/all_gather | solution.py:95
  56.1 5.3 %all-gather.1 = bf16[128,256]{1,0:T(8,128)(2,1)S(1)} all-gather(bf16[64,256]{1,0:T(8,128)(2,1)S(1)} %get-tuple-element.17), channel_id=3, replica_groups=mesh['zl'=2,'y'=8,'x'=8,'zh'=4,'c'=2] {'zl'}, dimensions={0}, use_global_device_ids=true | all-gather | bytes 98304 | tf_op jit(solution)/shard_map/all_gather | solution.py:98
  61.5 1.1 %convolution_convert_fusion = bf16[128,2048]{1,0:T(8,128)(2,1)} fusion(bf16[128,256]{1,0:T(8,128)(2,1)S(1)} %collective-permute-done.1, bf16[256,2048]{1,0:T(8,128)(2,1)S(1)} %reshape.89.w_ref), kind=kOutput, calls=%fused_computation.2 | convolution fusion | flops 134479872 | bytes 1638400 | tf_op jit(solution)/shard_map/dot_general | solution.py:34
  62.6 3.4 %collective-permute-start.2 = (bf16[128,2048]{1,0:T(8,128)(2,1)}, bf16[128,2048]{1,0:T(8,128)(2,1)S(1)}, u32[]{:S(2)}, u32[]{:S(2)}) collective-permute-start(bf16[128,2048]{1,0:T(8,128)(2,1)} %convolution_convert_fusion), channel_id=1, source_target_pairs={{0,512},{512,0},{1,513},{513,1},{2,514},{514,2},{3,515},{515,3},{4... | collective-permute-start | bytes 1572872 | tf_op jit(solution)/shard_map/ppermute | solution.py:105
  66.0 0.0 copy-done.2
  66.0 31.7 %all-gather.2 = bf16[256,512]{1,0:T(8,128)(2,1)S(1)} all-gather(bf16[64,512]{1,0:T(8,128)(2,1)S(1)} %maximum_select_fusion), channel_id=4, replica_groups=mesh['zl'=2,'y'=8,'x'=8,'zh'=4,'c'=2] {'zh'}, dimensions={0}, use_global_device_ids=true | all-gather | bytes 327680 | tf_op jit(solution)/shard_map/all_gather | solution.py:106
  97.7 0.0 collective-permute-done.2.add_ref
  97.7 1.1 %grad.1 = bf16[128,2048]{1,0:T(8,128)(2,1)} custom-call(bf16[128,256]{1,0:T(8,128)(2,1)S(1)} %get-tuple-element.28.kb_ref, bf16[256,2048]{1,0:T(8,128)(2,1)S(1)} %reshape.89.w_ref, bf16[128,2048]{1,0:T(8,128)(2,1)S(1)} %collective-permute-done.2.add_ref), custom_call_target="tpu_custom_call" | custom-call | tf_op jit(solution)/shard_map/grad/pallas_call | solution.py:114
  98.9 0.2 subtract_convert_fusion.1
  99.1 0.1 pad_maximum_fusion.1
  99.2 5.5 %all_gather.27 = bf16[128,512]{1,0:T(8,128)(2,1)S(1)} all-gather(bf16[64,512]{1,0:T(8,128)(2,1)S(1)} %bitcast.22), channel_id=1, replica_groups=mesh['zl'=2,'y'=8,'x'=8,'zh'=4,'c'=2] {'c'}, dimensions={0}, use_global_device_ids=true | all-gather | bytes 196608 | tf_op jit(solution)/shard_map/all_gather | solution.py:112
  104.7 0.0 all-to-all-done.1
  104.7 1.1 convert_reduce_fusion
  105.8 0.7 copy.14
  (11 shorter events, 0.2 us)
Async XLA Ops:
  0.6 15.9 %copy-start = (bf16[128,2048]{1,0:T(8,128)(2,1)S(1)}, bf16[128,2048]{1,0:T(8,128)(2,1)}, u32[]{:S(2)}) copy-start(bf16[128,2048]{1,0:T(8,128)(2,1)} %tok_ref.1) | copy-start | bytes 1572868
  0.6 0.8 copy-start.1
  1.4 20.1 %copy-start.3 = (bf16[128,512]{1,0:T(8,128)(2,1)S(1)}, bf16[128,512]{1,0:T(8,128)(2,1)}, u32[]{:S(2)}) copy-start(bf16[128,512]{1,0:T(8,128)(2,1)} %param.7) | copy-start | bytes 393220
  1.4 20.2 %copy-start.4 = (s32[1,128]{1,0:T(1,128)S(1)}, s32[1,128]{1,0:T(1,128)}, u32[]{:S(2)}) copy-start(s32[1,128]{1,0:T(1,128)} %param.5) | copy-start | bytes 1540
  2.5 37.6 %all-to-all-start = ((bf16[64,4,2048]{2,1,0:T(4,128)(2,1)}), bf16[64,4,2048]{2,1,0:T(4,128)(2,1)S(1)}, u32[]{:S(2)}, u32[]{:S(2)}) async-start(bf16[64,4,2048]{2,1,0:T(4,128)(2,1)} %spread.1), calls=%async_computation | async-start | bytes 2097152 | tf_op jit(solution)/shard_map/all_to_all | solution.py:79
  16.6 16.0 %collective-permute-start = (bf16[128,2048]{1,0:T(8,128)(2,1)S(1)}, bf16[128,2048]{1,0:T(8,128)(2,1)S(1)}, u32[]{:S(2)}, u32[]{:S(2)}) collective-permute-start(bf16[128,2048]{1,0:T(8,128)(2,1)S(1)} %copy-done), channel_id=1, source_target_pairs={{0,512},{512,0},{1,513},{513,1},{2,514},{514,2},{3,515},{515,3},{4... | collective-permute-start | bytes 1572872 | tf_op jit(solution)/shard_map/ppermute | solution.py:80
  23.3 9.3 %collective-permute-start.1 = (bf16[128,256]{1,0:T(8,128)(2,1)S(1)}, bf16[128,256]{1,0:T(8,128)(2,1)S(1)}, u32[]{:S(2)}, u32[]{:S(2)}) collective-permute-start(bf16[128,256]{1,0:T(8,128)(2,1)S(1)} %get-tuple-element.27), channel_id=1, source_target_pairs={{0,512},{512,0},{1,513},{513,1},{2,514},{514,2},{3,515},{515,3},{4... | collective-permute-start | bytes 196616 | tf_op jit(solution)/shard_map/ppermute | solution.py:85
  40.8 25.2 %copy-start.2 = (f32[128,64]{1,0:T(8,128)S(1)}, f32[128,64]{1,0:T(8,128)}, u32[]{:S(2)}) copy-start(f32[128,64]{1,0:T(8,128)} %get-tuple-element.31) | copy-start | bytes 98308
  40.8 63.9 %all-to-all-start.1 = ((bf16[64,4,2048]{2,1,0:T(4,128)(2,1)}), bf16[64,4,2048]{2,1,0:T(4,128)(2,1)S(1)}, u32[]{:S(2)}, u32[]{:S(2)}) async-start(bf16[64,4,2048]{2,1,0:T(4,128)(2,1)} %reshape.92), calls=%async_computation.1 | async-start | bytes 2097152 | tf_op jit(solution)/shard_map/all_to_all | solution.py:99
  62.6 35.1 %collective-permute-start.2 = (bf16[128,2048]{1,0:T(8,128)(2,1)}, bf16[128,2048]{1,0:T(8,128)(2,1)S(1)}, u32[]{:S(2)}, u32[]{:S(2)}) collective-permute-start(bf16[128,2048]{1,0:T(8,128)(2,1)} %convolution_convert_fusion), channel_id=1, source_target_pairs={{0,512},{512,0},{1,513},{513,1},{2,514},{514,2},{3,515},{515,3},{4... | collective-permute-start | bytes 1572872 | tf_op jit(solution)/shard_map/ppermute | solution.py:105

commit v6 on v5

--- a/solution.py
+++ b/solution.py
@@ -34,24 +34,55 @@
     return lax.dot_general(a, b, (((da,), (db,)), ((), ())), preferred_element_type=jnp.float32)
 
 
+def ahead(k):
+    pairs = []
+    for y in range(8):
+        for x in range(8):
+            pairs.append(((y * 8 + x) * 2, ((y + k) % 8 * 8 + x) * 2))
+            pairs.append(((y * 8 + x) * 2 + 1, (y * 8 + (x + k) % 8) * 2 + 1))
+    return pairs
+
+
+def across():
+    rows = [[(y * 8 + x) * 2 for x in range(8)] for y in range(8)]
+    return rows + [[(y * 8 + x) * 2 + 1 for y in range(8)] for x in range(8)]
+
+
 def spread_kernel(w_ref, out_ref):
     out_ref[...] = jnp.broadcast_to(w_ref[...][None], out_ref.shape)
 
 
-def kraw_kernel(tok_ref, par_ref, w_ref, keep_ref, send_ref):
-    mine = pl.multiple_of(lax.axis_index("c") * 64, 64)
-    other = pl.multiple_of(64 - mine, 64)
-    halves = [ref[pl.ds(at, 64), :] for at in (mine, other) for ref in (tok_ref, par_ref)]
-    out = dot(jnp.concatenate(halves, axis=0), w_ref[...], 1, 1)
-    keep_ref[...] = out[:128]
-    send_ref[...] = out[128:].astype(jnp.bfloat16)
+def partial_kernel(kb_ref, kbp_ref, tok_ref, par_ref, own_ref, *out_refs):
+    bf16 = jnp.bfloat16
+    core = lax.axis_index("c")
+    place = jnp.where(core == 0, lax.axis_index("y"), lax.axis_index("x"))
+    row = lax.broadcasted_iota(jnp.int32, (256, 256), 0)
+    feature = lax.broadcasted_iota(jnp.int32, (256, 256), 1)
+    ahead, inner = ((row >> 5) + place) & 7, row & 31
+    by_y = ahead * 32 + inner
+    by_x = (inner >> 2) * 32 + ahead * 4 + (inner & 3)
+    pick = jnp.where(feature == jnp.where(core == 0, by_y, by_x), 1.0, 0.0).astype(bf16)
+    out = dot(dot(pick, kb_ref[...], 1, 1).astype(bf16), tok_ref[...], 1, 0)
+    out = out + dot(dot(pick, kbp_ref[...], 1, 1).astype(bf16), par_ref[...], 1, 0)
+    own_ref[...] = out[:32]
+    for k, out_ref in enumerate(out_refs):
+        out_ref[...] = out[32 * (k + 1) : 32 * (k + 2)].astype(bf16)
 
 
-def merge_kernel(keep_ref, c_ref, own_ref, far_ref):
-    theirs = c_ref[1 - lax.axis_index("c")].astype(jnp.float32)
-    out = (keep_ref[...] + theirs).astype(jnp.bfloat16)
-    own_ref[...] = out[:64]
-    far_ref[...] = out[64:]
+def total_kernel(own_ref, *refs):
+    total = own_ref[...]
+    for ref in refs[:-1]:
+        total = total + ref[...].astype(jnp.float32)
+    refs[-1][...] = total.astype(jnp.bfloat16)
+
+
+def kraw_kernel(tok_ref, par_ref, w_ref, out_ref):
+    at = lax.axis_index("zl") * 128
+    own, far = pl.multiple_of(at, 128), pl.multiple_of(128 - at, 128)
+    both = jnp.concatenate([tok_ref[...], par_ref[...]], axis=0)
+    out = dot(both, w_ref[...], 1, 1).astype(jnp.bfloat16)
+    out_ref[pl.ds(own, 128), :] = out[:128]
+    out_ref[pl.ds(far, 128), :] = out[128:]
 
 
 def grad_kernel(kb_ref, w_ref, add_ref, out_ref):
@@ -74,7 +105,7 @@
 def body(tokens, seg_ids, key_weight, key_grad):
     bf16, f32 = jnp.bfloat16, jnp.float32
     shape = jax.ShapeDtypeStruct
-    zl, core = lax.axis_index("zl"), lax.axis_index("c")
+    zl, t = lax.axis_index("zl"), lax.axis_index("zh") * 2 + lax.axis_index("c")
     spread = whole(spread_kernel, shape((64, 4, 2048), bf16), 1, "spread")(key_weight)
     gathered = lax.all_to_all(spread, ("y", "x"), 0, 0)
     tok_p = lax.ppermute(tokens, "zl", SWAP)
@@ -85,31 +116,30 @@
     kb_p = lax.ppermute(jnp.where(zl == 0, right, left), "zl", SWAP)
     kb = jnp.where(zl == 0, left, right)
 
-    partial = (dot(kb, tokens, 0, 0) + dot(kb_p, tok_p, 0, 0)).astype(bf16).reshape(64, 4, 2048)
+    part = shape((32, 2048), bf16)
+    own, *parts = whole(
+        partial_kernel, (shape((32, 2048), f32),) + (part,) * 7, 4, "partial"
+    )(kb, kb_p, tokens, tok_p)
+    arrived = [
+        lax.ppermute(parts[k - 1], ("y", "x", "c"), ahead(k)) for k in range(1, 8)
+    ]
+    summed = whole(total_kernel, part, 8, "total")(own, *arrived)
 
+    gathered, summed = lax.optimization_barrier((gathered, summed))
     weights = gathered.reshape(256, 2048)
-    keep, to_c = whole(kraw_kernel, (shape((128, 256), f32), shape((128, 256), bf16)), 3, "kraw")(
-        tokens, tok_p, weights
+    ks = whole(kraw_kernel, shape((256, 256), bf16), 3, "kraw")(tokens, tok_p, weights)
+    ks = lax.all_to_all(ks.reshape(16, 16, 256), ("zl", "zh", "c"), 0, 0)
+    g_par = lax.ppermute(dot(kb_p, weights, 1, 0).astype(bf16), "zl", SWAP)
+    ks, summed, g_par = lax.optimization_barrier((ks, summed, g_par))
+    scattered = lax.all_to_all(
+        summed.reshape(8, 4, 2048), ("y", "x", "c"), 0, 0, axis_index_groups=across()
     )
-    to_c, partial = lax.optimization_barrier((to_c, partial))
-    from_c = lax.all_gather(to_c, "c")
-    half = shape((64, 256), bf16)
-    own, to_z = whole(merge_kernel, (half, half), 2, "merge")(keep, from_c)
-    from_z = lax.all_gather(to_z, "zl")
-    scattered = lax.all_to_all(partial, ("y", "x"), 0, 0)
-
-    total_b = jnp.where(
-        zl == 0, jnp.concatenate([own, from_z[1]], 1), jnp.concatenate([from_z[0], own], 1)
-    )
-    total_b, kb_p = lax.optimization_barrier((total_b, kb_p))
-    g_par = lax.ppermute(dot(kb_p, weights, 1, 0).astype(bf16), "zl", SWAP)
-    every = lax.all_gather(total_b, "zh")
-    every, g_par = lax.optimization_barrier((every, g_par))
-    total = jnp.sum(every.astype(f32), axis=0)
-    own_cos = lax.dynamic_slice_in_dim(cosine, core * 64, 64, 0)
-    own_sin = lax.dynamic_slice_in_dim(sine, core * 64, 64, 0)
+    total = jnp.sum(ks.reshape(2, 8, 16, 256).astype(f32), axis=1)
+    total = total.transpose(1, 0, 2).reshape(16, 512)
+    own_cos = lax.dynamic_slice_in_dim(cosine, t * 16, 16, 0)
+    own_sin = lax.dynamic_slice_in_dim(sine, t * 16, 16, 0)
     keys = rotate(total, own_cos, own_sin, 1.0).astype(bf16)
-    keys = lax.all_gather(keys, "c", axis=0, tiled=True)
+    keys = lax.all_gather(lax.all_gather(keys, "c", axis=0, tiled=True), "zh", axis=0, tiled=True)
 
     grad_tokens = whole(grad_kernel, shape((128, 2048), bf16), 3, "grad")(kb, weights, g_par)
     grad_key_weight = jnp.sum(scattered.astype(f32), axis=0)

time: 107 us -> 125 us (1.17)
  the two profiles are of different devices: /device:TPU:1 before, /device:TPU:2 now
where the time goes in v6:
time: 125 us; the launch traced here: 124 us
  starting transfers between devices  79.1 us (63%)
  waiting for transfers between devices  19 us (15%)
  blocking collectives  15.8 us (13%)
  Pallas kernels  4.32 us (3%)
  local copies, waits for them, and re-layouts  3.2 us (3%)
  other arithmetic  1.85 us (1%)
    ppermute x7, starting transfers between devices, body(): lax.ppermute(parts[k - 1], ('y', 'x', 'c'), ahead(k))  30 us
    all_to_all x1, starting transfers between devices, body(): gathered = lax.all_to_all(spread, ('y', 'x'), 0, 0)  17.4 us
    all_to_all x1, starting transfers between devices, body(): ks = lax.all_to_all(ks.reshape(16, 16, 256), ('zl', 'zh', 'c'), 0, 0)  15 us
    all_gather x1, blocking collectives, body(): lax.all_gather(lax.all_gather(keys, 'c', axis=0, tiled=True), 'zh', axis=...  13.9 us
    all_to_all x1, waiting for transfers between devices, body(): ks = lax.all_to_all(ks.reshape(16, 16, 256), ('zl', 'zh', 'c'), 0, 0)  8.89 us
    all_to_all x1, starting transfers between devices, body(): lax.all_to_all(summed.reshape(8, 4, 2048), ('y', 'x', 'c'), 0, 0, axis_in...  7.22 us
    ppermute x1, waiting for transfers between devices, body(): kb_p = lax.ppermute(jnp.where(zl == 0, right, left), 'zl', SWAP)  6.56 us
    ppermute x1, starting transfers between devices, body(): kb_p = lax.ppermute(jnp.where(zl == 0, right, left), 'zl', SWAP)  3.92 us
  transfers between devices with their start and end apart: 13, of which 4 were waited for; matrix products, arithmetic and copies ran while one was open for 1% of the time, Pallas kernels for 3%

profile of v6, /device:TPU:2, one launch (start us, length us, event | category | flops | bytes accessed | tf_op | source)
XLA Modules:
  0.0 124.5 jit_solution(4235517922032226257)
XLA Ops:
  0.6 0.0 copy-start.1
  0.6 0.7 copy-done.1
  1.3 1.1 spread.1
  2.5 0.0 copy-start
  2.5 0.0 copy-start.2
  2.5 17.4 %all-to-all-start = ((bf16[64,4,2048]{2,1,0:T(4,128)(2,1)}), bf16[64,4,2048]{2,1,0:T(4,128)(2,1)S(1)}, u32[]{:S(2)}, u32[]{:S(2)}) async-start(bf16[64,4,2048]{2,1,0:T(4,128)(2,1)} %spread.1), calls=%async_computation | async-start | bytes 2097152 | tf_op jit(solution)/shard_map/all_to_all | solution.py:110
  19.9 0.0 copy-done
  19.9 1.9 %collective-permute-start = (bf16[128,2048]{1,0:T(8,128)(2,1)S(1)}, bf16[128,2048]{1,0:T(8,128)(2,1)S(1)}, u32[]{:S(2)}, u32[]{:S(2)}) collective-permute-start(bf16[128,2048]{1,0:T(8,128)(2,1)S(1)} %copy-done), channel_id=1, source_target_pairs={{0,512},{512,0},{1,513},{513,1},{2,514},{514,2},{3,515},{515,3},{4... | collective-permute-start | bytes 1572872 | tf_op jit(solution)/shard_map/ppermute | solution.py:111
  21.8 0.0 copy-done.2
  21.8 0.1 reshape.98
  21.9 0.0 copy-start.3
  21.9 0.6 copy-done.3
  22.6 0.2 convert_reduce_fusion.2
  22.8 0.3 multiply_sine_fusion
  23.1 0.3 subtract_convert_fusion
  23.4 0.2 pad_maximum_fusion
  23.6 3.9 %collective-permute-start.1 = (bf16[128,256]{1,0:T(8,128)(2,1)S(1)}, bf16[128,256]{1,0:T(8,128)(2,1)S(1)}, u32[]{:S(2)}, u32[]{:S(2)}) collective-permute-start(bf16[128,256]{1,0:T(8,128)(2,1)S(1)} %get-tuple-element.31), channel_id=1, source_target_pairs={{0,512},{512,0},{1,513},{513,1},{2,514},{514,2},{3,515},{515,3},{4... | collective-permute-start | bytes 196616 | tf_op jit(solution)/shard_map/ppermute | solution.py:116
  27.6 6.6 %collective-permute-done.1.kbp_ref = bf16[128,256]{1,0:T(8,128)(2,1)S(1)} collective-permute-done((bf16[128,256]{1,0:T(8,128)(2,1)S(1)}, bf16[128,256]{1,0:T(8,128)(2,1)S(1)}, u32[]{:S(2)}, u32[]{:S(2)}) %collective-permute-start.1) | collective-permute-done | bytes 65568 | tf_op jit(solution)/shard_map/ppermute | solution.py:116
  34.1 0.0 collective-permute-done.par_ref
  34.1 0.8 partial.1
  35.0 3.4 %collective-permute-start.2 = (bf16[32,2048]{1,0:T(8,128)(2,1)S(1)}, bf16[32,2048]{1,0:T(8,128)(2,1)S(1)}, u32[]{:S(2)}, u32[]{:S(2)}) collective-permute-start(bf16[32,2048]{1,0:T(8,128)(2,1)S(1)} %get-tuple-element.17), channel_id=1, source_target_pairs={{0,64},{1,9},{8,72},{9,17},{16,80},{17,25},{24,88},{25,33},{32,96}... | collective-permute-start | bytes 393224 | tf_op jit(solution)/shard_map/ppermute | solution.py:124
  38.4 4.3 %collective-permute-start.3 = (bf16[32,2048]{1,0:T(8,128)(2,1)S(1)}, bf16[32,2048]{1,0:T(8,128)(2,1)S(1)}, u32[]{:S(2)}, u32[]{:S(2)}) collective-permute-start(bf16[32,2048]{1,0:T(8,128)(2,1)S(1)} %get-tuple-element.18), channel_id=1, source_target_pairs={{0,128},{1,17},{8,136},{9,25},{16,144},{17,33},{24,152},{25,41},{3... | collective-permute-start | bytes 393224 | tf_op jit(solution)/shard_map/ppermute | solution.py:124
  42.7 4.7 %collective-permute-start.4 = (bf16[32,2048]{1,0:T(8,128)(2,1)S(1)}, bf16[32,2048]{1,0:T(8,128)(2,1)S(1)}, u32[]{:S(2)}, u32[]{:S(2)}) collective-permute-start(bf16[32,2048]{1,0:T(8,128)(2,1)S(1)} %get-tuple-element.19), channel_id=1, source_target_pairs={{0,192},{1,25},{8,200},{9,33},{16,208},{17,41},{24,216},{25,49},{3... | collective-permute-start | bytes 393224 | tf_op jit(solution)/shard_map/ppermute | solution.py:124
  47.4 4.1 %collective-permute-start.5 = (bf16[32,2048]{1,0:T(8,128)(2,1)S(1)}, bf16[32,2048]{1,0:T(8,128)(2,1)S(1)}, u32[]{:S(2)}, u32[]{:S(2)}) collective-permute-start(bf16[32,2048]{1,0:T(8,128)(2,1)S(1)} %get-tuple-element.20), channel_id=1, source_target_pairs={{0,256},{1,33},{8,264},{9,41},{16,272},{17,49},{24,280},{25,57},{3... | collective-permute-start | bytes 393224 | tf_op jit(solution)/shard_map/ppermute | solution.py:124
  51.5 4.8 %collective-permute-start.6 = (bf16[32,2048]{1,0:T(8,128)(2,1)S(1)}, bf16[32,2048]{1,0:T(8,128)(2,1)S(1)}, u32[]{:S(2)}, u32[]{:S(2)}) collective-permute-start(bf16[32,2048]{1,0:T(8,128)(2,1)S(1)} %get-tuple-element.21), channel_id=1, source_target_pairs={{0,320},{1,41},{8,328},{9,49},{16,336},{17,57},{24,344},{25,1},{32... | collective-permute-start | bytes 393224 | tf_op jit(solution)/shard_map/ppermute | solution.py:124
  56.4 0.0 collective-permute-done.2.refs_0_
  56.4 5.4 %collective-permute-start.7 = (bf16[32,2048]{1,0:T(8,128)(2,1)S(1)}, bf16[32,2048]{1,0:T(8,128)(2,1)S(1)}, u32[]{:S(2)}, u32[]{:S(2)}) collective-permute-start(bf16[32,2048]{1,0:T(8,128)(2,1)S(1)} %get-tuple-element.22), channel_id=1, source_target_pairs={{0,384},{1,49},{8,392},{9,57},{16,400},{17,1},{24,408},{25,9},{32,... | collective-permute-start | bytes 393224 | tf_op jit(solution)/shard_map/ppermute | solution.py:124
  61.8 0.0 collective-permute-done.3.refs_1_
  61.8 3.3 %collective-permute-start.8 = (bf16[32,2048]{1,0:T(8,128)(2,1)S(1)}, bf16[32,2048]{1,0:T(8,128)(2,1)S(1)}, u32[]{:S(2)}, u32[]{:S(2)}) collective-permute-start(bf16[32,2048]{1,0:T(8,128)(2,1)S(1)} %get-tuple-element.23), channel_id=1, source_target_pairs={{0,448},{1,57},{8,456},{9,1},{16,464},{17,9},{24,472},{25,17},{32,... | collective-permute-start | bytes 393224 | tf_op jit(solution)/shard_map/ppermute | solution.py:124
  65.1 0.0 collective-permute-done.4.refs_2_
  65.1 0.0 collective-permute-done.5.refs_3_
  65.1 0.0 collective-permute-done.6.refs_4_
  65.1 1.5 %collective-permute-done.7.refs_5_ = bf16[32,2048]{1,0:T(8,128)(2,1)S(1)} collective-permute-done((bf16[32,2048]{1,0:T(8,128)(2,1)S(1)}, bf16[32,2048]{1,0:T(8,128)(2,1)S(1)}, u32[]{:S(2)}, u32[]{:S(2)}) %collective-permute-start.7) | collective-permute-done | bytes 131104 | tf_op jit(solution)/shard_map/ppermute | solution.py:124
  66.6 2.0 %collective-permute-done.8.refs_6_ = bf16[32,2048]{1,0:T(8,128)(2,1)S(1)} collective-permute-done((bf16[32,2048]{1,0:T(8,128)(2,1)S(1)}, bf16[32,2048]{1,0:T(8,128)(2,1)S(1)}, u32[]{:S(2)}, u32[]{:S(2)}) %collective-permute-start.8) | collective-permute-done | bytes 131104 | tf_op jit(solution)/shard_map/ppermute | solution.py:124
  68.6 0.1 total.1
  68.8 0.0 all-to-all-done
  68.8 0.3 reshape.94.w_ref
  69.1 0.3 convolution_convert_fusion
  69.4 3.6 %collective-permute-start.9 = (bf16[128,2048]{1,0:T(8,128)(2,1)S(1)}, bf16[128,2048]{1,0:T(8,128)(2,1)S(1)}, u32[]{:S(2)}, u32[]{:S(2)}) collective-permute-start(bf16[128,2048]{1,0:T(8,128)(2,1)S(1)} %convolution_convert_fusion), channel_id=1, source_target_pairs={{0,512},{512,0},{1,513},{513,1},{2,514},{514,2},{3,515},{515,3},{4... | collective-permute-start | bytes 1572872 | tf_op jit(solution)/shard_map/ppermute | solution.py:132
  73.0 1.1 kraw.1
  74.2 15.0 %all-to-all-start.1 = ((bf16[16,16,256]{2,1,0:T(8,128)(2,1)}), bf16[16,16,256]{2,1,0:T(8,128)(2,1)S(1)}, u32[]{:S(2)}, u32[]{:S(2)}) async-start(bf16[16,16,256]{2,1,0:T(8,128)(2,1)} %bitcast.1), calls=%async_computation.1 | async-start | bytes 262144 | tf_op jit(solution)/shard_map/all_to_all | solution.py:131
  89.2 8.9 %all-to-all-done.1 = bf16[16,16,256]{2,1,0:T(8,128)(2,1)S(1)} async-done(((bf16[16,16,256]{2,1,0:T(8,128)(2,1)}), bf16[16,16,256]{2,1,0:T(8,128)(2,1)S(1)}, u32[]{:S(2)}, u32[]{:S(2)}) %all-to-all-start.1) | async-done | bytes 131104 | tf_op jit(solution)/shard_map/all_to_all | solution.py:131
  98.0 0.0 collective-permute-done.9.add_ref
  98.2 0.7 reshape.96
  98.9 7.2 %all-to-all-start.2 = ((bf16[8,4,2048]{2,1,0:T(4,128)(2,1)}), bf16[8,4,2048]{2,1,0:T(4,128)(2,1)S(1)}, u32[]{:S(2)}, u32[]{:S(2)}) async-start(bf16[8,4,2048]{2,1,0:T(4,128)(2,1)} %reshape.96), calls=%async_computation.2 | async-start | bytes 262144 | tf_op jit(solution)/shard_map/all_to_all | solution.py:134
  106.1 0.1 subtract_convert_fusion.1
  106.2 1.1 grad.1
  107.3 0.1 pad_maximum_fusion.1
  107.4 1.8 %all_gather.6 = bf16[32,512]{1,0:T(8,128)(2,1)S(1)} all-gather(bf16[16,512]{1,0:T(8,128)(2,1)S(1)} %bitcast.20), channel_id=1, replica_groups=mesh['zl'=2,'y'=8,'x'=8,'zh'=4,'c'=2] {'c'}, dimensions={0}, use_global_device_ids=true | all-gather | bytes 49152 | tf_op jit(solution)/shard_map/all_gather | solution.py:142
  109.2 13.9 %all_gather.7 = bf16[128,512]{1,0:T(8,128)(2,1)S(1)} all-gather(bf16[32,512]{1,0:T(8,128)(2,1)S(1)} %all_gather.6), channel_id=1, replica_groups=mesh['zl'=2,'y'=8,'x'=8,'zh'=4,'c'=2] {'zh'}, dimensions={0}, use_global_device_ids=true | all-gather | bytes 163840 | tf_op jit(solution)/shard_map/all_gather | solution.py:142
  123.2 0.0 all-to-all-done.2
  123.2 0.7 convert_reduce_fusion.1
  123.8 0.7 copy.16
  (9 shorter events, 0.1 us)
Async XLA Ops:
  0.6 0.7 copy-start.1
  2.5 17.4 %copy-start = (bf16[128,2048]{1,0:T(8,128)(2,1)S(1)}, bf16[128,2048]{1,0:T(8,128)(2,1)}, u32[]{:S(2)}) copy-start(bf16[128,2048]{1,0:T(8,128)(2,1)} %tok_ref.3) | copy-start | bytes 1572868
  2.5 19.4 %copy-start.2 = (bf16[128,512]{1,0:T(8,128)(2,1)S(1)}, bf16[128,512]{1,0:T(8,128)(2,1)}, u32[]{:S(2)}) copy-start(bf16[128,512]{1,0:T(8,128)(2,1)} %param.7) | copy-start | bytes 393220
  2.5 66.3 %all-to-all-start = ((bf16[64,4,2048]{2,1,0:T(4,128)(2,1)}), bf16[64,4,2048]{2,1,0:T(4,128)(2,1)S(1)}, u32[]{:S(2)}, u32[]{:S(2)}) async-start(bf16[64,4,2048]{2,1,0:T(4,128)(2,1)} %spread.1), calls=%async_computation | async-start | bytes 2097152 | tf_op jit(solution)/shard_map/all_to_all | solution.py:110
  19.9 14.2 %collective-permute-start = (bf16[128,2048]{1,0:T(8,128)(2,1)S(1)}, bf16[128,2048]{1,0:T(8,128)(2,1)S(1)}, u32[]{:S(2)}, u32[]{:S(2)}) collective-permute-start(bf16[128,2048]{1,0:T(8,128)(2,1)S(1)} %copy-done), channel_id=1, source_target_pairs={{0,512},{512,0},{1,513},{513,1},{2,514},{514,2},{3,515},{515,3},{4... | collective-permute-start | bytes 1572872 | tf_op jit(solution)/shard_map/ppermute | solution.py:111
  21.9 0.7 copy-start.3
  23.6 10.5 %collective-permute-start.1 = (bf16[128,256]{1,0:T(8,128)(2,1)S(1)}, bf16[128,256]{1,0:T(8,128)(2,1)S(1)}, u32[]{:S(2)}, u32[]{:S(2)}) collective-permute-start(bf16[128,256]{1,0:T(8,128)(2,1)S(1)} %get-tuple-element.31), channel_id=1, source_target_pairs={{0,512},{512,0},{1,513},{513,1},{2,514},{514,2},{3,515},{515,3},{4... | collective-permute-start | bytes 196616 | tf_op jit(solution)/shard_map/ppermute | solution.py:116
  35.0 21.4 %collective-permute-start.2 = (bf16[32,2048]{1,0:T(8,128)(2,1)S(1)}, bf16[32,2048]{1,0:T(8,128)(2,1)S(1)}, u32[]{:S(2)}, u32[]{:S(2)}) collective-permute-start(bf16[32,2048]{1,0:T(8,128)(2,1)S(1)} %get-tuple-element.17), channel_id=1, source_target_pairs={{0,64},{1,9},{8,72},{9,17},{16,80},{17,25},{24,88},{25,33},{32,96}... | collective-permute-start | bytes 393224 | tf_op jit(solution)/shard_map/ppermute | solution.py:124
  38.4 23.4 %collective-permute-start.3 = (bf16[32,2048]{1,0:T(8,128)(2,1)S(1)}, bf16[32,2048]{1,0:T(8,128)(2,1)S(1)}, u32[]{:S(2)}, u32[]{:S(2)}) collective-permute-start(bf16[32,2048]{1,0:T(8,128)(2,1)S(1)} %get-tuple-element.18), channel_id=1, source_target_pairs={{0,128},{1,17},{8,136},{9,25},{16,144},{17,33},{24,152},{25,41},{3... | collective-permute-start | bytes 393224 | tf_op jit(solution)/shard_map/ppermute | solution.py:124
  42.7 22.4 %collective-permute-start.4 = (bf16[32,2048]{1,0:T(8,128)(2,1)S(1)}, bf16[32,2048]{1,0:T(8,128)(2,1)S(1)}, u32[]{:S(2)}, u32[]{:S(2)}) collective-permute-start(bf16[32,2048]{1,0:T(8,128)(2,1)S(1)} %get-tuple-element.19), channel_id=1, source_target_pairs={{0,192},{1,25},{8,200},{9,33},{16,208},{17,41},{24,216},{25,49},{3... | collective-permute-start | bytes 393224 | tf_op jit(solution)/shard_map/ppermute | solution.py:124
  47.4 17.7 %collective-permute-start.5 = (bf16[32,2048]{1,0:T(8,128)(2,1)S(1)}, bf16[32,2048]{1,0:T(8,128)(2,1)S(1)}, u32[]{:S(2)}, u32[]{:S(2)}) collective-permute-start(bf16[32,2048]{1,0:T(8,128)(2,1)S(1)} %get-tuple-element.20), channel_id=1, source_target_pairs={{0,256},{1,33},{8,264},{9,41},{16,272},{17,49},{24,280},{25,57},{3... | collective-permute-start | bytes 393224 | tf_op jit(solution)/shard_map/ppermute | solution.py:124
  51.5 13.6 %collective-permute-start.6 = (bf16[32,2048]{1,0:T(8,128)(2,1)S(1)}, bf16[32,2048]{1,0:T(8,128)(2,1)S(1)}, u32[]{:S(2)}, u32[]{:S(2)}) collective-permute-start(bf16[32,2048]{1,0:T(8,128)(2,1)S(1)} %get-tuple-element.21), channel_id=1, source_target_pairs={{0,320},{1,41},{8,328},{9,49},{16,336},{17,57},{24,344},{25,1},{32... | collective-permute-start | bytes 393224 | tf_op jit(solution)/shard_map/ppermute | solution.py:124
  56.4 10.2 %collective-permute-start.7 = (bf16[32,2048]{1,0:T(8,128)(2,1)S(1)}, bf16[32,2048]{1,0:T(8,128)(2,1)S(1)}, u32[]{:S(2)}, u32[]{:S(2)}) collective-permute-start(bf16[32,2048]{1,0:T(8,128)(2,1)S(1)} %get-tuple-element.22), channel_id=1, source_target_pairs={{0,384},{1,49},{8,392},{9,57},{16,400},{17,1},{24,408},{25,9},{32,... | collective-permute-start | bytes 393224 | tf_op jit(solution)/shard_map/ppermute | solution.py:124
  61.8 6.9 %collective-permute-start.8 = (bf16[32,2048]{1,0:T(8,128)(2,1)S(1)}, bf16[32,2048]{1,0:T(8,128)(2,1)S(1)}, u32[]{:S(2)}, u32[]{:S(2)}) collective-permute-start(bf16[32,2048]{1,0:T(8,128)(2,1)S(1)} %get-tuple-element.23), channel_id=1, source_target_pairs={{0,448},{1,57},{8,456},{9,1},{16,464},{17,9},{24,472},{25,17},{32,... | collective-permute-start | bytes 393224 | tf_op jit(solution)/shard_map/ppermute | solution.py:124
  69.4 28.7 %collective-permute-start.9 = (bf16[128,2048]{1,0:T(8,128)(2,1)S(1)}, bf16[128,2048]{1,0:T(8,128)(2,1)S(1)}, u32[]{:S(2)}, u32[]{:S(2)}) collective-permute-start(bf16[128,2048]{1,0:T(8,128)(2,1)S(1)} %convolution_convert_fusion), channel_id=1, source_target_pairs={{0,512},{512,0},{1,513},{513,1},{2,514},{514,2},{3,515},{515,3},{4... | collective-permute-start | bytes 1572872 | tf_op jit(solution)/shard_map/ppermute | solution.py:132
  74.2 23.9 %all-to-all-start.1 = ((bf16[16,16,256]{2,1,0:T(8,128)(2,1)}), bf16[16,16,256]{2,1,0:T(8,128)(2,1)S(1)}, u32[]{:S(2)}, u32[]{:S(2)}) async-start(bf16[16,16,256]{2,1,0:T(8,128)(2,1)} %bitcast.1), calls=%async_computation.1 | async-start | bytes 262144 | tf_op jit(solution)/shard_map/all_to_all | solution.py:131
  98.9 24.3 %all-to-all-start.2 = ((bf16[8,4,2048]{2,1,0:T(4,128)(2,1)}), bf16[8,4,2048]{2,1,0:T(4,128)(2,1)S(1)}, u32[]{:S(2)}, u32[]{:S(2)}) async-start(bf16[8,4,2048]{2,1,0:T(4,128)(2,1)} %reshape.96), calls=%async_computation.2 | async-start | bytes 262144 | tf_op jit(solution)/shard_map/all_to_all | solution.py:134

commit v7 on v5

--- a/solution.py
+++ b/solution.py
@@ -38,13 +38,14 @@
     out_ref[...] = jnp.broadcast_to(w_ref[...][None], out_ref.shape)
 
 
-def kraw_kernel(tok_ref, par_ref, w_ref, keep_ref, send_ref):
+def kraw_kernel(tok_ref, par_ref, kb_ref, w_ref, keep_ref, send_ref, grad_ref):
     mine = pl.multiple_of(lax.axis_index("c") * 64, 64)
     other = pl.multiple_of(64 - mine, 64)
     halves = [ref[pl.ds(at, 64), :] for at in (mine, other) for ref in (tok_ref, par_ref)]
     out = dot(jnp.concatenate(halves, axis=0), w_ref[...], 1, 1)
     keep_ref[...] = out[:128]
     send_ref[...] = out[128:].astype(jnp.bfloat16)
+    grad_ref[...] = dot(kb_ref[...], w_ref[...], 1, 0).astype(jnp.bfloat16)
 
 
 def merge_kernel(keep_ref, c_ref, own_ref, far_ref):
@@ -88,9 +89,13 @@
     partial = (dot(kb, tokens, 0, 0) + dot(kb_p, tok_p, 0, 0)).astype(bf16).reshape(64, 4, 2048)
 
     weights = gathered.reshape(256, 2048)
-    keep, to_c = whole(kraw_kernel, (shape((128, 256), f32), shape((128, 256), bf16)), 3, "kraw")(
-        tokens, tok_p, weights
-    )
+    keep, to_c, g_send = whole(
+        kraw_kernel,
+        (shape((128, 256), f32), shape((128, 256), bf16), shape((128, 2048), bf16)),
+        4,
+        "kraw",
+    )(tokens, tok_p, kb_p, weights)
+    g_par = lax.ppermute(g_send, "zl", SWAP)
     to_c, partial = lax.optimization_barrier((to_c, partial))
     from_c = lax.all_gather(to_c, "c")
     half = shape((64, 256), bf16)
@@ -101,18 +106,19 @@
     total_b = jnp.where(
         zl == 0, jnp.concatenate([own, from_z[1]], 1), jnp.concatenate([from_z[0], own], 1)
     )
-    total_b, kb_p = lax.optimization_barrier((total_b, kb_p))
-    g_par = lax.ppermute(dot(kb_p, weights, 1, 0).astype(bf16), "zl", SWAP)
-    every = lax.all_gather(total_b, "zh")
-    every, g_par = lax.optimization_barrier((every, g_par))
-    total = jnp.sum(every.astype(f32), axis=0)
+    one, three, two = (
+        lax.ppermute(total_b, "zh", [(i, (i + step) % 4) for i in range(4)])
+        for step in (1, 3, 2)
+    )
+    total = (total_b.astype(f32) + two.astype(f32)) + (one.astype(f32) + three.astype(f32))
     own_cos = lax.dynamic_slice_in_dim(cosine, core * 64, 64, 0)
     own_sin = lax.dynamic_slice_in_dim(sine, core * 64, 64, 0)
     keys = rotate(total, own_cos, own_sin, 1.0).astype(bf16)
     keys = lax.all_gather(keys, "c", axis=0, tiled=True)
 
+    grad_key_weight = jnp.sum(scattered.astype(f32), axis=0)
+    grad_key_weight, g_par = lax.optimization_barrier((grad_key_weight, g_par))
     grad_tokens = whole(grad_kernel, shape((128, 2048), bf16), 3, "grad")(kb, weights, g_par)
-    grad_key_weight = jnp.sum(scattered.astype(f32), axis=0)
     return keys, grad_tokens, grad_key_weight
 
 

time: 107 us -> 103 us (0.963)
  blocking collectives: 47.9 us -> 15.9 us
  starting transfers between devices: 34.1 us -> 55.5 us
  waiting for transfers between devices: 12.7 us -> 18.5 us
  matrix products: 2.01 us -> 0.9 us
    all_gather x1 -> x0, blocking collectives: 31.7 us -> none  [body(): every = lax.all_gather(total_b, 'zh')]
    ppermute x1 -> x4, starting transfers between devices: 3.38 us -> 24.5 us  [the longest x3 21.1 us: body(): lax.ppermute(total_b, 'zh', [(i, (i + step) % 4) for i in range(4)])]
    ppermute x1 -> x4, waiting for transfers between devices: 0.01 us -> 5.54 us  [the longest x1 5 us: body(): g_par = lax.ppermute(g_send, 'zl', SWAP)]
    reduce_sum x1, other arithmetic: 1.06 us -> 2.29 us  [body(): grad_key_weight = jnp.sum(scattered.astype(f32), axis=0)]
    dot_general x3 -> x2, matrix products: 2.01 us -> 0.9 us  [dot(): lax.dot_general(a, b, (((da,), (db,)), ((), ())), preferred_element_type=...]
    reshape x1, local copies, waits for them, and re-layouts: 0.26 us -> 1.33 us  [body(): weights = gathered.reshape(256, 2048)]
  transfers between devices with their start and end apart: 5 -> 8, of which waited for: 2 -> 4; matrix products, arithmetic and copies ran while one was open for 5% -> 6% of each run, Pallas kernels for 1% -> 0%
where the time goes in v7:
time: 103 us; the launch traced here: 102 us
  starting transfers between devices  55.5 us (54%)
  waiting for transfers between devices  18.5 us (18%)
  blocking collectives  15.9 us (15%)
  local copies, waits for them, and re-layouts  4.17 us (4%)
  other arithmetic  3.61 us (4%)
  Pallas kernels  2.83 us (3%)
    ppermute x3, starting transfers between devices, body(): lax.ppermute(total_b, 'zh', [(i, (i + step) % 4) for i in range(4)])  21.1 us
    all_to_all x1, starting transfers between devices, body(): gathered = lax.all_to_all(spread, ('y', 'x'), 0, 0)  14.3 us
    all_to_all x1, starting transfers between devices, body(): scattered = lax.all_to_all(partial, ('y', 'x'), 0, 0)  9.83 us
    ppermute x1, waiting for transfers between devices, body(): kb_p = lax.ppermute(jnp.where(zl == 0, right, left), 'zl', SWAP)  6.94 us
    all_to_all x1, waiting for transfers between devices, body(): gathered = lax.all_to_all(spread, ('y', 'x'), 0, 0)  5.97 us
    all_gather x1, blocking collectives, body(): from_c = lax.all_gather(to_c, 'c')  5.87 us
    all_gather x1, blocking collectives, body(): from_z = lax.all_gather(to_z, 'zl')  5.4 us
    ppermute x1, waiting for transfers between devices, body(): g_par = lax.ppermute(g_send, 'zl', SWAP)  5 us
  transfers between devices with their start and end apart: 8, of which 4 were waited for; matrix products, arithmetic and copies ran while one was open for 6% of the time, Pallas kernels for 0%

profile of v7, /device:TPU:1, one launch (start us, length us, event | category | flops | bytes accessed | tf_op | source)
XLA Modules:
  0.0 102.3 jit_solution(5829573676703949010)
XLA Ops:
  0.6 0.0 copy-start
  0.6 0.0 copy-start.1
  0.7 0.8 copy-done.1
  1.4 0.0 copy-start.2
  1.4 0.0 copy-start.3
  1.4 1.1 %spread.1 = bf16[64,4,2048]{2,1,0:T(4,128)(2,1)} custom-call(bf16[4,2048]{1,0:T(4,128)(2,1)S(1)} %copy-done.1), custom_call_target="tpu_custom_call" | custom-call | tf_op jit(solution)/shard_map/spread/pallas_call | solution.py:79
  2.5 14.3 %all-to-all-start = ((bf16[64,4,2048]{2,1,0:T(4,128)(2,1)}), bf16[64,4,2048]{2,1,0:T(4,128)(2,1)}, u32[]{:S(2)}, u32[]{:S(2)}) async-start(bf16[64,4,2048]{2,1,0:T(4,128)(2,1)} %spread.1), calls=%async_computation | async-start | bytes 2097152 | tf_op jit(solution)/shard_map/all_to_all | solution.py:80
  16.8 0.0 copy-done
  16.8 4.9 %collective-permute-start = (bf16[128,2048]{1,0:T(8,128)(2,1)S(1)}, bf16[128,2048]{1,0:T(8,128)(2,1)S(1)}, u32[]{:S(2)}, u32[]{:S(2)}) collective-permute-start(bf16[128,2048]{1,0:T(8,128)(2,1)S(1)} %copy-done), channel_id=1, source_target_pairs={{0,512},{512,0},{1,513},{513,1},{2,514},{514,2},{3,515},{515,3},{4... | collective-permute-start | bytes 1572872 | tf_op jit(solution)/shard_map/ppermute | solution.py:81
  21.7 0.0 copy-done.2
  21.8 0.1 reshape.95
  21.9 0.0 copy-done.3
  21.9 0.2 convert_reduce_fusion.1
  22.1 0.3 multiply_sine_fusion
  22.4 0.3 subtract_convert_fusion
  22.7 0.2 pad_maximum_fusion
  22.9 1.9 %collective-permute-start.1 = (bf16[128,256]{1,0:T(8,128)(2,1)S(1)}, bf16[128,256]{1,0:T(8,128)(2,1)S(1)}, u32[]{:S(2)}, u32[]{:S(2)}) collective-permute-start(bf16[128,256]{1,0:T(8,128)(2,1)S(1)} %get-tuple-element.26), channel_id=1, source_target_pairs={{0,512},{512,0},{1,513},{513,1},{2,514},{514,2},{3,515},{515,3},{4... | collective-permute-start | bytes 196616 | tf_op jit(solution)/shard_map/ppermute | solution.py:86
  24.9 0.5 fusion.2
  25.3 6.9 %collective-permute-done.1.kb_ref = bf16[128,256]{1,0:T(8,128)(2,1)S(1)} collective-permute-done((bf16[128,256]{1,0:T(8,128)(2,1)S(1)}, bf16[128,256]{1,0:T(8,128)(2,1)S(1)}, u32[]{:S(2)}, u32[]{:S(2)}) %collective-permute-start.1) | collective-permute-done | bytes 65568 | tf_op jit(solution)/shard_map/ppermute | solution.py:86
  32.2 0.0 collective-permute-done.par_ref
  32.3 0.5 fusion
  32.7 1.2 %reshape.92 = bf16[64,4,2048]{2,1,0:T(4,128)(2,1)} reshape(bf16[256,2048]{1,0:T(8,128)(2,1)S(1)} %fusion) | data formatting | bytes 2097152 | tf_op jit(solution)/shard_map/reshape | solution.py:89
  33.9 6.0 %all-to-all-done = bf16[64,4,2048]{2,1,0:T(4,128)(2,1)} async-done(((bf16[64,4,2048]{2,1,0:T(4,128)(2,1)}), bf16[64,4,2048]{2,1,0:T(4,128)(2,1)}, u32[]{:S(2)}, u32[]{:S(2)}) %all-to-all-start) | async-done | bytes 1048608 | tf_op jit(solution)/shard_map/all_to_all | solution.py:80
  39.9 1.3 %reshape.91.w_ref = bf16[256,2048]{1,0:T(8,128)(2,1)S(1)} reshape(bf16[64,4,2048]{2,1,0:T(4,128)(2,1)} %all-to-all-done) | data formatting | bytes 2097152 | tf_op jit(solution)/shard_map/reshape | solution.py:91
  41.2 0.6 kraw.1
  41.9 9.8 %all-to-all-start.1 = ((bf16[64,4,2048]{2,1,0:T(4,128)(2,1)}), bf16[64,4,2048]{2,1,0:T(4,128)(2,1)}, u32[]{:S(2)}, u32[]{:S(2)}) async-start(bf16[64,4,2048]{2,1,0:T(4,128)(2,1)} %reshape.92), calls=%async_computation.1 | async-start | bytes 2097152 | tf_op jit(solution)/shard_map/all_to_all | solution.py:104
  51.7 5.9 %all-gather = bf16[256,256]{1,0:T(8,128)(2,1)S(1)} all-gather(bf16[128,256]{1,0:T(8,128)(2,1)S(1)} %get-tuple-element.14), channel_id=2, replica_groups=mesh['zl'=2,'y'=8,'x'=8,'zh'=4,'c'=2] {'c'}, dimensions={0}, use_global_device_ids=true | all-gather | bytes 196608 | tf_op jit(solution)/shard_map/all_gather | solution.py:100
  57.6 5.4 %all-gather.1 = bf16[128,256]{1,0:T(8,128)(2,1)S(1)} all-gather(bf16[64,256]{1,0:T(8,128)(2,1)S(1)} %get-tuple-element.16), channel_id=3, replica_groups=mesh['zl'=2,'y'=8,'x'=8,'zh'=4,'c'=2] {'zl'}, dimensions={0}, use_global_device_ids=true | all-gather | bytes 98304 | tf_op jit(solution)/shard_map/all_gather | solution.py:103
  63.0 13.4 %collective-permute-start.2 = (bf16[64,512]{1,0:T(8,128)(2,1)S(1)}, bf16[64,512]{1,0:T(8,128)(2,1)S(1)}, u32[]{:S(2)}, u32[]{:S(2)}) collective-permute-start(bf16[64,512]{1,0:T(8,128)(2,1)S(1)} %maximum_select_fusion), channel_id=1, source_target_pairs={{0,4},{2,6},{4,0},{6,2},{1,5},{3,7},{5,1},{7,3},{8,12},{10,14},{12... | collective-permute-start | bytes 196616 | tf_op jit(solution)/shard_map/ppermute | solution.py:110
  76.4 5.8 %collective-permute-start.3 = (bf16[64,512]{1,0:T(8,128)(2,1)S(1)}, bf16[64,512]{1,0:T(8,128)(2,1)S(1)}, u32[]{:S(2)}, u32[]{:S(2)}) collective-permute-start(bf16[64,512]{1,0:T(8,128)(2,1)S(1)} %maximum_select_fusion), channel_id=1, source_target_pairs={{0,2},{2,4},{4,6},{6,0},{1,3},{3,5},{5,7},{7,1},{8,10},{10,12},{12... | collective-permute-start | bytes 196616 | tf_op jit(solution)/shard_map/ppermute | solution.py:110
  82.2 1.9 %collective-permute-start.4 = (bf16[64,512]{1,0:T(8,128)(2,1)S(1)}, bf16[64,512]{1,0:T(8,128)(2,1)S(1)}, u32[]{:S(2)}, u32[]{:S(2)}) collective-permute-start(bf16[64,512]{1,0:T(8,128)(2,1)S(1)} %maximum_select_fusion), channel_id=1, source_target_pairs={{0,6},{2,0},{4,2},{6,4},{1,7},{3,1},{5,3},{7,5},{8,14},{10,8},{12,... | collective-permute-start | bytes 196616 | tf_op jit(solution)/shard_map/ppermute | solution.py:110
  84.2 3.4 %collective-permute-start.5 = (bf16[128,2048]{1,0:T(8,128)(2,1)S(1)}, bf16[128,2048]{1,0:T(8,128)(2,1)S(1)}, u32[]{:S(2)}, u32[]{:S(2)}) collective-permute-start(bf16[128,2048]{1,0:T(8,128)(2,1)S(1)} %get-tuple-element.18), channel_id=1, source_target_pairs={{0,512},{512,0},{1,513},{513,1},{2,514},{514,2},{3,515},{515,3},{4... | collective-permute-start | bytes 1572872 | tf_op jit(solution)/shard_map/ppermute | solution.py:98
  87.6 0.0 collective-permute-done.2
  87.6 0.0 collective-permute-done.3
  87.6 0.5 collective-permute-done.4
  88.2 0.2 subtract_convert_fusion.1
  88.4 0.1 pad_maximum_fusion.1
  88.6 4.7 %all_gather.19 = bf16[128,512]{1,0:T(8,128)(2,1)S(1)} all-gather(bf16[64,512]{1,0:T(8,128)(2,1)S(1)} %bitcast.18), channel_id=1, replica_groups=mesh['zl'=2,'y'=8,'x'=8,'zh'=4,'c'=2] {'c'}, dimensions={0}, use_global_device_ids=true | all-gather | bytes 196608 | tf_op jit(solution)/shard_map/all_gather | solution.py:117
  93.2 0.0 all-to-all-done.1
  93.2 2.3 %convert_reduce_fusion = f32[4,2048]{1,0:T(4,128)} fusion(bf16[64,4,2048]{2,1,0:T(4,128)(2,1)} %all-to-all-done.1), kind=kLoop, calls=%fused_computation.2 | loop fusion | flops 1040384 | bytes 1081344 | tf_op jit(solution)/shard_map/reduce_sum | solution.py:119
  95.5 5.0 %collective-permute-done.5.add_ref = bf16[128,2048]{1,0:T(8,128)(2,1)S(1)} collective-permute-done((bf16[128,2048]{1,0:T(8,128)(2,1)S(1)}, bf16[128,2048]{1,0:T(8,128)(2,1)S(1)}, u32[]{:S(2)}, u32[]{:S(2)}) %collective-permute-start.5) | collective-permute-done | bytes 524320 | tf_op jit(solution)/shard_map/ppermute | solution.py:98
  100.5 1.1 %grad.1 = bf16[128,2048]{1,0:T(8,128)(2,1)} custom-call(bf16[128,256]{1,0:T(8,128)(2,1)S(1)} %get-tuple-element.25.kb_ref, bf16[256,2048]{1,0:T(8,128)(2,1)S(1)} %reshape.91.w_ref, bf16[128,2048]{1,0:T(8,128)(2,1)S(1)} %collective-permute-done.5.add_ref), custom_call_target="tpu_custom_call" | custom-call | tf_op jit(solution)/shard_map/grad/pallas_call | solution.py:121
  101.6 0.7 copy.14
  (11 shorter events, 0.2 us)
Async XLA Ops:
  0.6 16.2 %copy-start = (bf16[128,2048]{1,0:T(8,128)(2,1)S(1)}, bf16[128,2048]{1,0:T(8,128)(2,1)}, u32[]{:S(2)}) copy-start(bf16[128,2048]{1,0:T(8,128)(2,1)} %tok_ref.1) | copy-start | bytes 1572868
  0.6 0.8 copy-start.1
  1.4 20.3 %copy-start.2 = (bf16[128,512]{1,0:T(8,128)(2,1)S(1)}, bf16[128,512]{1,0:T(8,128)(2,1)}, u32[]{:S(2)}) copy-start(bf16[128,512]{1,0:T(8,128)(2,1)} %param.7) | copy-start | bytes 393220
  1.4 20.4 %copy-start.3 = (s32[1,128]{1,0:T(1,128)S(1)}, s32[1,128]{1,0:T(1,128)}, u32[]{:S(2)}) copy-start(s32[1,128]{1,0:T(1,128)} %param.5) | copy-start | bytes 1540
  2.5 37.4 %all-to-all-start = ((bf16[64,4,2048]{2,1,0:T(4,128)(2,1)}), bf16[64,4,2048]{2,1,0:T(4,128)(2,1)}, u32[]{:S(2)}, u32[]{:S(2)}) async-start(bf16[64,4,2048]{2,1,0:T(4,128)(2,1)} %spread.1), calls=%async_computation | async-start | bytes 2097152 | tf_op jit(solution)/shard_map/all_to_all | solution.py:80
  16.8 15.4 %collective-permute-start = (bf16[128,2048]{1,0:T(8,128)(2,1)S(1)}, bf16[128,2048]{1,0:T(8,128)(2,1)S(1)}, u32[]{:S(2)}, u32[]{:S(2)}) collective-permute-start(bf16[128,2048]{1,0:T(8,128)(2,1)S(1)} %copy-done), channel_id=1, source_target_pairs={{0,512},{512,0},{1,513},{513,1},{2,514},{514,2},{3,515},{515,3},{4... | collective-permute-start | bytes 1572872 | tf_op jit(solution)/shard_map/ppermute | solution.py:81
  22.9 9.3 %collective-permute-start.1 = (bf16[128,256]{1,0:T(8,128)(2,1)S(1)}, bf16[128,256]{1,0:T(8,128)(2,1)S(1)}, u32[]{:S(2)}, u32[]{:S(2)}) collective-permute-start(bf16[128,256]{1,0:T(8,128)(2,1)S(1)} %get-tuple-element.26), channel_id=1, source_target_pairs={{0,512},{512,0},{1,513},{513,1},{2,514},{514,2},{3,515},{515,3},{4... | collective-permute-start | bytes 196616 | tf_op jit(solution)/shard_map/ppermute | solution.py:86
  41.9 51.4 %all-to-all-start.1 = ((bf16[64,4,2048]{2,1,0:T(4,128)(2,1)}), bf16[64,4,2048]{2,1,0:T(4,128)(2,1)}, u32[]{:S(2)}, u32[]{:S(2)}) async-start(bf16[64,4,2048]{2,1,0:T(4,128)(2,1)} %reshape.92), calls=%async_computation.1 | async-start | bytes 2097152 | tf_op jit(solution)/shard_map/all_to_all | solution.py:104
  63.0 24.6 %collective-permute-start.2 = (bf16[64,512]{1,0:T(8,128)(2,1)S(1)}, bf16[64,512]{1,0:T(8,128)(2,1)S(1)}, u32[]{:S(2)}, u32[]{:S(2)}) collective-permute-start(bf16[64,512]{1,0:T(8,128)(2,1)S(1)} %maximum_select_fusion), channel_id=1, source_target_pairs={{0,4},{2,6},{4,0},{6,2},{1,5},{3,7},{5,1},{7,3},{8,12},{10,14},{12... | collective-permute-start | bytes 196616 | tf_op jit(solution)/shard_map/ppermute | solution.py:110
  76.4 11.2 %collective-permute-start.3 = (bf16[64,512]{1,0:T(8,128)(2,1)S(1)}, bf16[64,512]{1,0:T(8,128)(2,1)S(1)}, u32[]{:S(2)}, u32[]{:S(2)}) collective-permute-start(bf16[64,512]{1,0:T(8,128)(2,1)S(1)} %maximum_select_fusion), channel_id=1, source_target_pairs={{0,2},{2,4},{4,6},{6,0},{1,3},{3,5},{5,7},{7,1},{8,10},{10,12},{12... | collective-permute-start | bytes 196616 | tf_op jit(solution)/shard_map/ppermute | solution.py:110
  82.2 5.9 %collective-permute-start.4 = (bf16[64,512]{1,0:T(8,128)(2,1)S(1)}, bf16[64,512]{1,0:T(8,128)(2,1)S(1)}, u32[]{:S(2)}, u32[]{:S(2)}) collective-permute-start(bf16[64,512]{1,0:T(8,128)(2,1)S(1)} %maximum_select_fusion), channel_id=1, source_target_pairs={{0,6},{2,0},{4,2},{6,4},{1,7},{3,1},{5,3},{7,5},{8,14},{10,8},{12,... | collective-permute-start | bytes 196616 | tf_op jit(solution)/shard_map/ppermute | solution.py:110
  84.2 16.3 %collective-permute-start.5 = (bf16[128,2048]{1,0:T(8,128)(2,1)S(1)}, bf16[128,2048]{1,0:T(8,128)(2,1)S(1)}, u32[]{:S(2)}, u32[]{:S(2)}) collective-permute-start(bf16[128,2048]{1,0:T(8,128)(2,1)S(1)} %get-tuple-element.18), channel_id=1, source_target_pairs={{0,512},{512,0},{1,513},{513,1},{2,514},{514,2},{3,515},{515,3},{4... | collective-permute-start | bytes 1572872 | tf_op jit(solution)/shard_map/ppermute | solution.py:98

commit v8 on v7

--- a/solution.py
+++ b/solution.py
@@ -60,6 +60,10 @@
     out_ref[...] = out.astype(jnp.bfloat16)
 
 
+def sum_kernel(in_ref, out_ref):
+    out_ref[...] = jnp.sum(in_ref[...].astype(jnp.float32), axis=0)
+
+
 def whole(kernel, outs, n_in, name):
     vmem = pl.BlockSpec(memory_space=pltpu.VMEM)
     return pl.pallas_call(
@@ -67,7 +71,7 @@
         out_shape=outs,
         in_specs=[vmem] * n_in,
         out_specs=jax.tree.map(lambda _: vmem, outs),
-        compiler_params=pltpu.CompilerParams(vmem_limit_bytes=32 << 20),
+        compiler_params=pltpu.CompilerParams(vmem_limit_bytes=12 << 20),
         name=name,
     )
 
@@ -96,7 +100,6 @@
         "kraw",
     )(tokens, tok_p, kb_p, weights)
     g_par = lax.ppermute(g_send, "zl", SWAP)
-    to_c, partial = lax.optimization_barrier((to_c, partial))
     from_c = lax.all_gather(to_c, "c")
     half = shape((64, 256), bf16)
     own, to_z = whole(merge_kernel, (half, half), 2, "merge")(keep, from_c)
@@ -116,7 +119,7 @@
     keys = rotate(total, own_cos, own_sin, 1.0).astype(bf16)
     keys = lax.all_gather(keys, "c", axis=0, tiled=True)
 
-    grad_key_weight = jnp.sum(scattered.astype(f32), axis=0)
+    grad_key_weight = whole(sum_kernel, shape((4, 2048), f32), 1, "sum")(scattered)
     grad_key_weight, g_par = lax.optimization_barrier((grad_key_weight, g_par))
     grad_tokens = whole(grad_kernel, shape((128, 2048), bf16), 3, "grad")(kb, weights, g_par)
     return keys, grad_tokens, grad_key_weight

time: 103 us -> 104 us (level)
  waiting for transfers between devices: 18.5 us -> 21.6 us
  other arithmetic: 3.61 us -> 1.32 us
  Pallas kernels: 2.83 us -> 4.71 us
  blocking collectives: 15.9 us -> 14.6 us
    reduce_sum x1 -> x0, other arithmetic: 2.29 us -> none  [body(): grad_key_weight = jnp.sum(scattered.astype(f32), axis=0)]
    ppermute x1, waiting for transfers between devices: 5 us -> 6.68 us  [body(): g_par = lax.ppermute(g_send, 'zl', SWAP)]
    pallas_call x0 -> x1, Pallas kernels: none -> 1.06 us  [body(): whole(sum_kernel, shape((4, 2048), f32), 1, 'sum')(scattered)]
  transfers between devices with their start and end apart: 8 -> 8, of which waited for: 4 -> 4; matrix products, arithmetic and copies ran while one was open for 6% -> 5% of each run, Pallas kernels for 0% -> 2%
where the time goes in v8:
time: 104 us; the launch traced here: 103 us
  starting transfers between devices  55.1 us (53%)
  waiting for transfers between devices  21.6 us (21%)
  blocking collectives  14.6 us (14%)
  Pallas kernels  4.71 us (5%)
  local copies, waits for them, and re-layouts  4.18 us (4%)
  other arithmetic  1.32 us (1%)
    ppermute x3, starting transfers between devices, body(): lax.ppermute(total_b, 'zh', [(i, (i + step) % 4) for i in range(4)])  21.1 us
    all_to_all x1, starting transfers between devices, body(): gathered = lax.all_to_all(spread, ('y', 'x'), 0, 0)  14 us
    all_to_all x1, starting transfers between devices, body(): scattered = lax.all_to_all(partial, ('y', 'x'), 0, 0)  9.71 us
    ppermute x1, waiting for transfers between devices, body(): kb_p = lax.ppermute(jnp.where(zl == 0, right, left), 'zl', SWAP)  7.54 us
    ppermute x1, waiting for transfers between devices, body(): g_par = lax.ppermute(g_send, 'zl', SWAP)  6.68 us
    all_to_all x1, waiting for transfers between devices, body(): gathered = lax.all_to_all(spread, ('y', 'x'), 0, 0)  5.81 us
    all_gather x1, blocking collectives, body(): from_c = lax.all_gather(to_c, 'c')  5.41 us
    all_gather x1, blocking collectives, body(): from_z = lax.all_gather(to_z, 'zl')  5.29 us
  transfers between devices with their start and end apart: 8, of which 4 were waited for; matrix products, arithmetic and copies ran while one was open for 5% of the time, Pallas kernels for 2%

profile of v8, /device:TPU:1, one launch (start us, length us, event | category | flops | bytes accessed | tf_op | source)
XLA Modules:
  0.0 103.3 jit_solution(506345318773313605)
XLA Ops:
  0.6 0.0 copy-start
  0.6 0.0 copy-start.1
  0.7 0.8 copy-done.1
  1.4 0.0 copy-start.3
  1.4 0.0 copy-start.4
  1.4 1.1 %spread.1 = bf16[64,4,2048]{2,1,0:T(4,128)(2,1)} custom-call(bf16[4,2048]{1,0:T(4,128)(2,1)S(1)} %copy-done.1), custom_call_target="tpu_custom_call" | custom-call | tf_op jit(solution)/shard_map/spread/pallas_call | solution.py:83
  2.5 14.0 %all-to-all-start = ((bf16[64,4,2048]{2,1,0:T(4,128)(2,1)}), bf16[64,4,2048]{2,1,0:T(4,128)(2,1)S(1)}, u32[]{:S(2)}, u32[]{:S(2)}) async-start(bf16[64,4,2048]{2,1,0:T(4,128)(2,1)} %spread.1), calls=%async_computation | async-start | bytes 2097152 | tf_op jit(solution)/shard_map/all_to_all | solution.py:84
  16.6 0.0 copy-done
  16.6 4.9 %collective-permute-start = (bf16[128,2048]{1,0:T(8,128)(2,1)S(1)}, bf16[128,2048]{1,0:T(8,128)(2,1)S(1)}, u32[]{:S(2)}, u32[]{:S(2)}) collective-permute-start(bf16[128,2048]{1,0:T(8,128)(2,1)S(1)} %copy-done), channel_id=1, source_target_pairs={{0,512},{512,0},{1,513},{513,1},{2,514},{514,2},{3,515},{515,3},{4... | collective-permute-start | bytes 1572872 | tf_op jit(solution)/shard_map/ppermute | solution.py:85
  21.5 0.0 copy-done.3
  21.5 0.1 reshape.95
  21.6 0.0 copy-done.4
  21.6 0.2 convert_reduce_fusion
  21.8 0.3 multiply_sine_fusion
  22.1 0.3 subtract_convert_fusion
  22.4 0.2 pad_maximum_fusion
  22.7 1.9 %collective-permute-start.1 = (bf16[128,256]{1,0:T(8,128)(2,1)S(1)}, bf16[128,256]{1,0:T(8,128)(2,1)S(1)}, u32[]{:S(2)}, u32[]{:S(2)}) collective-permute-start(bf16[128,256]{1,0:T(8,128)(2,1)S(1)} %get-tuple-element.22), channel_id=1, source_target_pairs={{0,512},{512,0},{1,513},{513,1},{2,514},{514,2},{3,515},{515,3},{4... | collective-permute-start | bytes 196616 | tf_op jit(solution)/shard_map/ppermute | solution.py:90
  24.6 0.5 fusion.2
  25.1 7.5 %collective-permute-done.1.kb_ref = bf16[128,256]{1,0:T(8,128)(2,1)S(1)} collective-permute-done((bf16[128,256]{1,0:T(8,128)(2,1)S(1)}, bf16[128,256]{1,0:T(8,128)(2,1)S(1)}, u32[]{:S(2)}, u32[]{:S(2)}) %collective-permute-start.1) | collective-permute-done | bytes 65568 | tf_op jit(solution)/shard_map/ppermute | solution.py:90
  32.6 0.0 collective-permute-done.par_ref
  32.6 0.5 fusion
  33.1 1.2 %reshape.93 = bf16[64,4,2048]{2,1,0:T(4,128)(2,1)} reshape(bf16[256,2048]{1,0:T(8,128)(2,1)S(1)} %fusion) | data formatting | bytes 2097152 | tf_op jit(solution)/shard_map/reshape | solution.py:93
  34.3 5.8 %all-to-all-done = bf16[64,4,2048]{2,1,0:T(4,128)(2,1)S(1)} async-done(((bf16[64,4,2048]{2,1,0:T(4,128)(2,1)}), bf16[64,4,2048]{2,1,0:T(4,128)(2,1)S(1)}, u32[]{:S(2)}, u32[]{:S(2)}) %all-to-all-start) | async-done | bytes 1048608 | tf_op jit(solution)/shard_map/all_to_all | solution.py:84
  40.1 0.0 copy-start.2
  40.1 9.7 %all-to-all-start.1 = ((bf16[64,4,2048]{2,1,0:T(4,128)(2,1)}), bf16[64,4,2048]{2,1,0:T(4,128)(2,1)S(1)}, u32[]{:S(2)}, u32[]{:S(2)}) async-start(bf16[64,4,2048]{2,1,0:T(4,128)(2,1)} %reshape.93), calls=%async_computation.1 | async-start | bytes 2097152 | tf_op jit(solution)/shard_map/all_to_all | solution.py:107
  49.8 0.0 copy-done.2
  49.8 1.3 %reshape.91.w_ref = bf16[256,2048]{1,0:T(8,128)(2,1)S(1)} reshape(bf16[64,4,2048]{2,1,0:T(4,128)(2,1)} %copy-done.2) | data formatting | bytes 2097152 | tf_op jit(solution)/shard_map/reshape | solution.py:95
  51.2 1.4 %kraw.1 = (f32[128,256]{1,0:T(8,128)S(1)}, bf16[128,256]{1,0:T(8,128)(2,1)S(1)}, bf16[128,2048]{1,0:T(8,128)(2,1)}) custom-call(bf16[128,2048]{1,0:T(8,128)(2,1)S(1)} %copy-done, bf16[128,2048]{1,0:T(8,128)(2,1)S(1)} %collective-permute-done.par_ref, bf16[128,256]{1,0:T(8,128)(2,1)S(1)} %collective-permute-done.1.kb_ref, bf16[256,2048]{1,0:T(8,128)(2,1)S(1)} %reshape.91.w_ref), custom_call_target="tpu_custom_call" | custom-call | tf_op jit(solution)/shard_map/kraw/pallas_call | solution.py:96
  52.6 5.4 %all-gather = bf16[256,256]{1,0:T(8,128)(2,1)S(1)} all-gather(bf16[128,256]{1,0:T(8,128)(2,1)S(1)} %get-tuple-element.11), channel_id=2, replica_groups=mesh['zl'=2,'y'=8,'x'=8,'zh'=4,'c'=2] {'c'}, dimensions={0}, use_global_device_ids=true | all-gather | bytes 196608 | tf_op jit(solution)/shard_map/all_gather | solution.py:103
  58.0 5.3 %all-gather.1 = bf16[128,256]{1,0:T(8,128)(2,1)S(1)} all-gather(bf16[64,256]{1,0:T(8,128)(2,1)S(1)} %get-tuple-element.13), channel_id=3, replica_groups=mesh['zl'=2,'y'=8,'x'=8,'zh'=4,'c'=2] {'zl'}, dimensions={0}, use_global_device_ids=true | all-gather | bytes 98304 | tf_op jit(solution)/shard_map/all_gather | solution.py:106
  63.3 15.2 %collective-permute-start.4 = (bf16[64,512]{1,0:T(8,128)(2,1)S(1)}, bf16[64,512]{1,0:T(8,128)(2,1)S(1)}, u32[]{:S(2)}, u32[]{:S(2)}) collective-permute-start(bf16[64,512]{1,0:T(8,128)(2,1)S(1)} %maximum_select_fusion), channel_id=1, source_target_pairs={{0,6},{2,0},{4,2},{6,4},{1,7},{3,1},{5,3},{7,5},{8,14},{10,8},{12,... | collective-permute-start | bytes 196616 | tf_op jit(solution)/shard_map/ppermute | solution.py:113
  78.6 1.9 %collective-permute-start.3 = (bf16[64,512]{1,0:T(8,128)(2,1)S(1)}, bf16[64,512]{1,0:T(8,128)(2,1)S(1)}, u32[]{:S(2)}, u32[]{:S(2)}) collective-permute-start(bf16[64,512]{1,0:T(8,128)(2,1)S(1)} %maximum_select_fusion), channel_id=1, source_target_pairs={{0,2},{2,4},{4,6},{6,0},{1,3},{3,5},{5,7},{7,1},{8,10},{10,12},{12... | collective-permute-start | bytes 196616 | tf_op jit(solution)/shard_map/ppermute | solution.py:113
  80.5 4.0 %collective-permute-start.2 = (bf16[64,512]{1,0:T(8,128)(2,1)S(1)}, bf16[64,512]{1,0:T(8,128)(2,1)S(1)}, u32[]{:S(2)}, u32[]{:S(2)}) collective-permute-start(bf16[64,512]{1,0:T(8,128)(2,1)S(1)} %maximum_select_fusion), channel_id=1, source_target_pairs={{0,4},{2,6},{4,0},{6,2},{1,5},{3,7},{5,1},{7,3},{8,12},{10,14},{12... | collective-permute-start | bytes 196616 | tf_op jit(solution)/shard_map/ppermute | solution.py:113
  84.5 3.4 %collective-permute-start.5 = (bf16[128,2048]{1,0:T(8,128)(2,1)}, bf16[128,2048]{1,0:T(8,128)(2,1)S(1)}, u32[]{:S(2)}, u32[]{:S(2)}) collective-permute-start(bf16[128,2048]{1,0:T(8,128)(2,1)} %get-tuple-element.14), channel_id=1, source_target_pairs={{0,512},{512,0},{1,513},{513,1},{2,514},{514,2},{3,515},{515,3},{4... | collective-permute-start | bytes 1572872 | tf_op jit(solution)/shard_map/ppermute | solution.py:102
  87.9 0.0 collective-permute-done.4
  87.9 0.0 collective-permute-done.3
  87.9 1.6 %collective-permute-done.2 = bf16[64,512]{1,0:T(8,128)(2,1)S(1)} collective-permute-done((bf16[64,512]{1,0:T(8,128)(2,1)S(1)}, bf16[64,512]{1,0:T(8,128)(2,1)S(1)}, u32[]{:S(2)}, u32[]{:S(2)}) %collective-permute-start.2) | collective-permute-done | bytes 65568 | tf_op jit(solution)/shard_map/ppermute | solution.py:113
  89.6 0.2 subtract_convert_fusion.1
  89.8 0.1 pad_maximum_fusion.1
  89.9 3.9 %all_gather.19 = bf16[128,512]{1,0:T(8,128)(2,1)S(1)} all-gather(bf16[64,512]{1,0:T(8,128)(2,1)S(1)} %bitcast.18), channel_id=1, replica_groups=mesh['zl'=2,'y'=8,'x'=8,'zh'=4,'c'=2] {'c'}, dimensions={0}, use_global_device_ids=true | all-gather | bytes 196608 | tf_op jit(solution)/shard_map/all_gather | solution.py:120
  93.8 0.0 all-to-all-done.1.in_ref
  93.8 1.1 %sum.1 = f32[4,2048]{1,0:T(4,128)} custom-call(bf16[64,4,2048]{2,1,0:T(4,128)(2,1)S(1)} %all-to-all-done.1.in_ref), custom_call_target="tpu_custom_call" | custom-call | tf_op jit(solution)/shard_map/sum/pallas_call | solution.py:122
  94.8 6.7 %collective-permute-done.5.add_ref = bf16[128,2048]{1,0:T(8,128)(2,1)S(1)} collective-permute-done((bf16[128,2048]{1,0:T(8,128)(2,1)}, bf16[128,2048]{1,0:T(8,128)(2,1)S(1)}, u32[]{:S(2)}, u32[]{:S(2)}) %collective-permute-start.5) | collective-permute-done | bytes 524320 | tf_op jit(solution)/shard_map/ppermute | solution.py:102
  101.5 1.1 %grad.1 = bf16[128,2048]{1,0:T(8,128)(2,1)} custom-call(bf16[128,256]{1,0:T(8,128)(2,1)S(1)} %get-tuple-element.21.kb_ref, bf16[256,2048]{1,0:T(8,128)(2,1)S(1)} %reshape.91.w_ref, bf16[128,2048]{1,0:T(8,128)(2,1)S(1)} %collective-permute-done.5.add_ref), custom_call_target="tpu_custom_call" | custom-call | tf_op jit(solution)/shard_map/grad/pallas_call | solution.py:124
  102.6 0.7 copy.14
  (11 shorter events, 0.2 us)
Async XLA Ops:
  0.6 15.9 %copy-start = (bf16[128,2048]{1,0:T(8,128)(2,1)S(1)}, bf16[128,2048]{1,0:T(8,128)(2,1)}, u32[]{:S(2)}) copy-start(bf16[128,2048]{1,0:T(8,128)(2,1)} %tok_ref.1) | copy-start | bytes 1572868
  0.6 0.8 copy-start.1
  1.4 20.1 %copy-start.3 = (bf16[128,512]{1,0:T(8,128)(2,1)S(1)}, bf16[128,512]{1,0:T(8,128)(2,1)}, u32[]{:S(2)}) copy-start(bf16[128,512]{1,0:T(8,128)(2,1)} %param.7) | copy-start | bytes 393220
  1.4 20.2 %copy-start.4 = (s32[1,128]{1,0:T(1,128)S(1)}, s32[1,128]{1,0:T(1,128)}, u32[]{:S(2)}) copy-start(s32[1,128]{1,0:T(1,128)} %param.5) | copy-start | bytes 1540
  2.5 37.6 %all-to-all-start = ((bf16[64,4,2048]{2,1,0:T(4,128)(2,1)}), bf16[64,4,2048]{2,1,0:T(4,128)(2,1)S(1)}, u32[]{:S(2)}, u32[]{:S(2)}) async-start(bf16[64,4,2048]{2,1,0:T(4,128)(2,1)} %spread.1), calls=%async_computation | async-start | bytes 2097152 | tf_op jit(solution)/shard_map/all_to_all | solution.py:84
  16.6 16.0 %collective-permute-start = (bf16[128,2048]{1,0:T(8,128)(2,1)S(1)}, bf16[128,2048]{1,0:T(8,128)(2,1)S(1)}, u32[]{:S(2)}, u32[]{:S(2)}) collective-permute-start(bf16[128,2048]{1,0:T(8,128)(2,1)S(1)} %copy-done), channel_id=1, source_target_pairs={{0,512},{512,0},{1,513},{513,1},{2,514},{514,2},{3,515},{515,3},{4... | collective-permute-start | bytes 1572872 | tf_op jit(solution)/shard_map/ppermute | solution.py:85
  22.7 9.9 %collective-permute-start.1 = (bf16[128,256]{1,0:T(8,128)(2,1)S(1)}, bf16[128,256]{1,0:T(8,128)(2,1)S(1)}, u32[]{:S(2)}, u32[]{:S(2)}) collective-permute-start(bf16[128,256]{1,0:T(8,128)(2,1)S(1)} %get-tuple-element.22), channel_id=1, source_target_pairs={{0,512},{512,0},{1,513},{513,1},{2,514},{514,2},{3,515},{515,3},{4... | collective-permute-start | bytes 196616 | tf_op jit(solution)/shard_map/ppermute | solution.py:90
  40.1 9.7 %copy-start.2 = (bf16[64,4,2048]{2,1,0:T(4,128)(2,1)}, bf16[64,4,2048]{2,1,0:T(4,128)(2,1)S(1)}, u32[]{:S(2)}) copy-start(bf16[64,4,2048]{2,1,0:T(4,128)(2,1)S(1)} %all-to-all-done) | copy-start | bytes 3145732
  40.1 53.7 %all-to-all-start.1 = ((bf16[64,4,2048]{2,1,0:T(4,128)(2,1)}), bf16[64,4,2048]{2,1,0:T(4,128)(2,1)S(1)}, u32[]{:S(2)}, u32[]{:S(2)}) async-start(bf16[64,4,2048]{2,1,0:T(4,128)(2,1)} %reshape.93), calls=%async_computation.1 | async-start | bytes 2097152 | tf_op jit(solution)/shard_map/all_to_all | solution.py:107
  63.3 24.6 %collective-permute-start.4 = (bf16[64,512]{1,0:T(8,128)(2,1)S(1)}, bf16[64,512]{1,0:T(8,128)(2,1)S(1)}, u32[]{:S(2)}, u32[]{:S(2)}) collective-permute-start(bf16[64,512]{1,0:T(8,128)(2,1)S(1)} %maximum_select_fusion), channel_id=1, source_target_pairs={{0,6},{2,0},{4,2},{6,4},{1,7},{3,1},{5,3},{7,5},{8,14},{10,8},{12,... | collective-permute-start | bytes 196616 | tf_op jit(solution)/shard_map/ppermute | solution.py:113
  78.6 9.4 %collective-permute-start.3 = (bf16[64,512]{1,0:T(8,128)(2,1)S(1)}, bf16[64,512]{1,0:T(8,128)(2,1)S(1)}, u32[]{:S(2)}, u32[]{:S(2)}) collective-permute-start(bf16[64,512]{1,0:T(8,128)(2,1)S(1)} %maximum_select_fusion), channel_id=1, source_target_pairs={{0,2},{2,4},{4,6},{6,0},{1,3},{3,5},{5,7},{7,1},{8,10},{10,12},{12... | collective-permute-start | bytes 196616 | tf_op jit(solution)/shard_map/ppermute | solution.py:113
  80.5 9.0 %collective-permute-start.2 = (bf16[64,512]{1,0:T(8,128)(2,1)S(1)}, bf16[64,512]{1,0:T(8,128)(2,1)S(1)}, u32[]{:S(2)}, u32[]{:S(2)}) collective-permute-start(bf16[64,512]{1,0:T(8,128)(2,1)S(1)} %maximum_select_fusion), channel_id=1, source_target_pairs={{0,4},{2,6},{4,0},{6,2},{1,5},{3,7},{5,1},{7,3},{8,12},{10,14},{12... | collective-permute-start | bytes 196616 | tf_op jit(solution)/shard_map/ppermute | solution.py:113
  84.5 17.0 %collective-permute-start.5 = (bf16[128,2048]{1,0:T(8,128)(2,1)}, bf16[128,2048]{1,0:T(8,128)(2,1)S(1)}, u32[]{:S(2)}, u32[]{:S(2)}) collective-permute-start(bf16[128,2048]{1,0:T(8,128)(2,1)} %get-tuple-element.14), channel_id=1, source_target_pairs={{0,512},{512,0},{1,513},{513,1},{2,514},{514,2},{3,515},{515,3},{4... | collective-permute-start | bytes 1572872 | tf_op jit(solution)/shard_map/ppermute | solution.py:102

commit v9 on v7

--- a/solution.py
+++ b/solution.py
@@ -67,7 +67,7 @@
         out_shape=outs,
         in_specs=[vmem] * n_in,
         out_specs=jax.tree.map(lambda _: vmem, outs),
-        compiler_params=pltpu.CompilerParams(vmem_limit_bytes=32 << 20),
+        compiler_params=pltpu.CompilerParams(vmem_limit_bytes=12 << 20),
         name=name,
     )
 
@@ -96,7 +96,6 @@
         "kraw",
     )(tokens, tok_p, kb_p, weights)
     g_par = lax.ppermute(g_send, "zl", SWAP)
-    to_c, partial = lax.optimization_barrier((to_c, partial))
     from_c = lax.all_gather(to_c, "c")
     half = shape((64, 256), bf16)
     own, to_z = whole(merge_kernel, (half, half), 2, "merge")(keep, from_c)
@@ -110,7 +109,7 @@
         lax.ppermute(total_b, "zh", [(i, (i + step) % 4) for i in range(4)])
         for step in (1, 3, 2)
     )
-    total = (total_b.astype(f32) + two.astype(f32)) + (one.astype(f32) + three.astype(f32))
+    total = (three.astype(f32) + one.astype(f32)) + (two.astype(f32) + total_b.astype(f32))
     own_cos = lax.dynamic_slice_in_dim(cosine, core * 64, 64, 0)
     own_sin = lax.dynamic_slice_in_dim(sine, core * 64, 64, 0)
     keys = rotate(total, own_cos, own_sin, 1.0).astype(bf16)

time: 103 us -> 102 us (level)
  local copies, waits for them, and re-layouts: 4.17 us -> 3.12 us
    reshape x1, local copies, waits for them, and re-layouts: 1.33 us -> 0.28 us  [body(): weights = gathered.reshape(256, 2048)]
  transfers between devices with their start and end apart: 8 -> 8, of which waited for: 4 -> 4; matrix products, arithmetic and copies ran while one was open for 6% -> 6% of each run, Pallas kernels for 0% -> 1%
where the time goes in v9:
time: 102 us; the launch traced here: 101 us
  starting transfers between devices  55.4 us (54%)
  waiting for transfers between devices  18.9 us (19%)
  blocking collectives  15.5 us (15%)
  other arithmetic  3.61 us (4%)
  local copies, waits for them, and re-layouts  3.12 us (3%)
  Pallas kernels  2.85 us (3%)
    ppermute x3, starting transfers between devices, body(): lax.ppermute(total_b, 'zh', [(i, (i + step) % 4) for i in range(4)])  21.1 us
    all_to_all x1, starting transfers between devices, body(): gathered = lax.all_to_all(spread, ('y', 'x'), 0, 0)  14 us
    all_to_all x1, starting transfers between devices, body(): scattered = lax.all_to_all(partial, ('y', 'x'), 0, 0)  9.98 us
    ppermute x1, waiting for transfers between devices, body(): kb_p = lax.ppermute(jnp.where(zl == 0, right, left), 'zl', SWAP)  7.54 us
    all_to_all x1, waiting for transfers between devices, body(): gathered = lax.all_to_all(spread, ('y', 'x'), 0, 0)  5.81 us
    all_gather x1, blocking collectives, body(): from_c = lax.all_gather(to_c, 'c')  5.44 us
    all_gather x1, blocking collectives, body(): from_z = lax.all_gather(to_z, 'zl')  5.39 us
    ppermute x1, waiting for transfers between devices, body(): g_par = lax.ppermute(g_send, 'zl', SWAP)  5 us
  transfers between devices with their start and end apart: 8, of which 4 were waited for; matrix products, arithmetic and copies ran while one was open for 6% of the time, Pallas kernels for 1%

profile of v9, /device:TPU:1, one launch (start us, length us, event | category | flops | bytes accessed | tf_op | source)
XLA Modules:
  0.0 101.1 jit_solution(9216829164357675836)
XLA Ops:
  0.6 0.0 copy-start
  0.6 0.0 copy-start.1
  0.7 0.8 copy-done.1
  1.4 0.0 copy-start.2
  1.4 0.0 copy-start.3
  1.4 1.1 %spread.1 = bf16[64,4,2048]{2,1,0:T(4,128)(2,1)} custom-call(bf16[4,2048]{1,0:T(4,128)(2,1)S(1)} %copy-done.1), custom_call_target="tpu_custom_call" | custom-call | tf_op jit(solution)/shard_map/spread/pallas_call | solution.py:79
  2.5 14.0 %all-to-all-start = ((bf16[64,4,2048]{2,1,0:T(4,128)(2,1)}), bf16[64,4,2048]{2,1,0:T(4,128)(2,1)S(1)}, u32[]{:S(2)}, u32[]{:S(2)}) async-start(bf16[64,4,2048]{2,1,0:T(4,128)(2,1)} %spread.1), calls=%async_computation | async-start | bytes 2097152 | tf_op jit(solution)/shard_map/all_to_all | solution.py:80
  16.6 0.0 copy-done
  16.6 4.9 %collective-permute-start = (bf16[128,2048]{1,0:T(8,128)(2,1)S(1)}, bf16[128,2048]{1,0:T(8,128)(2,1)S(1)}, u32[]{:S(2)}, u32[]{:S(2)}) collective-permute-start(bf16[128,2048]{1,0:T(8,128)(2,1)S(1)} %copy-done), channel_id=1, source_target_pairs={{0,512},{512,0},{1,513},{513,1},{2,514},{514,2},{3,515},{515,3},{4... | collective-permute-start | bytes 1572872 | tf_op jit(solution)/shard_map/ppermute | solution.py:81
  21.5 0.0 copy-done.2
  21.5 0.1 reshape.95
  21.6 0.0 copy-done.3
  21.6 0.2 convert_reduce_fusion.1
  21.8 0.3 multiply_sine_fusion
  22.1 0.3 subtract_convert_fusion
  22.4 0.2 pad_maximum_fusion
  22.7 1.9 %collective-permute-start.1 = (bf16[128,256]{1,0:T(8,128)(2,1)S(1)}, bf16[128,256]{1,0:T(8,128)(2,1)S(1)}, u32[]{:S(2)}, u32[]{:S(2)}) collective-permute-start(bf16[128,256]{1,0:T(8,128)(2,1)S(1)} %get-tuple-element.22), channel_id=1, source_target_pairs={{0,512},{512,0},{1,513},{513,1},{2,514},{514,2},{3,515},{515,3},{4... | collective-permute-start | bytes 196616 | tf_op jit(solution)/shard_map/ppermute | solution.py:86
  24.6 0.5 fusion.2
  25.1 7.5 %collective-permute-done.1.kb_ref = bf16[128,256]{1,0:T(8,128)(2,1)S(1)} collective-permute-done((bf16[128,256]{1,0:T(8,128)(2,1)S(1)}, bf16[128,256]{1,0:T(8,128)(2,1)S(1)}, u32[]{:S(2)}, u32[]{:S(2)}) %collective-permute-start.1) | collective-permute-done | bytes 65568 | tf_op jit(solution)/shard_map/ppermute | solution.py:86
  32.6 0.0 collective-permute-done.par_ref
  32.6 0.5 fusion
  33.1 1.2 %reshape.93 = bf16[64,4,2048]{2,1,0:T(4,128)(2,1)} reshape(bf16[256,2048]{1,0:T(8,128)(2,1)S(1)} %fusion) | data formatting | bytes 2097152 | tf_op jit(solution)/shard_map/reshape | solution.py:89
  34.3 5.8 %all-to-all-done = bf16[64,4,2048]{2,1,0:T(4,128)(2,1)S(1)} async-done(((bf16[64,4,2048]{2,1,0:T(4,128)(2,1)}), bf16[64,4,2048]{2,1,0:T(4,128)(2,1)S(1)}, u32[]{:S(2)}, u32[]{:S(2)}) %all-to-all-start) | async-done | bytes 1048608 | tf_op jit(solution)/shard_map/all_to_all | solution.py:80
  40.1 10.0 %all-to-all-start.1 = ((bf16[64,4,2048]{2,1,0:T(4,128)(2,1)}), bf16[64,4,2048]{2,1,0:T(4,128)(2,1)}, u32[]{:S(2)}, u32[]{:S(2)}) async-start(bf16[64,4,2048]{2,1,0:T(4,128)(2,1)} %reshape.93), calls=%async_computation.1 | async-start | bytes 2097152 | tf_op jit(solution)/shard_map/all_to_all | solution.py:103
  50.1 0.3 reshape.91.w_ref
  50.4 0.6 kraw.1
  51.0 5.4 %all-gather = bf16[256,256]{1,0:T(8,128)(2,1)S(1)} all-gather(bf16[128,256]{1,0:T(8,128)(2,1)S(1)} %get-tuple-element.11), channel_id=2, replica_groups=mesh['zl'=2,'y'=8,'x'=8,'zh'=4,'c'=2] {'c'}, dimensions={0}, use_global_device_ids=true | all-gather | bytes 196608 | tf_op jit(solution)/shard_map/all_gather | solution.py:99
  56.4 5.4 %all-gather.1 = bf16[128,256]{1,0:T(8,128)(2,1)S(1)} all-gather(bf16[64,256]{1,0:T(8,128)(2,1)S(1)} %get-tuple-element.13), channel_id=3, replica_groups=mesh['zl'=2,'y'=8,'x'=8,'zh'=4,'c'=2] {'zl'}, dimensions={0}, use_global_device_ids=true | all-gather | bytes 98304 | tf_op jit(solution)/shard_map/all_gather | solution.py:102
  61.9 13.4 %collective-permute-start.4 = (bf16[64,512]{1,0:T(8,128)(2,1)S(1)}, bf16[64,512]{1,0:T(8,128)(2,1)S(1)}, u32[]{:S(2)}, u32[]{:S(2)}) collective-permute-start(bf16[64,512]{1,0:T(8,128)(2,1)S(1)} %maximum_select_fusion), channel_id=1, source_target_pairs={{0,4},{2,6},{4,0},{6,2},{1,5},{3,7},{5,1},{7,3},{8,12},{10,14},{12... | collective-permute-start | bytes 196616 | tf_op jit(solution)/shard_map/ppermute | solution.py:109
  75.2 5.8 %collective-permute-start.3 = (bf16[64,512]{1,0:T(8,128)(2,1)S(1)}, bf16[64,512]{1,0:T(8,128)(2,1)S(1)}, u32[]{:S(2)}, u32[]{:S(2)}) collective-permute-start(bf16[64,512]{1,0:T(8,128)(2,1)S(1)} %maximum_select_fusion), channel_id=1, source_target_pairs={{0,2},{2,4},{4,6},{6,0},{1,3},{3,5},{5,7},{7,1},{8,10},{10,12},{12... | collective-permute-start | bytes 196616 | tf_op jit(solution)/shard_map/ppermute | solution.py:109
  81.1 1.9 %collective-permute-start.2 = (bf16[64,512]{1,0:T(8,128)(2,1)S(1)}, bf16[64,512]{1,0:T(8,128)(2,1)S(1)}, u32[]{:S(2)}, u32[]{:S(2)}) collective-permute-start(bf16[64,512]{1,0:T(8,128)(2,1)S(1)} %maximum_select_fusion), channel_id=1, source_target_pairs={{0,6},{2,0},{4,2},{6,4},{1,7},{3,1},{5,3},{7,5},{8,14},{10,8},{12,... | collective-permute-start | bytes 196616 | tf_op jit(solution)/shard_map/ppermute | solution.py:109
  83.0 3.4 %collective-permute-start.5 = (bf16[128,2048]{1,0:T(8,128)(2,1)S(1)}, bf16[128,2048]{1,0:T(8,128)(2,1)S(1)}, u32[]{:S(2)}, u32[]{:S(2)}) collective-permute-start(bf16[128,2048]{1,0:T(8,128)(2,1)S(1)} %get-tuple-element.14), channel_id=1, source_target_pairs={{0,512},{512,0},{1,513},{513,1},{2,514},{514,2},{3,515},{515,3},{4... | collective-permute-start | bytes 1572872 | tf_op jit(solution)/shard_map/ppermute | solution.py:98
  86.4 0.0 collective-permute-done.4
  86.5 0.0 collective-permute-done.3
  86.5 0.5 collective-permute-done.2
  87.1 0.2 subtract_convert_fusion.1
  87.3 0.1 pad_maximum_fusion.1
  87.4 4.7 %all_gather.19 = bf16[128,512]{1,0:T(8,128)(2,1)S(1)} all-gather(bf16[64,512]{1,0:T(8,128)(2,1)S(1)} %bitcast.18), channel_id=1, replica_groups=mesh['zl'=2,'y'=8,'x'=8,'zh'=4,'c'=2] {'c'}, dimensions={0}, use_global_device_ids=true | all-gather | bytes 196608 | tf_op jit(solution)/shard_map/all_gather | solution.py:116
  92.1 0.0 all-to-all-done.1
  92.1 2.3 %convert_reduce_fusion = f32[4,2048]{1,0:T(4,128)} fusion(bf16[64,4,2048]{2,1,0:T(4,128)(2,1)} %all-to-all-done.1), kind=kLoop, calls=%fused_computation.2 | loop fusion | flops 1040384 | bytes 1081344 | tf_op jit(solution)/shard_map/reduce_sum | solution.py:118
  94.4 5.0 %collective-permute-done.5.add_ref = bf16[128,2048]{1,0:T(8,128)(2,1)S(1)} collective-permute-done((bf16[128,2048]{1,0:T(8,128)(2,1)S(1)}, bf16[128,2048]{1,0:T(8,128)(2,1)S(1)}, u32[]{:S(2)}, u32[]{:S(2)}) %collective-permute-start.5) | collective-permute-done | bytes 524320 | tf_op jit(solution)/shard_map/ppermute | solution.py:98
  99.4 1.1 %grad.1 = bf16[128,2048]{1,0:T(8,128)(2,1)} custom-call(bf16[128,256]{1,0:T(8,128)(2,1)S(1)} %get-tuple-element.21.kb_ref, bf16[256,2048]{1,0:T(8,128)(2,1)S(1)} %reshape.91.w_ref, bf16[128,2048]{1,0:T(8,128)(2,1)S(1)} %collective-permute-done.5.add_ref), custom_call_target="tpu_custom_call" | custom-call | tf_op jit(solution)/shard_map/grad/pallas_call | solution.py:120
  100.5 0.7 copy.14
  (11 shorter events, 0.2 us)
Async XLA Ops:
  0.6 16.0 %copy-start = (bf16[128,2048]{1,0:T(8,128)(2,1)S(1)}, bf16[128,2048]{1,0:T(8,128)(2,1)}, u32[]{:S(2)}) copy-start(bf16[128,2048]{1,0:T(8,128)(2,1)} %tok_ref.1) | copy-start | bytes 1572868
  0.6 0.8 copy-start.1
  1.4 20.1 %copy-start.2 = (bf16[128,512]{1,0:T(8,128)(2,1)S(1)}, bf16[128,512]{1,0:T(8,128)(2,1)}, u32[]{:S(2)}) copy-start(bf16[128,512]{1,0:T(8,128)(2,1)} %param.7) | copy-start | bytes 393220
  1.4 20.2 %copy-start.3 = (s32[1,128]{1,0:T(1,128)S(1)}, s32[1,128]{1,0:T(1,128)}, u32[]{:S(2)}) copy-start(s32[1,128]{1,0:T(1,128)} %param.5) | copy-start | bytes 1540
  2.5 37.6 %all-to-all-start = ((bf16[64,4,2048]{2,1,0:T(4,128)(2,1)}), bf16[64,4,2048]{2,1,0:T(4,128)(2,1)S(1)}, u32[]{:S(2)}, u32[]{:S(2)}) async-start(bf16[64,4,2048]{2,1,0:T(4,128)(2,1)} %spread.1), calls=%async_computation | async-start | bytes 2097152 | tf_op jit(solution)/shard_map/all_to_all | solution.py:80
  16.6 16.0 %collective-permute-start = (bf16[128,2048]{1,0:T(8,128)(2,1)S(1)}, bf16[128,2048]{1,0:T(8,128)(2,1)S(1)}, u32[]{:S(2)}, u32[]{:S(2)}) collective-permute-start(bf16[128,2048]{1,0:T(8,128)(2,1)S(1)} %copy-done), channel_id=1, source_target_pairs={{0,512},{512,0},{1,513},{513,1},{2,514},{514,2},{3,515},{515,3},{4... | collective-permute-start | bytes 1572872 | tf_op jit(solution)/shard_map/ppermute | solution.py:81
  22.7 9.9 %collective-permute-start.1 = (bf16[128,256]{1,0:T(8,128)(2,1)S(1)}, bf16[128,256]{1,0:T(8,128)(2,1)S(1)}, u32[]{:S(2)}, u32[]{:S(2)}) collective-permute-start(bf16[128,256]{1,0:T(8,128)(2,1)S(1)} %get-tuple-element.22), channel_id=1, source_target_pairs={{0,512},{512,0},{1,513},{513,1},{2,514},{514,2},{3,515},{515,3},{4... | collective-permute-start | bytes 196616 | tf_op jit(solution)/shard_map/ppermute | solution.py:86
  40.1 52.0 %all-to-all-start.1 = ((bf16[64,4,2048]{2,1,0:T(4,128)(2,1)}), bf16[64,4,2048]{2,1,0:T(4,128)(2,1)}, u32[]{:S(2)}, u32[]{:S(2)}) async-start(bf16[64,4,2048]{2,1,0:T(4,128)(2,1)} %reshape.93), calls=%async_computation.1 | async-start | bytes 2097152 | tf_op jit(solution)/shard_map/all_to_all | solution.py:103
  61.9 24.6 %collective-permute-start.4 = (bf16[64,512]{1,0:T(8,128)(2,1)S(1)}, bf16[64,512]{1,0:T(8,128)(2,1)S(1)}, u32[]{:S(2)}, u32[]{:S(2)}) collective-permute-start(bf16[64,512]{1,0:T(8,128)(2,1)S(1)} %maximum_select_fusion), channel_id=1, source_target_pairs={{0,4},{2,6},{4,0},{6,2},{1,5},{3,7},{5,1},{7,3},{8,12},{10,14},{12... | collective-permute-start | bytes 196616 | tf_op jit(solution)/shard_map/ppermute | solution.py:109
  75.2 11.2 %collective-permute-start.3 = (bf16[64,512]{1,0:T(8,128)(2,1)S(1)}, bf16[64,512]{1,0:T(8,128)(2,1)S(1)}, u32[]{:S(2)}, u32[]{:S(2)}) collective-permute-start(bf16[64,512]{1,0:T(8,128)(2,1)S(1)} %maximum_select_fusion), channel_id=1, source_target_pairs={{0,2},{2,4},{4,6},{6,0},{1,3},{3,5},{5,7},{7,1},{8,10},{10,12},{12... | collective-permute-start | bytes 196616 | tf_op jit(solution)/shard_map/ppermute | solution.py:109
  81.1 5.9 %collective-permute-start.2 = (bf16[64,512]{1,0:T(8,128)(2,1)S(1)}, bf16[64,512]{1,0:T(8,128)(2,1)S(1)}, u32[]{:S(2)}, u32[]{:S(2)}) collective-permute-start(bf16[64,512]{1,0:T(8,128)(2,1)S(1)} %maximum_select_fusion), channel_id=1, source_target_pairs={{0,6},{2,0},{4,2},{6,4},{1,7},{3,1},{5,3},{7,5},{8,14},{10,8},{12,... | collective-permute-start | bytes 196616 | tf_op jit(solution)/shard_map/ppermute | solution.py:109
  83.0 16.3 %collective-permute-start.5 = (bf16[128,2048]{1,0:T(8,128)(2,1)S(1)}, bf16[128,2048]{1,0:T(8,128)(2,1)S(1)}, u32[]{:S(2)}, u32[]{:S(2)}) collective-permute-start(bf16[128,2048]{1,0:T(8,128)(2,1)S(1)} %get-tuple-element.14), channel_id=1, source_target_pairs={{0,512},{512,0},{1,513},{513,1},{2,514},{514,2},{3,515},{515,3},{4... | collective-permute-start | bytes 1572872 | tf_op jit(solution)/shard_map/ppermute | solution.py:98

commit v10 on v9

--- a/solution.py
+++ b/solution.py
@@ -95,7 +95,6 @@
         4,
         "kraw",
     )(tokens, tok_p, kb_p, weights)
-    g_par = lax.ppermute(g_send, "zl", SWAP)
     from_c = lax.all_gather(to_c, "c")
     half = shape((64, 256), bf16)
     own, to_z = whole(merge_kernel, (half, half), 2, "merge")(keep, from_c)
@@ -105,10 +104,14 @@
     total_b = jnp.where(
         zl == 0, jnp.concatenate([own, from_z[1]], 1), jnp.concatenate([from_z[0], own], 1)
     )
+    total_b, g_send = lax.optimization_barrier((total_b, g_send))
+    g_par = lax.ppermute(g_send, "zl", SWAP)
     one, three, two = (
         lax.ppermute(total_b, "zh", [(i, (i + step) % 4) for i in range(4)])
         for step in (1, 3, 2)
     )
+    grad_tokens = whole(grad_kernel, shape((128, 2048), bf16), 3, "grad")(kb, weights, g_par)
+    three, one, two, grad_tokens = lax.optimization_barrier((three, one, two, grad_tokens))
     total = (three.astype(f32) + one.astype(f32)) + (two.astype(f32) + total_b.astype(f32))
     own_cos = lax.dynamic_slice_in_dim(cosine, core * 64, 64, 0)
     own_sin = lax.dynamic_slice_in_dim(sine, core * 64, 64, 0)
@@ -116,8 +119,6 @@
     keys = lax.all_gather(keys, "c", axis=0, tiled=True)
 
     grad_key_weight = jnp.sum(scattered.astype(f32), axis=0)
-    grad_key_weight, g_par = lax.optimization_barrier((grad_key_weight, g_par))
-    grad_tokens = whole(grad_kernel, shape((128, 2048), bf16), 3, "grad")(kb, weights, g_par)
     return keys, grad_tokens, grad_key_weight
 
 

time: 102 us -> 103 us (level)
  waiting for transfers between devices: 18.9 us -> 20.5 us
    ppermute x3, waiting for transfers between devices: 0.54 us -> 7.16 us  [body(): lax.ppermute(total_b, 'zh', [(i, (i + step) % 4) for i in range(4)])]
    ppermute x1, waiting for transfers between devices: 5 us -> 0.01 us  [body(): g_par = lax.ppermute(g_send, 'zl', SWAP)]
  transfers between devices with their start and end apart: 8 -> 8, of which waited for: 4 -> 4; matrix products, arithmetic and copies ran while one was open for 6% -> 4% of each run, Pallas kernels for 1% -> 2%
where the time goes in v10:
time: 103 us; the launch traced here: 102 us
  starting transfers between devices  55.4 us (54%)
  waiting for transfers between devices  20.5 us (20%)
  blocking collectives  14.7 us (14%)
  other arithmetic  3.61 us (4%)
  local copies, waits for them, and re-layouts  3.11 us (3%)
  Pallas kernels  2.85 us (3%)
    ppermute x3, starting transfers between devices, body(): lax.ppermute(total_b, 'zh', [(i, (i + step) % 4) for i in range(4)])  21.1 us
    all_to_all x1, starting transfers between devices, body(): gathered = lax.all_to_all(spread, ('y', 'x'), 0, 0)  14 us
    all_to_all x1, starting transfers between devices, body(): scattered = lax.all_to_all(partial, ('y', 'x'), 0, 0)  9.98 us
    ppermute x1, waiting for transfers between devices, body(): kb_p = lax.ppermute(jnp.where(zl == 0, right, left), 'zl', SWAP)  7.54 us
    ppermute x3, waiting for transfers between devices, body(): lax.ppermute(total_b, 'zh', [(i, (i + step) % 4) for i in range(4)])  7.16 us
    all_to_all x1, waiting for transfers between devices, body(): gathered = lax.all_to_all(spread, ('y', 'x'), 0, 0)  5.81 us
    all_gather x1, blocking collectives, body(): from_c = lax.all_gather(to_c, 'c')  5.44 us
    all_gather x1, blocking collectives, body(): from_z = lax.all_gather(to_z, 'zl')  5.4 us
  transfers between devices with their start and end apart: 8, of which 4 were waited for; matrix products, arithmetic and copies ran while one was open for 4% of the time, Pallas kernels for 2%

profile of v10, /device:TPU:1, one launch (start us, length us, event | category | flops | bytes accessed | tf_op | source)
XLA Modules:
  0.0 101.9 jit_solution(14806397649870506040)
XLA Ops:
  0.6 0.0 copy-start
  0.6 0.0 copy-start.1
  0.7 0.8 copy-done.1
  1.4 0.0 copy-start.2
  1.4 0.0 copy-start.3
  1.4 1.1 %spread.1 = bf16[64,4,2048]{2,1,0:T(4,128)(2,1)} custom-call(bf16[4,2048]{1,0:T(4,128)(2,1)S(1)} %copy-done.1), custom_call_target="tpu_custom_call" | custom-call | tf_op jit(solution)/shard_map/spread/pallas_call | solution.py:79
  2.5 14.0 %all-to-all-start = ((bf16[64,4,2048]{2,1,0:T(4,128)(2,1)}), bf16[64,4,2048]{2,1,0:T(4,128)(2,1)S(1)}, u32[]{:S(2)}, u32[]{:S(2)}) async-start(bf16[64,4,2048]{2,1,0:T(4,128)(2,1)} %spread.1), calls=%async_computation | async-start | bytes 2097152 | tf_op jit(solution)/shard_map/all_to_all | solution.py:80
  16.6 0.0 copy-done
  16.6 4.9 %collective-permute-start = (bf16[128,2048]{1,0:T(8,128)(2,1)S(1)}, bf16[128,2048]{1,0:T(8,128)(2,1)S(1)}, u32[]{:S(2)}, u32[]{:S(2)}) collective-permute-start(bf16[128,2048]{1,0:T(8,128)(2,1)S(1)} %copy-done), channel_id=1, source_target_pairs={{0,512},{512,0},{1,513},{513,1},{2,514},{514,2},{3,515},{515,3},{4... | collective-permute-start | bytes 1572872 | tf_op jit(solution)/shard_map/ppermute | solution.py:81
  21.5 0.0 copy-done.2
  21.5 0.1 reshape.95
  21.6 0.0 copy-done.3
  21.6 0.2 convert_reduce_fusion.1
  21.8 0.3 multiply_sine_fusion
  22.1 0.3 subtract_convert_fusion
  22.4 0.2 pad_maximum_fusion
  22.7 1.9 %collective-permute-start.1 = (bf16[128,256]{1,0:T(8,128)(2,1)S(1)}, bf16[128,256]{1,0:T(8,128)(2,1)S(1)}, u32[]{:S(2)}, u32[]{:S(2)}) collective-permute-start(bf16[128,256]{1,0:T(8,128)(2,1)S(1)} %get-tuple-element.30), channel_id=1, source_target_pairs={{0,512},{512,0},{1,513},{513,1},{2,514},{514,2},{3,515},{515,3},{4... | collective-permute-start | bytes 196616 | tf_op jit(solution)/shard_map/ppermute | solution.py:86
  24.6 0.5 fusion.2
  25.1 7.5 %collective-permute-done.1.kb_ref = bf16[128,256]{1,0:T(8,128)(2,1)S(1)} collective-permute-done((bf16[128,256]{1,0:T(8,128)(2,1)S(1)}, bf16[128,256]{1,0:T(8,128)(2,1)S(1)}, u32[]{:S(2)}, u32[]{:S(2)}) %collective-permute-start.1) | collective-permute-done | bytes 65568 | tf_op jit(solution)/shard_map/ppermute | solution.py:86
  32.6 0.0 collective-permute-done.par_ref
  32.6 0.5 fusion
  33.1 1.2 %reshape.93 = bf16[64,4,2048]{2,1,0:T(4,128)(2,1)} reshape(bf16[256,2048]{1,0:T(8,128)(2,1)S(1)} %fusion) | data formatting | bytes 2097152 | tf_op jit(solution)/shard_map/reshape | solution.py:89
  34.3 5.8 %all-to-all-done = bf16[64,4,2048]{2,1,0:T(4,128)(2,1)S(1)} async-done(((bf16[64,4,2048]{2,1,0:T(4,128)(2,1)}), bf16[64,4,2048]{2,1,0:T(4,128)(2,1)S(1)}, u32[]{:S(2)}, u32[]{:S(2)}) %all-to-all-start) | async-done | bytes 1048608 | tf_op jit(solution)/shard_map/all_to_all | solution.py:80
  40.1 10.0 %all-to-all-start.1 = ((bf16[64,4,2048]{2,1,0:T(4,128)(2,1)}), bf16[64,4,2048]{2,1,0:T(4,128)(2,1)}, u32[]{:S(2)}, u32[]{:S(2)}) async-start(bf16[64,4,2048]{2,1,0:T(4,128)(2,1)} %reshape.93), calls=%async_computation.1 | async-start | bytes 2097152 | tf_op jit(solution)/shard_map/all_to_all | solution.py:102
  50.1 0.3 reshape.91.w_ref
  50.4 0.6 kraw.1
  51.0 5.4 %all-gather = bf16[256,256]{1,0:T(8,128)(2,1)S(1)} all-gather(bf16[128,256]{1,0:T(8,128)(2,1)S(1)} %get-tuple-element.15), channel_id=2, replica_groups=mesh['zl'=2,'y'=8,'x'=8,'zh'=4,'c'=2] {'c'}, dimensions={0}, use_global_device_ids=true | all-gather | bytes 196608 | tf_op jit(solution)/shard_map/all_gather | solution.py:98
  56.4 5.4 %all-gather.1 = bf16[128,256]{1,0:T(8,128)(2,1)S(1)} all-gather(bf16[64,256]{1,0:T(8,128)(2,1)S(1)} %get-tuple-element.17), channel_id=3, replica_groups=mesh['zl'=2,'y'=8,'x'=8,'zh'=4,'c'=2] {'zl'}, dimensions={0}, use_global_device_ids=true | all-gather | bytes 98304 | tf_op jit(solution)/shard_map/all_gather | solution.py:101
  61.9 3.4 %collective-permute-start.5 = (bf16[128,2048]{1,0:T(8,128)(2,1)S(1)}, bf16[128,2048]{1,0:T(8,128)(2,1)S(1)}, u32[]{:S(2)}, u32[]{:S(2)}) collective-permute-start(bf16[128,2048]{1,0:T(8,128)(2,1)S(1)} %get-tuple-element.20), channel_id=1, source_target_pairs={{0,512},{512,0},{1,513},{513,1},{2,514},{514,2},{3,515},{515,3},{4... | collective-permute-start | bytes 1572872 | tf_op jit(solution)/shard_map/ppermute | solution.py:108
  65.3 13.4 %collective-permute-start.4 = (bf16[64,512]{1,0:T(8,128)(2,1)S(1)}, bf16[64,512]{1,0:T(8,128)(2,1)S(1)}, u32[]{:S(2)}, u32[]{:S(2)}) collective-permute-start(bf16[64,512]{1,0:T(8,128)(2,1)S(1)} %maximum_select_fusion), channel_id=1, source_target_pairs={{0,4},{2,6},{4,0},{6,2},{1,5},{3,7},{5,1},{7,3},{8,12},{10,14},{12... | collective-permute-start | bytes 196616 | tf_op jit(solution)/shard_map/ppermute | solution.py:110
  78.7 5.8 %collective-permute-start.3 = (bf16[64,512]{1,0:T(8,128)(2,1)S(1)}, bf16[64,512]{1,0:T(8,128)(2,1)S(1)}, u32[]{:S(2)}, u32[]{:S(2)}) collective-permute-start(bf16[64,512]{1,0:T(8,128)(2,1)S(1)} %maximum_select_fusion), channel_id=1, source_target_pairs={{0,2},{2,4},{4,6},{6,0},{1,3},{3,5},{5,7},{7,1},{8,10},{10,12},{12... | collective-permute-start | bytes 196616 | tf_op jit(solution)/shard_map/ppermute | solution.py:110
  84.5 1.9 %collective-permute-start.2 = (bf16[64,512]{1,0:T(8,128)(2,1)S(1)}, bf16[64,512]{1,0:T(8,128)(2,1)S(1)}, u32[]{:S(2)}, u32[]{:S(2)}) collective-permute-start(bf16[64,512]{1,0:T(8,128)(2,1)S(1)} %maximum_select_fusion), channel_id=1, source_target_pairs={{0,6},{2,0},{4,2},{6,4},{1,7},{3,1},{5,3},{7,5},{8,14},{10,8},{12,... | collective-permute-start | bytes 196616 | tf_op jit(solution)/shard_map/ppermute | solution.py:110
  86.4 0.0 collective-permute-done.5.add_ref
  86.5 1.1 %grad.1 = bf16[128,2048]{1,0:T(8,128)(2,1)} custom-call(bf16[128,256]{1,0:T(8,128)(2,1)S(1)} %get-tuple-element.29.kb_ref, bf16[256,2048]{1,0:T(8,128)(2,1)S(1)} %reshape.91.w_ref, bf16[128,2048]{1,0:T(8,128)(2,1)S(1)} %collective-permute-done.5.add_ref), custom_call_target="tpu_custom_call" | custom-call | tf_op jit(solution)/shard_map/grad/pallas_call | solution.py:113
  87.6 3.6 %collective-permute-done.4 = bf16[64,512]{1,0:T(8,128)(2,1)S(1)} collective-permute-done((bf16[64,512]{1,0:T(8,128)(2,1)S(1)}, bf16[64,512]{1,0:T(8,128)(2,1)S(1)}, u32[]{:S(2)}, u32[]{:S(2)}) %collective-permute-start.4) | collective-permute-done | bytes 65568 | tf_op jit(solution)/shard_map/ppermute | solution.py:110
  91.1 3.6 %collective-permute-done.3 = bf16[64,512]{1,0:T(8,128)(2,1)S(1)} collective-permute-done((bf16[64,512]{1,0:T(8,128)(2,1)S(1)}, bf16[64,512]{1,0:T(8,128)(2,1)S(1)}, u32[]{:S(2)}, u32[]{:S(2)}) %collective-permute-start.3) | collective-permute-done | bytes 65568 | tf_op jit(solution)/shard_map/ppermute | solution.py:110
  94.7 0.0 collective-permute-done.2
  94.8 0.2 subtract_convert_fusion.1
  95.0 0.1 pad_maximum_fusion.1
  95.1 3.9 %all_gather.19 = bf16[128,512]{1,0:T(8,128)(2,1)S(1)} all-gather(bf16[64,512]{1,0:T(8,128)(2,1)S(1)} %bitcast.18), channel_id=1, replica_groups=mesh['zl'=2,'y'=8,'x'=8,'zh'=4,'c'=2] {'c'}, dimensions={0}, use_global_device_ids=true | all-gather | bytes 196608 | tf_op jit(solution)/shard_map/all_gather | solution.py:119
  99.0 0.0 all-to-all-done.1
  99.0 2.3 %convert_reduce_fusion = f32[4,2048]{1,0:T(4,128)} fusion(bf16[64,4,2048]{2,1,0:T(4,128)(2,1)} %all-to-all-done.1), kind=kLoop, calls=%fused_computation.2 | loop fusion | flops 1040384 | bytes 1081344 | tf_op jit(solution)/shard_map/reduce_sum | solution.py:121
  101.3 0.7 copy.14
  (11 shorter events, 0.2 us)
Async XLA Ops:
  0.6 16.0 %copy-start = (bf16[128,2048]{1,0:T(8,128)(2,1)S(1)}, bf16[128,2048]{1,0:T(8,128)(2,1)}, u32[]{:S(2)}) copy-start(bf16[128,2048]{1,0:T(8,128)(2,1)} %tok_ref.1) | copy-start | bytes 1572868
  0.6 0.8 copy-start.1
  1.4 20.1 %copy-start.2 = (bf16[128,512]{1,0:T(8,128)(2,1)S(1)}, bf16[128,512]{1,0:T(8,128)(2,1)}, u32[]{:S(2)}) copy-start(bf16[128,512]{1,0:T(8,128)(2,1)} %param.7) | copy-start | bytes 393220
  1.4 20.2 %copy-start.3 = (s32[1,128]{1,0:T(1,128)S(1)}, s32[1,128]{1,0:T(1,128)}, u32[]{:S(2)}) copy-start(s32[1,128]{1,0:T(1,128)} %param.5) | copy-start | bytes 1540
  2.5 37.6 %all-to-all-start = ((bf16[64,4,2048]{2,1,0:T(4,128)(2,1)}), bf16[64,4,2048]{2,1,0:T(4,128)(2,1)S(1)}, u32[]{:S(2)}, u32[]{:S(2)}) async-start(bf16[64,4,2048]{2,1,0:T(4,128)(2,1)} %spread.1), calls=%async_computation | async-start | bytes 2097152 | tf_op jit(solution)/shard_map/all_to_all | solution.py:80
  16.6 16.0 %collective-permute-start = (bf16[128,2048]{1,0:T(8,128)(2,1)S(1)}, bf16[128,2048]{1,0:T(8,128)(2,1)S(1)}, u32[]{:S(2)}, u32[]{:S(2)}) collective-permute-start(bf16[128,2048]{1,0:T(8,128)(2,1)S(1)} %copy-done), channel_id=1, source_target_pairs={{0,512},{512,0},{1,513},{513,1},{2,514},{514,2},{3,515},{515,3},{4... | collective-permute-start | bytes 1572872 | tf_op jit(solution)/shard_map/ppermute | solution.py:81
  22.7 9.9 %collective-permute-start.1 = (bf16[128,256]{1,0:T(8,128)(2,1)S(1)}, bf16[128,256]{1,0:T(8,128)(2,1)S(1)}, u32[]{:S(2)}, u32[]{:S(2)}) collective-permute-start(bf16[128,256]{1,0:T(8,128)(2,1)S(1)} %get-tuple-element.30), channel_id=1, source_target_pairs={{0,512},{512,0},{1,513},{513,1},{2,514},{514,2},{3,515},{515,3},{4... | collective-permute-start | bytes 196616 | tf_op jit(solution)/shard_map/ppermute | solution.py:86
  40.1 58.9 %all-to-all-start.1 = ((bf16[64,4,2048]{2,1,0:T(4,128)(2,1)}), bf16[64,4,2048]{2,1,0:T(4,128)(2,1)}, u32[]{:S(2)}, u32[]{:S(2)}) async-start(bf16[64,4,2048]{2,1,0:T(4,128)(2,1)} %reshape.93), calls=%async_computation.1 | async-start | bytes 2097152 | tf_op jit(solution)/shard_map/all_to_all | solution.py:102
  61.9 24.6 %collective-permute-start.5 = (bf16[128,2048]{1,0:T(8,128)(2,1)S(1)}, bf16[128,2048]{1,0:T(8,128)(2,1)S(1)}, u32[]{:S(2)}, u32[]{:S(2)}) collective-permute-start(bf16[128,2048]{1,0:T(8,128)(2,1)S(1)} %get-tuple-element.20), channel_id=1, source_target_pairs={{0,512},{512,0},{1,513},{513,1},{2,514},{514,2},{3,515},{515,3},{4... | collective-permute-start | bytes 1572872 | tf_op jit(solution)/shard_map/ppermute | solution.py:108
  65.3 25.9 %collective-permute-start.4 = (bf16[64,512]{1,0:T(8,128)(2,1)S(1)}, bf16[64,512]{1,0:T(8,128)(2,1)S(1)}, u32[]{:S(2)}, u32[]{:S(2)}) collective-permute-start(bf16[64,512]{1,0:T(8,128)(2,1)S(1)} %maximum_select_fusion), channel_id=1, source_target_pairs={{0,4},{2,6},{4,0},{6,2},{1,5},{3,7},{5,1},{7,3},{8,12},{10,14},{12... | collective-permute-start | bytes 196616 | tf_op jit(solution)/shard_map/ppermute | solution.py:110
  78.7 16.1 %collective-permute-start.3 = (bf16[64,512]{1,0:T(8,128)(2,1)S(1)}, bf16[64,512]{1,0:T(8,128)(2,1)S(1)}, u32[]{:S(2)}, u32[]{:S(2)}) collective-permute-start(bf16[64,512]{1,0:T(8,128)(2,1)S(1)} %maximum_select_fusion), channel_id=1, source_target_pairs={{0,2},{2,4},{4,6},{6,0},{1,3},{3,5},{5,7},{7,1},{8,10},{10,12},{12... | collective-permute-start | bytes 196616 | tf_op jit(solution)/shard_map/ppermute | solution.py:110
  84.5 10.2 %collective-permute-start.2 = (bf16[64,512]{1,0:T(8,128)(2,1)S(1)}, bf16[64,512]{1,0:T(8,128)(2,1)S(1)}, u32[]{:S(2)}, u32[]{:S(2)}) collective-permute-start(bf16[64,512]{1,0:T(8,128)(2,1)S(1)} %maximum_select_fusion), channel_id=1, source_target_pairs={{0,6},{2,0},{4,2},{6,4},{1,7},{3,1},{5,3},{7,5},{8,14},{10,8},{12,... | collective-permute-start | bytes 196616 | tf_op jit(solution)/shard_map/ppermute | solution.py:110

commit v11 on v10

--- a/solution.py
+++ b/solution.py
@@ -111,14 +111,16 @@
         for step in (1, 3, 2)
     )
     grad_tokens = whole(grad_kernel, shape((128, 2048), bf16), 3, "grad")(kb, weights, g_par)
-    three, one, two, grad_tokens = lax.optimization_barrier((three, one, two, grad_tokens))
+    grad_key_weight = jnp.sum(scattered.astype(f32), axis=0)
+    three, one, two, grad_tokens, grad_key_weight = lax.optimization_barrier(
+        (three, one, two, grad_tokens, grad_key_weight)
+    )
     total = (three.astype(f32) + one.astype(f32)) + (two.astype(f32) + total_b.astype(f32))
     own_cos = lax.dynamic_slice_in_dim(cosine, core * 64, 64, 0)
     own_sin = lax.dynamic_slice_in_dim(sine, core * 64, 64, 0)
     keys = rotate(total, own_cos, own_sin, 1.0).astype(bf16)
     keys = lax.all_gather(keys, "c", axis=0, tiled=True)
 
-    grad_key_weight = jnp.sum(scattered.astype(f32), axis=0)
     return keys, grad_tokens, grad_key_weight
 
 

time: 103 us -> 100 us (0.971)
  waiting for transfers between devices: 20.5 us -> 18.2 us
    ppermute x3, waiting for transfers between devices: 7.16 us -> 4.87 us  [body(): lax.ppermute(total_b, 'zh', [(i, (i + step) % 4) for i in range(4)])]
  transfers between devices with their start and end apart: 8 -> 8, of which waited for: 4 -> 4; matrix products, arithmetic and copies ran while one was open for 4% -> 6% of each run, Pallas kernels for 2% -> 2%
where the time goes in v11:
time: 100 us; the launch traced here: 99.7 us
  starting transfers between devices  55.4 us (55%)
  waiting for transfers between devices  18.2 us (18%)
  blocking collectives  14.7 us (15%)
  other arithmetic  3.61 us (4%)
  local copies, waits for them, and re-layouts  3.11 us (3%)
  Pallas kernels  2.85 us (3%)
    ppermute x3, starting transfers between devices, body(): lax.ppermute(total_b, 'zh', [(i, (i + step) % 4) for i in range(4)])  21.1 us
    all_to_all x1, starting transfers between devices, body(): gathered = lax.all_to_all(spread, ('y', 'x'), 0, 0)  14 us
    all_to_all x1, starting transfers between devices, body(): scattered = lax.all_to_all(partial, ('y', 'x'), 0, 0)  9.98 us
    ppermute x1, waiting for transfers between devices, body(): kb_p = lax.ppermute(jnp.where(zl == 0, right, left), 'zl', SWAP)  7.54 us
    all_to_all x1, waiting for transfers between devices, body(): gathered = lax.all_to_all(spread, ('y', 'x'), 0, 0)  5.81 us
    all_gather x1, blocking collectives, body(): from_c = lax.all_gather(to_c, 'c')  5.44 us
    all_gather x1, blocking collectives, body(): from_z = lax.all_gather(to_z, 'zl')  5.4 us
    ppermute x1, starting transfers between devices, body(): tok_p = lax.ppermute(tokens, 'zl', SWAP)  4.91 us
  transfers between devices with their start and end apart: 8, of which 4 were waited for; matrix products, arithmetic and copies ran while one was open for 6% of the time, Pallas kernels for 2%

profile of v11, /device:TPU:1, one launch (start us, length us, event | category | flops | bytes accessed | tf_op | source)
XLA Modules:
  0.0 99.7 jit_solution(877726670853470884)
XLA Ops:
  0.6 0.0 copy-start
  0.6 0.0 copy-start.1
  0.7 0.8 copy-done.1
  1.4 0.0 copy-start.2
  1.4 0.0 copy-start.3
  1.4 1.1 %spread.1 = bf16[64,4,2048]{2,1,0:T(4,128)(2,1)} custom-call(bf16[4,2048]{1,0:T(4,128)(2,1)S(1)} %copy-done.1), custom_call_target="tpu_custom_call" | custom-call | tf_op jit(solution)/shard_map/spread/pallas_call | solution.py:79
  2.5 14.0 %all-to-all-start = ((bf16[64,4,2048]{2,1,0:T(4,128)(2,1)}), bf16[64,4,2048]{2,1,0:T(4,128)(2,1)S(1)}, u32[]{:S(2)}, u32[]{:S(2)}) async-start(bf16[64,4,2048]{2,1,0:T(4,128)(2,1)} %spread.1), calls=%async_computation | async-start | bytes 2097152 | tf_op jit(solution)/shard_map/all_to_all | solution.py:80
  16.6 0.0 copy-done
  16.6 4.9 %collective-permute-start = (bf16[128,2048]{1,0:T(8,128)(2,1)S(1)}, bf16[128,2048]{1,0:T(8,128)(2,1)S(1)}, u32[]{:S(2)}, u32[]{:S(2)}) collective-permute-start(bf16[128,2048]{1,0:T(8,128)(2,1)S(1)} %copy-done), channel_id=1, source_target_pairs={{0,512},{512,0},{1,513},{513,1},{2,514},{514,2},{3,515},{515,3},{4... | collective-permute-start | bytes 1572872 | tf_op jit(solution)/shard_map/ppermute | solution.py:81
  21.5 0.0 copy-done.2
  21.5 0.1 reshape.95
  21.6 0.0 copy-done.3
  21.6 0.2 convert_reduce_fusion.1
  21.8 0.3 multiply_sine_fusion
  22.1 0.3 subtract_convert_fusion
  22.4 0.2 pad_maximum_fusion
  22.7 1.9 %collective-permute-start.1 = (bf16[128,256]{1,0:T(8,128)(2,1)S(1)}, bf16[128,256]{1,0:T(8,128)(2,1)S(1)}, u32[]{:S(2)}, u32[]{:S(2)}) collective-permute-start(bf16[128,256]{1,0:T(8,128)(2,1)S(1)} %get-tuple-element.32), channel_id=1, source_target_pairs={{0,512},{512,0},{1,513},{513,1},{2,514},{514,2},{3,515},{515,3},{4... | collective-permute-start | bytes 196616 | tf_op jit(solution)/shard_map/ppermute | solution.py:86
  24.6 0.5 fusion.2
  25.1 7.5 %collective-permute-done.1.kb_ref = bf16[128,256]{1,0:T(8,128)(2,1)S(1)} collective-permute-done((bf16[128,256]{1,0:T(8,128)(2,1)S(1)}, bf16[128,256]{1,0:T(8,128)(2,1)S(1)}, u32[]{:S(2)}, u32[]{:S(2)}) %collective-permute-start.1) | collective-permute-done | bytes 65568 | tf_op jit(solution)/shard_map/ppermute | solution.py:86
  32.6 0.0 collective-permute-done.par_ref
  32.6 0.5 fusion
  33.1 1.2 %reshape.92 = bf16[64,4,2048]{2,1,0:T(4,128)(2,1)} reshape(bf16[256,2048]{1,0:T(8,128)(2,1)S(1)} %fusion) | data formatting | bytes 2097152 | tf_op jit(solution)/shard_map/reshape | solution.py:89
  34.3 5.8 %all-to-all-done = bf16[64,4,2048]{2,1,0:T(4,128)(2,1)S(1)} async-done(((bf16[64,4,2048]{2,1,0:T(4,128)(2,1)}), bf16[64,4,2048]{2,1,0:T(4,128)(2,1)S(1)}, u32[]{:S(2)}, u32[]{:S(2)}) %all-to-all-start) | async-done | bytes 1048608 | tf_op jit(solution)/shard_map/all_to_all | solution.py:80
  40.1 10.0 %all-to-all-start.1 = ((bf16[64,4,2048]{2,1,0:T(4,128)(2,1)}), bf16[64,4,2048]{2,1,0:T(4,128)(2,1)}, u32[]{:S(2)}, u32[]{:S(2)}) async-start(bf16[64,4,2048]{2,1,0:T(4,128)(2,1)} %reshape.92), calls=%async_computation.1 | async-start | bytes 2097152 | tf_op jit(solution)/shard_map/all_to_all | solution.py:102
  50.1 0.3 reshape.91.w_ref
  50.4 0.6 kraw.1
  51.0 5.4 %all-gather = bf16[256,256]{1,0:T(8,128)(2,1)S(1)} all-gather(bf16[128,256]{1,0:T(8,128)(2,1)S(1)} %get-tuple-element.16), channel_id=2, replica_groups=mesh['zl'=2,'y'=8,'x'=8,'zh'=4,'c'=2] {'c'}, dimensions={0}, use_global_device_ids=true | all-gather | bytes 196608 | tf_op jit(solution)/shard_map/all_gather | solution.py:98
  56.4 5.4 %all-gather.1 = bf16[128,256]{1,0:T(8,128)(2,1)S(1)} all-gather(bf16[64,256]{1,0:T(8,128)(2,1)S(1)} %get-tuple-element.18), channel_id=3, replica_groups=mesh['zl'=2,'y'=8,'x'=8,'zh'=4,'c'=2] {'zl'}, dimensions={0}, use_global_device_ids=true | all-gather | bytes 98304 | tf_op jit(solution)/shard_map/all_gather | solution.py:101
  61.9 3.4 %collective-permute-start.5 = (bf16[128,2048]{1,0:T(8,128)(2,1)S(1)}, bf16[128,2048]{1,0:T(8,128)(2,1)S(1)}, u32[]{:S(2)}, u32[]{:S(2)}) collective-permute-start(bf16[128,2048]{1,0:T(8,128)(2,1)S(1)} %get-tuple-element.21), channel_id=1, source_target_pairs={{0,512},{512,0},{1,513},{513,1},{2,514},{514,2},{3,515},{515,3},{4... | collective-permute-start | bytes 1572872 | tf_op jit(solution)/shard_map/ppermute | solution.py:108
  65.3 13.4 %collective-permute-start.4 = (bf16[64,512]{1,0:T(8,128)(2,1)S(1)}, bf16[64,512]{1,0:T(8,128)(2,1)S(1)}, u32[]{:S(2)}, u32[]{:S(2)}) collective-permute-start(bf16[64,512]{1,0:T(8,128)(2,1)S(1)} %maximum_select_fusion), channel_id=1, source_target_pairs={{0,4},{2,6},{4,0},{6,2},{1,5},{3,7},{5,1},{7,3},{8,12},{10,14},{12... | collective-permute-start | bytes 196616 | tf_op jit(solution)/shard_map/ppermute | solution.py:110
  78.7 5.8 %collective-permute-start.3 = (bf16[64,512]{1,0:T(8,128)(2,1)S(1)}, bf16[64,512]{1,0:T(8,128)(2,1)S(1)}, u32[]{:S(2)}, u32[]{:S(2)}) collective-permute-start(bf16[64,512]{1,0:T(8,128)(2,1)S(1)} %maximum_select_fusion), channel_id=1, source_target_pairs={{0,2},{2,4},{4,6},{6,0},{1,3},{3,5},{5,7},{7,1},{8,10},{10,12},{12... | collective-permute-start | bytes 196616 | tf_op jit(solution)/shard_map/ppermute | solution.py:110
  84.5 1.9 %collective-permute-start.2 = (bf16[64,512]{1,0:T(8,128)(2,1)S(1)}, bf16[64,512]{1,0:T(8,128)(2,1)S(1)}, u32[]{:S(2)}, u32[]{:S(2)}) collective-permute-start(bf16[64,512]{1,0:T(8,128)(2,1)S(1)} %maximum_select_fusion), channel_id=1, source_target_pairs={{0,6},{2,0},{4,2},{6,4},{1,7},{3,1},{5,3},{7,5},{8,14},{10,8},{12,... | collective-permute-start | bytes 196616 | tf_op jit(solution)/shard_map/ppermute | solution.py:110
  86.4 0.0 all-to-all-done.1
  86.5 2.3 %convert_reduce_fusion = f32[4,2048]{1,0:T(4,128)} fusion(bf16[64,4,2048]{2,1,0:T(4,128)(2,1)} %all-to-all-done.1), kind=kLoop, calls=%fused_computation.2 | loop fusion | flops 1040384 | bytes 1081344 | tf_op jit(solution)/shard_map/reduce_sum | solution.py:114
  88.7 0.0 collective-permute-done.5.add_ref
  88.7 1.1 %grad.1 = bf16[128,2048]{1,0:T(8,128)(2,1)} custom-call(bf16[128,256]{1,0:T(8,128)(2,1)S(1)} %get-tuple-element.31.kb_ref, bf16[256,2048]{1,0:T(8,128)(2,1)S(1)} %reshape.91.w_ref, bf16[128,2048]{1,0:T(8,128)(2,1)S(1)} %collective-permute-done.5.add_ref), custom_call_target="tpu_custom_call" | custom-call | tf_op jit(solution)/shard_map/grad/pallas_call | solution.py:113
  89.8 1.3 %collective-permute-done.4 = bf16[64,512]{1,0:T(8,128)(2,1)S(1)} collective-permute-done((bf16[64,512]{1,0:T(8,128)(2,1)S(1)}, bf16[64,512]{1,0:T(8,128)(2,1)S(1)}, u32[]{:S(2)}, u32[]{:S(2)}) %collective-permute-start.4) | collective-permute-done | bytes 65568 | tf_op jit(solution)/shard_map/ppermute | solution.py:110
  91.1 3.6 %collective-permute-done.3 = bf16[64,512]{1,0:T(8,128)(2,1)S(1)} collective-permute-done((bf16[64,512]{1,0:T(8,128)(2,1)S(1)}, bf16[64,512]{1,0:T(8,128)(2,1)S(1)}, u32[]{:S(2)}, u32[]{:S(2)}) %collective-permute-start.3) | collective-permute-done | bytes 65568 | tf_op jit(solution)/shard_map/ppermute | solution.py:110
  94.7 0.0 collective-permute-done.2
  94.8 0.2 subtract_convert_fusion.1
  95.0 0.1 pad_maximum_fusion.1
  95.1 3.9 %all_gather.19 = bf16[128,512]{1,0:T(8,128)(2,1)S(1)} all-gather(bf16[64,512]{1,0:T(8,128)(2,1)S(1)} %bitcast.18), channel_id=1, replica_groups=mesh['zl'=2,'y'=8,'x'=8,'zh'=4,'c'=2] {'c'}, dimensions={0}, use_global_device_ids=true | all-gather | bytes 196608 | tf_op jit(solution)/shard_map/all_gather | solution.py:122
  99.0 0.7 copy.14
  (11 shorter events, 0.2 us)
Async XLA Ops:
  0.6 16.0 %copy-start = (bf16[128,2048]{1,0:T(8,128)(2,1)S(1)}, bf16[128,2048]{1,0:T(8,128)(2,1)}, u32[]{:S(2)}) copy-start(bf16[128,2048]{1,0:T(8,128)(2,1)} %tok_ref.1) | copy-start | bytes 1572868
  0.6 0.8 copy-start.1
  1.4 20.1 %copy-start.2 = (bf16[128,512]{1,0:T(8,128)(2,1)S(1)}, bf16[128,512]{1,0:T(8,128)(2,1)}, u32[]{:S(2)}) copy-start(bf16[128,512]{1,0:T(8,128)(2,1)} %param.7) | copy-start | bytes 393220
  1.4 20.2 %copy-start.3 = (s32[1,128]{1,0:T(1,128)S(1)}, s32[1,128]{1,0:T(1,128)}, u32[]{:S(2)}) copy-start(s32[1,128]{1,0:T(1,128)} %param.5) | copy-start | bytes 1540
  2.5 37.6 %all-to-all-start = ((bf16[64,4,2048]{2,1,0:T(4,128)(2,1)}), bf16[64,4,2048]{2,1,0:T(4,128)(2,1)S(1)}, u32[]{:S(2)}, u32[]{:S(2)}) async-start(bf16[64,4,2048]{2,1,0:T(4,128)(2,1)} %spread.1), calls=%async_computation | async-start | bytes 2097152 | tf_op jit(solution)/shard_map/all_to_all | solution.py:80
  16.6 16.0 %collective-permute-start = (bf16[128,2048]{1,0:T(8,128)(2,1)S(1)}, bf16[128,2048]{1,0:T(8,128)(2,1)S(1)}, u32[]{:S(2)}, u32[]{:S(2)}) collective-permute-start(bf16[128,2048]{1,0:T(8,128)(2,1)S(1)} %copy-done), channel_id=1, source_target_pairs={{0,512},{512,0},{1,513},{513,1},{2,514},{514,2},{3,515},{515,3},{4... | collective-permute-start | bytes 1572872 | tf_op jit(solution)/shard_map/ppermute | solution.py:81
  22.7 9.9 %collective-permute-start.1 = (bf16[128,256]{1,0:T(8,128)(2,1)S(1)}, bf16[128,256]{1,0:T(8,128)(2,1)S(1)}, u32[]{:S(2)}, u32[]{:S(2)}) collective-permute-start(bf16[128,256]{1,0:T(8,128)(2,1)S(1)} %get-tuple-element.32), channel_id=1, source_target_pairs={{0,512},{512,0},{1,513},{513,1},{2,514},{514,2},{3,515},{515,3},{4... | collective-permute-start | bytes 196616 | tf_op jit(solution)/shard_map/ppermute | solution.py:86
  40.1 46.4 %all-to-all-start.1 = ((bf16[64,4,2048]{2,1,0:T(4,128)(2,1)}), bf16[64,4,2048]{2,1,0:T(4,128)(2,1)}, u32[]{:S(2)}, u32[]{:S(2)}) async-start(bf16[64,4,2048]{2,1,0:T(4,128)(2,1)} %reshape.92), calls=%async_computation.1 | async-start | bytes 2097152 | tf_op jit(solution)/shard_map/all_to_all | solution.py:102
  61.9 26.9 %collective-permute-start.5 = (bf16[128,2048]{1,0:T(8,128)(2,1)S(1)}, bf16[128,2048]{1,0:T(8,128)(2,1)S(1)}, u32[]{:S(2)}, u32[]{:S(2)}) collective-permute-start(bf16[128,2048]{1,0:T(8,128)(2,1)S(1)} %get-tuple-element.21), channel_id=1, source_target_pairs={{0,512},{512,0},{1,513},{513,1},{2,514},{514,2},{3,515},{515,3},{4... | collective-permute-start | bytes 1572872 | tf_op jit(solution)/shard_map/ppermute | solution.py:108
  65.3 25.8 %collective-permute-start.4 = (bf16[64,512]{1,0:T(8,128)(2,1)S(1)}, bf16[64,512]{1,0:T(8,128)(2,1)S(1)}, u32[]{:S(2)}, u32[]{:S(2)}) collective-permute-start(bf16[64,512]{1,0:T(8,128)(2,1)S(1)} %maximum_select_fusion), channel_id=1, source_target_pairs={{0,4},{2,6},{4,0},{6,2},{1,5},{3,7},{5,1},{7,3},{8,12},{10,14},{12... | collective-permute-start | bytes 196616 | tf_op jit(solution)/shard_map/ppermute | solution.py:110
  78.7 16.0 %collective-permute-start.3 = (bf16[64,512]{1,0:T(8,128)(2,1)S(1)}, bf16[64,512]{1,0:T(8,128)(2,1)S(1)}, u32[]{:S(2)}, u32[]{:S(2)}) collective-permute-start(bf16[64,512]{1,0:T(8,128)(2,1)S(1)} %maximum_select_fusion), channel_id=1, source_target_pairs={{0,2},{2,4},{4,6},{6,0},{1,3},{3,5},{5,7},{7,1},{8,10},{10,12},{12... | collective-permute-start | bytes 196616 | tf_op jit(solution)/shard_map/ppermute | solution.py:110
  84.5 10.2 %collective-permute-start.2 = (bf16[64,512]{1,0:T(8,128)(2,1)S(1)}, bf16[64,512]{1,0:T(8,128)(2,1)S(1)}, u32[]{:S(2)}, u32[]{:S(2)}) collective-permute-start(bf16[64,512]{1,0:T(8,128)(2,1)S(1)} %maximum_select_fusion), channel_id=1, source_target_pairs={{0,6},{2,0},{4,2},{6,4},{1,7},{3,1},{5,3},{7,5},{8,14},{10,8},{12,... | collective-permute-start | bytes 196616 | tf_op jit(solution)/shard_map/ppermute | solution.py:110

commit v12 on v11

--- a/solution.py
+++ b/solution.py
@@ -104,7 +104,6 @@
     total_b = jnp.where(
         zl == 0, jnp.concatenate([own, from_z[1]], 1), jnp.concatenate([from_z[0], own], 1)
     )
-    total_b, g_send = lax.optimization_barrier((total_b, g_send))
     g_par = lax.ppermute(g_send, "zl", SWAP)
     one, three, two = (
         lax.ppermute(total_b, "zh", [(i, (i + step) % 4) for i in range(4)])

time: 100 us -> 102 us (1.020)
  waiting for transfers between devices: 18.2 us -> 14 us
  starting transfers between devices: 55.4 us -> 58.8 us
  blocking collectives: 14.7 us -> 16.8 us
    ppermute x3, waiting for transfers between devices: 4.87 us -> 0.65 us  [body(): lax.ppermute(total_b, 'zh', [(i, (i + step) % 4) for i in range(4)])]
    ppermute x1, starting transfers between devices: 3.4 us -> 6.84 us  [body(): g_par = lax.ppermute(g_send, 'zl', SWAP)]
    all_gather x1, blocking collectives: 3.87 us -> 5.82 us  [body(): keys = lax.all_gather(keys, 'c', axis=0, tiled=True)]
    all_gather x1, blocking collectives: 5.4 us -> 7.18 us  [body(): from_z = lax.all_gather(to_z, 'zl')]
    all_gather x1, blocking collectives: 5.44 us -> 3.83 us  [body(): from_c = lax.all_gather(to_c, 'c')]
  transfers between devices with their start and end apart: 8 -> 8, of which waited for: 4 -> 3; matrix products, arithmetic and copies ran while one was open for 6% -> 6% of each run, Pallas kernels for 2% -> 2%
where the time goes in v12:
time: 102 us; the launch traced here: 101 us
  starting transfers between devices  58.8 us (58%)
  blocking collectives  16.8 us (16%)
  waiting for transfers between devices  14 us (14%)
  other arithmetic  3.61 us (4%)
  local copies, waits for them, and re-layouts  3.11 us (3%)
  Pallas kernels  2.85 us (3%)
    ppermute x3, starting transfers between devices, body(): lax.ppermute(total_b, 'zh', [(i, (i + step) % 4) for i in range(4)])  21.1 us
    all_to_all x1, starting transfers between devices, body(): gathered = lax.all_to_all(spread, ('y', 'x'), 0, 0)  14 us
    all_to_all x1, starting transfers between devices, body(): scattered = lax.all_to_all(partial, ('y', 'x'), 0, 0)  9.98 us
    ppermute x1, waiting for transfers between devices, body(): kb_p = lax.ppermute(jnp.where(zl == 0, right, left), 'zl', SWAP)  7.54 us
    all_gather x1, blocking collectives, body(): from_z = lax.all_gather(to_z, 'zl')  7.18 us
    ppermute x1, starting transfers between devices, body(): g_par = lax.ppermute(g_send, 'zl', SWAP)  6.84 us
    all_gather x1, blocking collectives, body(): keys = lax.all_gather(keys, 'c', axis=0, tiled=True)  5.82 us
    all_to_all x1, waiting for transfers between devices, body(): gathered = lax.all_to_all(spread, ('y', 'x'), 0, 0)  5.81 us
  transfers between devices with their start and end apart: 8, of which 3 were waited for; matrix products, arithmetic and copies ran while one was open for 6% of the time, Pallas kernels for 2%

profile of v12, /device:TPU:1, one launch (start us, length us, event | category | flops | bytes accessed | tf_op | source)
XLA Modules:
  0.0 101.0 jit_solution(18024742533150475943)
XLA Ops:
  0.6 0.0 copy-start
  0.6 0.0 copy-start.1
  0.7 0.8 copy-done.1
  1.4 0.0 copy-start.2
  1.4 0.0 copy-start.3
  1.4 1.1 %spread.1 = bf16[64,4,2048]{2,1,0:T(4,128)(2,1)} custom-call(bf16[4,2048]{1,0:T(4,128)(2,1)S(1)} %copy-done.1), custom_call_target="tpu_custom_call" | custom-call | tf_op jit(solution)/shard_map/spread/pallas_call | solution.py:79
  2.5 14.0 %all-to-all-start = ((bf16[64,4,2048]{2,1,0:T(4,128)(2,1)}), bf16[64,4,2048]{2,1,0:T(4,128)(2,1)S(1)}, u32[]{:S(2)}, u32[]{:S(2)}) async-start(bf16[64,4,2048]{2,1,0:T(4,128)(2,1)} %spread.1), calls=%async_computation | async-start | bytes 2097152 | tf_op jit(solution)/shard_map/all_to_all | solution.py:80
  16.6 0.0 copy-done
  16.6 4.9 %collective-permute-start = (bf16[128,2048]{1,0:T(8,128)(2,1)S(1)}, bf16[128,2048]{1,0:T(8,128)(2,1)S(1)}, u32[]{:S(2)}, u32[]{:S(2)}) collective-permute-start(bf16[128,2048]{1,0:T(8,128)(2,1)S(1)} %copy-done), channel_id=1, source_target_pairs={{0,512},{512,0},{1,513},{513,1},{2,514},{514,2},{3,515},{515,3},{4... | collective-permute-start | bytes 1572872 | tf_op jit(solution)/shard_map/ppermute | solution.py:81
  21.5 0.0 copy-done.2
  21.5 0.1 reshape.95
  21.6 0.0 copy-done.3
  21.6 0.2 convert_reduce_fusion.1
  21.8 0.3 multiply_sine_fusion
  22.1 0.3 subtract_convert_fusion
  22.4 0.2 pad_maximum_fusion
  22.7 1.9 %collective-permute-start.1 = (bf16[128,256]{1,0:T(8,128)(2,1)S(1)}, bf16[128,256]{1,0:T(8,128)(2,1)S(1)}, u32[]{:S(2)}, u32[]{:S(2)}) collective-permute-start(bf16[128,256]{1,0:T(8,128)(2,1)S(1)} %get-tuple-element.28), channel_id=1, source_target_pairs={{0,512},{512,0},{1,513},{513,1},{2,514},{514,2},{3,515},{515,3},{4... | collective-permute-start | bytes 196616 | tf_op jit(solution)/shard_map/ppermute | solution.py:86
  24.6 0.5 fusion.2
  25.1 7.5 %collective-permute-done.1.kb_ref = bf16[128,256]{1,0:T(8,128)(2,1)S(1)} collective-permute-done((bf16[128,256]{1,0:T(8,128)(2,1)S(1)}, bf16[128,256]{1,0:T(8,128)(2,1)S(1)}, u32[]{:S(2)}, u32[]{:S(2)}) %collective-permute-start.1) | collective-permute-done | bytes 65568 | tf_op jit(solution)/shard_map/ppermute | solution.py:86
  32.6 0.0 collective-permute-done.par_ref
  32.6 0.5 fusion
  33.1 1.2 %reshape.92 = bf16[64,4,2048]{2,1,0:T(4,128)(2,1)} reshape(bf16[256,2048]{1,0:T(8,128)(2,1)S(1)} %fusion) | data formatting | bytes 2097152 | tf_op jit(solution)/shard_map/reshape | solution.py:89
  34.3 5.8 %all-to-all-done = bf16[64,4,2048]{2,1,0:T(4,128)(2,1)S(1)} async-done(((bf16[64,4,2048]{2,1,0:T(4,128)(2,1)}), bf16[64,4,2048]{2,1,0:T(4,128)(2,1)S(1)}, u32[]{:S(2)}, u32[]{:S(2)}) %all-to-all-start) | async-done | bytes 1048608 | tf_op jit(solution)/shard_map/all_to_all | solution.py:80
  40.1 10.0 %all-to-all-start.1 = ((bf16[64,4,2048]{2,1,0:T(4,128)(2,1)}), bf16[64,4,2048]{2,1,0:T(4,128)(2,1)}, u32[]{:S(2)}, u32[]{:S(2)}) async-start(bf16[64,4,2048]{2,1,0:T(4,128)(2,1)} %reshape.92), calls=%async_computation.1 | async-start | bytes 2097152 | tf_op jit(solution)/shard_map/all_to_all | solution.py:102
  50.1 0.3 reshape.91.w_ref
  50.4 0.6 kraw.1
  51.0 6.8 %collective-permute-start.5 = (bf16[128,2048]{1,0:T(8,128)(2,1)S(1)}, bf16[128,2048]{1,0:T(8,128)(2,1)S(1)}, u32[]{:S(2)}, u32[]{:S(2)}) collective-permute-start(bf16[128,2048]{1,0:T(8,128)(2,1)S(1)} %get-tuple-element.17), channel_id=1, source_target_pairs={{0,512},{512,0},{1,513},{513,1},{2,514},{514,2},{3,515},{515,3},{4... | collective-permute-start | bytes 1572872 | tf_op jit(solution)/shard_map/ppermute | solution.py:107
  57.9 3.8 %all-gather = bf16[256,256]{1,0:T(8,128)(2,1)S(1)} all-gather(bf16[128,256]{1,0:T(8,128)(2,1)S(1)} %get-tuple-element.14), channel_id=2, replica_groups=mesh['zl'=2,'y'=8,'x'=8,'zh'=4,'c'=2] {'c'}, dimensions={0}, use_global_device_ids=true | all-gather | bytes 196608 | tf_op jit(solution)/shard_map/all_gather | solution.py:98
  61.7 7.2 %all-gather.1 = bf16[128,256]{1,0:T(8,128)(2,1)S(1)} all-gather(bf16[64,256]{1,0:T(8,128)(2,1)S(1)} %get-tuple-element.16), channel_id=3, replica_groups=mesh['zl'=2,'y'=8,'x'=8,'zh'=4,'c'=2] {'zl'}, dimensions={0}, use_global_device_ids=true | all-gather | bytes 98304 | tf_op jit(solution)/shard_map/all_gather | solution.py:101
  68.9 13.4 %collective-permute-start.4 = (bf16[64,512]{1,0:T(8,128)(2,1)S(1)}, bf16[64,512]{1,0:T(8,128)(2,1)S(1)}, u32[]{:S(2)}, u32[]{:S(2)}) collective-permute-start(bf16[64,512]{1,0:T(8,128)(2,1)S(1)} %maximum_select_fusion), channel_id=1, source_target_pairs={{0,4},{2,6},{4,0},{6,2},{1,5},{3,7},{5,1},{7,3},{8,12},{10,14},{12... | collective-permute-start | bytes 196616 | tf_op jit(solution)/shard_map/ppermute | solution.py:109
  82.3 5.8 %collective-permute-start.3 = (bf16[64,512]{1,0:T(8,128)(2,1)S(1)}, bf16[64,512]{1,0:T(8,128)(2,1)S(1)}, u32[]{:S(2)}, u32[]{:S(2)}) collective-permute-start(bf16[64,512]{1,0:T(8,128)(2,1)S(1)} %maximum_select_fusion), channel_id=1, source_target_pairs={{0,2},{2,4},{4,6},{6,0},{1,3},{3,5},{5,7},{7,1},{8,10},{10,12},{12... | collective-permute-start | bytes 196616 | tf_op jit(solution)/shard_map/ppermute | solution.py:109
  88.1 1.9 %collective-permute-start.2 = (bf16[64,512]{1,0:T(8,128)(2,1)S(1)}, bf16[64,512]{1,0:T(8,128)(2,1)S(1)}, u32[]{:S(2)}, u32[]{:S(2)}) collective-permute-start(bf16[64,512]{1,0:T(8,128)(2,1)S(1)} %maximum_select_fusion), channel_id=1, source_target_pairs={{0,6},{2,0},{4,2},{6,4},{1,7},{3,1},{5,3},{7,5},{8,14},{10,8},{12,... | collective-permute-start | bytes 196616 | tf_op jit(solution)/shard_map/ppermute | solution.py:109
  90.0 0.0 all-to-all-done.1
  90.1 2.3 %convert_reduce_fusion = f32[4,2048]{1,0:T(4,128)} fusion(bf16[64,4,2048]{2,1,0:T(4,128)(2,1)} %all-to-all-done.1), kind=kLoop, calls=%fused_computation.2 | loop fusion | flops 1040384 | bytes 1081344 | tf_op jit(solution)/shard_map/reduce_sum | solution.py:113
  92.3 0.0 collective-permute-done.5.add_ref
  92.3 1.1 %grad.1 = bf16[128,2048]{1,0:T(8,128)(2,1)} custom-call(bf16[128,256]{1,0:T(8,128)(2,1)S(1)} %get-tuple-element.27.kb_ref, bf16[256,2048]{1,0:T(8,128)(2,1)S(1)} %reshape.91.w_ref, bf16[128,2048]{1,0:T(8,128)(2,1)S(1)} %collective-permute-done.5.add_ref), custom_call_target="tpu_custom_call" | custom-call | tf_op jit(solution)/shard_map/grad/pallas_call | solution.py:112
  93.5 0.0 collective-permute-done.4
  93.5 0.0 collective-permute-done.3
  93.5 0.6 collective-permute-done.2
  94.2 0.2 subtract_convert_fusion.1
  94.4 0.1 pad_maximum_fusion.1
  94.5 5.8 %all_gather.19 = bf16[128,512]{1,0:T(8,128)(2,1)S(1)} all-gather(bf16[64,512]{1,0:T(8,128)(2,1)S(1)} %bitcast.18), channel_id=1, replica_groups=mesh['zl'=2,'y'=8,'x'=8,'zh'=4,'c'=2] {'c'}, dimensions={0}, use_global_device_ids=true | all-gather | bytes 196608 | tf_op jit(solution)/shard_map/all_gather | solution.py:121
  100.3 0.7 copy.14
  (11 shorter events, 0.2 us)
Async XLA Ops:
  0.6 16.0 %copy-start = (bf16[128,2048]{1,0:T(8,128)(2,1)S(1)}, bf16[128,2048]{1,0:T(8,128)(2,1)}, u32[]{:S(2)}) copy-start(bf16[128,2048]{1,0:T(8,128)(2,1)} %tok_ref.1) | copy-start | bytes 1572868
  0.6 0.8 copy-start.1
  1.4 20.1 %copy-start.2 = (bf16[128,512]{1,0:T(8,128)(2,1)S(1)}, bf16[128,512]{1,0:T(8,128)(2,1)}, u32[]{:S(2)}) copy-start(bf16[128,512]{1,0:T(8,128)(2,1)} %param.7) | copy-start | bytes 393220
  1.4 20.2 %copy-start.3 = (s32[1,128]{1,0:T(1,128)S(1)}, s32[1,128]{1,0:T(1,128)}, u32[]{:S(2)}) copy-start(s32[1,128]{1,0:T(1,128)} %param.5) | copy-start | bytes 1540
  2.5 37.6 %all-to-all-start = ((bf16[64,4,2048]{2,1,0:T(4,128)(2,1)}), bf16[64,4,2048]{2,1,0:T(4,128)(2,1)S(1)}, u32[]{:S(2)}, u32[]{:S(2)}) async-start(bf16[64,4,2048]{2,1,0:T(4,128)(2,1)} %spread.1), calls=%async_computation | async-start | bytes 2097152 | tf_op jit(solution)/shard_map/all_to_all | solution.py:80
  16.6 16.0 %collective-permute-start = (bf16[128,2048]{1,0:T(8,128)(2,1)S(1)}, bf16[128,2048]{1,0:T(8,128)(2,1)S(1)}, u32[]{:S(2)}, u32[]{:S(2)}) collective-permute-start(bf16[128,2048]{1,0:T(8,128)(2,1)S(1)} %copy-done), channel_id=1, source_target_pairs={{0,512},{512,0},{1,513},{513,1},{2,514},{514,2},{3,515},{515,3},{4... | collective-permute-start | bytes 1572872 | tf_op jit(solution)/shard_map/ppermute | solution.py:81
  22.7 9.9 %collective-permute-start.1 = (bf16[128,256]{1,0:T(8,128)(2,1)S(1)}, bf16[128,256]{1,0:T(8,128)(2,1)S(1)}, u32[]{:S(2)}, u32[]{:S(2)}) collective-permute-start(bf16[128,256]{1,0:T(8,128)(2,1)S(1)} %get-tuple-element.28), channel_id=1, source_target_pairs={{0,512},{512,0},{1,513},{513,1},{2,514},{514,2},{3,515},{515,3},{4... | collective-permute-start | bytes 196616 | tf_op jit(solution)/shard_map/ppermute | solution.py:86
  40.1 50.0 %all-to-all-start.1 = ((bf16[64,4,2048]{2,1,0:T(4,128)(2,1)}), bf16[64,4,2048]{2,1,0:T(4,128)(2,1)}, u32[]{:S(2)}, u32[]{:S(2)}) async-start(bf16[64,4,2048]{2,1,0:T(4,128)(2,1)} %reshape.92), calls=%async_computation.1 | async-start | bytes 2097152 | tf_op jit(solution)/shard_map/all_to_all | solution.py:102
  51.0 41.3 %collective-permute-start.5 = (bf16[128,2048]{1,0:T(8,128)(2,1)S(1)}, bf16[128,2048]{1,0:T(8,128)(2,1)S(1)}, u32[]{:S(2)}, u32[]{:S(2)}) collective-permute-start(bf16[128,2048]{1,0:T(8,128)(2,1)S(1)} %get-tuple-element.17), channel_id=1, source_target_pairs={{0,512},{512,0},{1,513},{513,1},{2,514},{514,2},{3,515},{515,3},{4... | collective-permute-start | bytes 1572872 | tf_op jit(solution)/shard_map/ppermute | solution.py:107
  68.9 24.6 %collective-permute-start.4 = (bf16[64,512]{1,0:T(8,128)(2,1)S(1)}, bf16[64,512]{1,0:T(8,128)(2,1)S(1)}, u32[]{:S(2)}, u32[]{:S(2)}) collective-permute-start(bf16[64,512]{1,0:T(8,128)(2,1)S(1)} %maximum_select_fusion), channel_id=1, source_target_pairs={{0,4},{2,6},{4,0},{6,2},{1,5},{3,7},{5,1},{7,3},{8,12},{10,14},{12... | collective-permute-start | bytes 196616 | tf_op jit(solution)/shard_map/ppermute | solution.py:109
  82.3 11.2 %collective-permute-start.3 = (bf16[64,512]{1,0:T(8,128)(2,1)S(1)}, bf16[64,512]{1,0:T(8,128)(2,1)S(1)}, u32[]{:S(2)}, u32[]{:S(2)}) collective-permute-start(bf16[64,512]{1,0:T(8,128)(2,1)S(1)} %maximum_select_fusion), channel_id=1, source_target_pairs={{0,2},{2,4},{4,6},{6,0},{1,3},{3,5},{5,7},{7,1},{8,10},{10,12},{12... | collective-permute-start | bytes 196616 | tf_op jit(solution)/shard_map/ppermute | solution.py:109
  88.1 6.0 %collective-permute-start.2 = (bf16[64,512]{1,0:T(8,128)(2,1)S(1)}, bf16[64,512]{1,0:T(8,128)(2,1)S(1)}, u32[]{:S(2)}, u32[]{:S(2)}) collective-permute-start(bf16[64,512]{1,0:T(8,128)(2,1)S(1)} %maximum_select_fusion), channel_id=1, source_target_pairs={{0,6},{2,0},{4,2},{6,4},{1,7},{3,1},{5,3},{7,5},{8,14},{10,8},{12,... | collective-permute-start | bytes 196616 | tf_op jit(solution)/shard_map/ppermute | solution.py:109

commit v13 on v12

--- a/solution.py
+++ b/solution.py
@@ -38,14 +38,16 @@
     out_ref[...] = jnp.broadcast_to(w_ref[...][None], out_ref.shape)
 
 
-def kraw_kernel(tok_ref, par_ref, kb_ref, w_ref, keep_ref, send_ref, grad_ref):
+def kraw_kernel(tok_ref, par_ref, kb_ref, w_ref, keep_ref, send_ref, a_ref, b_ref):
     mine = pl.multiple_of(lax.axis_index("c") * 64, 64)
     other = pl.multiple_of(64 - mine, 64)
     halves = [ref[pl.ds(at, 64), :] for at in (mine, other) for ref in (tok_ref, par_ref)]
     out = dot(jnp.concatenate(halves, axis=0), w_ref[...], 1, 1)
     keep_ref[...] = out[:128]
     send_ref[...] = out[128:].astype(jnp.bfloat16)
-    grad_ref[...] = dot(kb_ref[...], w_ref[...], 1, 0).astype(jnp.bfloat16)
+    grad = dot(kb_ref[...], w_ref[...], 1, 0).astype(jnp.bfloat16)
+    a_ref[...] = grad[:, :1024]
+    b_ref[...] = grad[:, 1024:]
 
 
 def merge_kernel(keep_ref, c_ref, own_ref, far_ref):
@@ -55,9 +57,10 @@
     far_ref[...] = out[64:]
 
 
-def grad_kernel(kb_ref, w_ref, add_ref, out_ref):
-    out = dot(kb_ref[...], w_ref[...], 1, 0) + add_ref[...].astype(jnp.float32)
-    out_ref[...] = out.astype(jnp.bfloat16)
+def grad_kernel(kb_ref, w_ref, a_ref, b_ref, out_ref):
+    out = dot(kb_ref[...], w_ref[...], 1, 0)
+    out_ref[:, :1024] = (out[:, :1024] + a_ref[...].astype(jnp.float32)).astype(jnp.bfloat16)
+    out_ref[:, 1024:] = (out[:, 1024:] + b_ref[...].astype(jnp.float32)).astype(jnp.bfloat16)
 
 
 def whole(kernel, outs, n_in, name):
@@ -89,9 +92,9 @@
     partial = (dot(kb, tokens, 0, 0) + dot(kb_p, tok_p, 0, 0)).astype(bf16).reshape(64, 4, 2048)
 
     weights = gathered.reshape(256, 2048)
-    keep, to_c, g_send = whole(
+    keep, to_c, a_send, b_send = whole(
         kraw_kernel,
-        (shape((128, 256), f32), shape((128, 256), bf16), shape((128, 2048), bf16)),
+        (shape((128, 256), f32), shape((128, 256), bf16)) + (shape((128, 1024), bf16),) * 2,
         4,
         "kraw",
     )(tokens, tok_p, kb_p, weights)
@@ -104,15 +107,15 @@
     total_b = jnp.where(
         zl == 0, jnp.concatenate([own, from_z[1]], 1), jnp.concatenate([from_z[0], own], 1)
     )
-    g_par = lax.ppermute(g_send, "zl", SWAP)
+    total_b, a_send, b_send = lax.optimization_barrier((total_b, a_send, b_send))
+    a_par, b_par = lax.ppermute(a_send, "zl", SWAP), lax.ppermute(b_send, "zl", SWAP)
     one, three, two = (
         lax.ppermute(total_b, "zh", [(i, (i + step) % 4) for i in range(4)])
         for step in (1, 3, 2)
     )
-    grad_tokens = whole(grad_kernel, shape((128, 2048), bf16), 3, "grad")(kb, weights, g_par)
     grad_key_weight = jnp.sum(scattered.astype(f32), axis=0)
-    three, one, two, grad_tokens, grad_key_weight = lax.optimization_barrier(
-        (three, one, two, grad_tokens, grad_key_weight)
+    three, one, two, a_par, grad_key_weight = lax.optimization_barrier(
+        (three, one, two, a_par, grad_key_weight)
     )
     total = (three.astype(f32) + one.astype(f32)) + (two.astype(f32) + total_b.astype(f32))
     own_cos = lax.dynamic_slice_in_dim(cosine, core * 64, 64, 0)
@@ -120,6 +123,7 @@
     keys = rotate(total, own_cos, own_sin, 1.0).astype(bf16)
     keys = lax.all_gather(keys, "c", axis=0, tiled=True)
 
+    grad_tokens = whole(grad_kernel, shape((128, 2048), bf16), 4, "grad")(kb, weights, a_par, b_par)
     return keys, grad_tokens, grad_key_weight
 
 

time: 102 us -> 98.8 us (0.969)
  blocking collectives: 16.8 us -> 15.3 us
  starting transfers between devices: 58.8 us -> 57.3 us
    all_gather x1, blocking collectives: 7.18 us -> 5.41 us  [body(): from_z = lax.all_gather(to_z, 'zl')]
    all_gather x1, blocking collectives: 3.83 us -> 5.43 us  [body(): from_c = lax.all_gather(to_c, 'c')]
    ppermute x1 -> x2, starting transfers between devices: 6.84 us -> 5.32 us  [the longest x1 3.4 us: body(): lax.ppermute(a_send, 'zl', SWAP)]
    all_gather x1, blocking collectives: 5.82 us -> 4.48 us  [body(): keys = lax.all_gather(keys, 'c', axis=0, tiled=True)]
  transfers between devices with their start and end apart: 8 -> 9, of which waited for: 3 -> 3; matrix products, arithmetic and copies ran while one was open for 6% -> 6% of each run, Pallas kernels for 2% -> 1%
where the time goes in v13:
time: 98.8 us; the launch traced here: 97.8 us
  starting transfers between devices  57.3 us (58%)
  blocking collectives  15.3 us (15%)
  waiting for transfers between devices  13.8 us (14%)
  other arithmetic  3.61 us (4%)
  local copies, waits for them, and re-layouts  3.12 us (3%)
  Pallas kernels  2.87 us (3%)
    ppermute x3, starting transfers between devices, body(): lax.ppermute(total_b, 'zh', [(i, (i + step) % 4) for i in range(4)])  21.1 us
    all_to_all x1, starting transfers between devices, body(): gathered = lax.all_to_all(spread, ('y', 'x'), 0, 0)  14 us
    all_to_all x1, starting transfers between devices, body(): scattered = lax.all_to_all(partial, ('y', 'x'), 0, 0)  9.98 us
    ppermute x1, waiting for transfers between devices, body(): kb_p = lax.ppermute(jnp.where(zl == 0, right, left), 'zl', SWAP)  7.54 us
    all_to_all x1, waiting for transfers between devices, body(): gathered = lax.all_to_all(spread, ('y', 'x'), 0, 0)  5.8 us
    all_gather x1, blocking collectives, body(): from_c = lax.all_gather(to_c, 'c')  5.43 us
    all_gather x1, blocking collectives, body(): from_z = lax.all_gather(to_z, 'zl')  5.41 us
    ppermute x1, starting transfers between devices, body(): tok_p = lax.ppermute(tokens, 'zl', SWAP)  4.91 us
  transfers between devices with their start and end apart: 9, of which 3 were waited for; matrix products, arithmetic and copies ran while one was open for 6% of the time, Pallas kernels for 1%

profile of v13, /device:TPU:1, one launch (start us, length us, event | category | flops | bytes accessed | tf_op | source)
XLA Modules:
  0.0 97.8 jit_solution(13580342095744930669)
XLA Ops:
  0.6 0.0 copy-start
  0.6 0.0 copy-start.1
  0.7 0.8 copy-done.1
  1.4 0.0 copy-start.2
  1.4 0.0 copy-start.3
  1.4 1.1 %spread.1 = bf16[64,4,2048]{2,1,0:T(4,128)(2,1)} custom-call(bf16[4,2048]{1,0:T(4,128)(2,1)S(1)} %copy-done.1), custom_call_target="tpu_custom_call" | custom-call | tf_op jit(solution)/shard_map/spread/pallas_call | solution.py:82
  2.5 14.0 %all-to-all-start = ((bf16[64,4,2048]{2,1,0:T(4,128)(2,1)}), bf16[64,4,2048]{2,1,0:T(4,128)(2,1)S(1)}, u32[]{:S(2)}, u32[]{:S(2)}) async-start(bf16[64,4,2048]{2,1,0:T(4,128)(2,1)} %spread.1), calls=%async_computation | async-start | bytes 2097152 | tf_op jit(solution)/shard_map/all_to_all | solution.py:83
  16.6 0.0 copy-done
  16.6 4.9 %collective-permute-start = (bf16[128,2048]{1,0:T(8,128)(2,1)S(1)}, bf16[128,2048]{1,0:T(8,128)(2,1)S(1)}, u32[]{:S(2)}, u32[]{:S(2)}) collective-permute-start(bf16[128,2048]{1,0:T(8,128)(2,1)S(1)} %copy-done), channel_id=1, source_target_pairs={{0,512},{512,0},{1,513},{513,1},{2,514},{514,2},{3,515},{515,3},{4... | collective-permute-start | bytes 1572872 | tf_op jit(solution)/shard_map/ppermute | solution.py:84
  21.5 0.0 copy-done.2
  21.5 0.1 reshape.95
  21.6 0.0 copy-done.3
  21.6 0.2 convert_reduce_fusion.1
  21.8 0.3 multiply_sine_fusion
  22.2 0.3 subtract_convert_fusion
  22.4 0.2 pad_maximum_fusion
  22.7 1.9 %collective-permute-start.1 = (bf16[128,256]{1,0:T(8,128)(2,1)S(1)}, bf16[128,256]{1,0:T(8,128)(2,1)S(1)}, u32[]{:S(2)}, u32[]{:S(2)}) collective-permute-start(bf16[128,256]{1,0:T(8,128)(2,1)S(1)} %get-tuple-element.36), channel_id=1, source_target_pairs={{0,512},{512,0},{1,513},{513,1},{2,514},{514,2},{3,515},{515,3},{4... | collective-permute-start | bytes 196616 | tf_op jit(solution)/shard_map/ppermute | solution.py:89
  24.6 0.5 fusion.2
  25.1 7.5 %collective-permute-done.1.kb_ref = bf16[128,256]{1,0:T(8,128)(2,1)S(1)} collective-permute-done((bf16[128,256]{1,0:T(8,128)(2,1)S(1)}, bf16[128,256]{1,0:T(8,128)(2,1)S(1)}, u32[]{:S(2)}, u32[]{:S(2)}) %collective-permute-start.1) | collective-permute-done | bytes 65568 | tf_op jit(solution)/shard_map/ppermute | solution.py:89
  32.6 0.0 collective-permute-done.par_ref
  32.6 0.5 fusion
  33.1 1.2 %reshape.92 = bf16[64,4,2048]{2,1,0:T(4,128)(2,1)} reshape(bf16[256,2048]{1,0:T(8,128)(2,1)S(1)} %fusion) | data formatting | bytes 2097152 | tf_op jit(solution)/shard_map/reshape | solution.py:92
  34.3 5.8 %all-to-all-done = bf16[64,4,2048]{2,1,0:T(4,128)(2,1)S(1)} async-done(((bf16[64,4,2048]{2,1,0:T(4,128)(2,1)}), bf16[64,4,2048]{2,1,0:T(4,128)(2,1)S(1)}, u32[]{:S(2)}, u32[]{:S(2)}) %all-to-all-start) | async-done | bytes 1048608 | tf_op jit(solution)/shard_map/all_to_all | solution.py:83
  40.1 10.0 %all-to-all-start.1 = ((bf16[64,4,2048]{2,1,0:T(4,128)(2,1)}), bf16[64,4,2048]{2,1,0:T(4,128)(2,1)}, u32[]{:S(2)}, u32[]{:S(2)}) async-start(bf16[64,4,2048]{2,1,0:T(4,128)(2,1)} %reshape.92), calls=%async_computation.1 | async-start | bytes 2097152 | tf_op jit(solution)/shard_map/all_to_all | solution.py:105
  50.1 0.3 reshape.91.w_ref
  50.4 0.6 kraw.1
  51.0 5.4 %all-gather = bf16[256,256]{1,0:T(8,128)(2,1)S(1)} all-gather(bf16[128,256]{1,0:T(8,128)(2,1)S(1)} %get-tuple-element.18), channel_id=2, replica_groups=mesh['zl'=2,'y'=8,'x'=8,'zh'=4,'c'=2] {'c'}, dimensions={0}, use_global_device_ids=true | all-gather | bytes 196608 | tf_op jit(solution)/shard_map/all_gather | solution.py:101
  56.5 5.4 %all-gather.1 = bf16[128,256]{1,0:T(8,128)(2,1)S(1)} all-gather(bf16[64,256]{1,0:T(8,128)(2,1)S(1)} %get-tuple-element.20), channel_id=3, replica_groups=mesh['zl'=2,'y'=8,'x'=8,'zh'=4,'c'=2] {'zl'}, dimensions={0}, use_global_device_ids=true | all-gather | bytes 98304 | tf_op jit(solution)/shard_map/all_gather | solution.py:104
  61.9 3.4 %collective-permute-start.5 = (bf16[128,1024]{1,0:T(8,128)(2,1)S(1)}, bf16[128,1024]{1,0:T(8,128)(2,1)S(1)}, u32[]{:S(2)}, u32[]{:S(2)}) collective-permute-start(bf16[128,1024]{1,0:T(8,128)(2,1)S(1)} %get-tuple-element.24), channel_id=1, source_target_pairs={{0,512},{512,0},{1,513},{513,1},{2,514},{514,2},{3,515},{515,3},{4... | collective-permute-start | bytes 786440 | tf_op jit(solution)/shard_map/ppermute | solution.py:111
  65.3 13.4 %collective-permute-start.4 = (bf16[64,512]{1,0:T(8,128)(2,1)S(1)}, bf16[64,512]{1,0:T(8,128)(2,1)S(1)}, u32[]{:S(2)}, u32[]{:S(2)}) collective-permute-start(bf16[64,512]{1,0:T(8,128)(2,1)S(1)} %maximum_select_fusion), channel_id=1, source_target_pairs={{0,4},{2,6},{4,0},{6,2},{1,5},{3,7},{5,1},{7,3},{8,12},{10,14},{12... | collective-permute-start | bytes 196616 | tf_op jit(solution)/shard_map/ppermute | solution.py:113
  78.7 5.8 %collective-permute-start.3 = (bf16[64,512]{1,0:T(8,128)(2,1)S(1)}, bf16[64,512]{1,0:T(8,128)(2,1)S(1)}, u32[]{:S(2)}, u32[]{:S(2)}) collective-permute-start(bf16[64,512]{1,0:T(8,128)(2,1)S(1)} %maximum_select_fusion), channel_id=1, source_target_pairs={{0,2},{2,4},{4,6},{6,0},{1,3},{3,5},{5,7},{7,1},{8,10},{10,12},{12... | collective-permute-start | bytes 196616 | tf_op jit(solution)/shard_map/ppermute | solution.py:113
  84.5 1.9 %collective-permute-start.2 = (bf16[64,512]{1,0:T(8,128)(2,1)S(1)}, bf16[64,512]{1,0:T(8,128)(2,1)S(1)}, u32[]{:S(2)}, u32[]{:S(2)}) collective-permute-start(bf16[64,512]{1,0:T(8,128)(2,1)S(1)} %maximum_select_fusion), channel_id=1, source_target_pairs={{0,6},{2,0},{4,2},{6,4},{1,7},{3,1},{5,3},{7,5},{8,14},{10,8},{12,... | collective-permute-start | bytes 196616 | tf_op jit(solution)/shard_map/ppermute | solution.py:113
  86.5 1.9 %collective-permute-start.6 = (bf16[128,1024]{1,0:T(8,128)(2,1)S(1)}, bf16[128,1024]{1,0:T(8,128)(2,1)S(1)}, u32[]{:S(2)}, u32[]{:S(2)}) collective-permute-start(bf16[128,1024]{1,0:T(8,128)(2,1)S(1)} %get-tuple-element.29), channel_id=1, source_target_pairs={{0,512},{512,0},{1,513},{513,1},{2,514},{514,2},{3,515},{515,3},{4... | collective-permute-start | bytes 786440 | tf_op jit(solution)/shard_map/ppermute | solution.py:111
  88.4 0.0 all-to-all-done.1
  88.4 2.3 %convert_reduce_fusion = f32[4,2048]{1,0:T(4,128)} fusion(bf16[64,4,2048]{2,1,0:T(4,128)(2,1)} %all-to-all-done.1), kind=kLoop, calls=%fused_computation.2 | loop fusion | flops 1040384 | bytes 1081344 | tf_op jit(solution)/shard_map/reduce_sum | solution.py:116
  90.7 0.0 collective-permute-done.4
  90.7 0.0 collective-permute-done.3
  90.7 0.5 collective-permute-done.2
  91.2 0.0 collective-permute-done.5.a_ref
  91.3 0.2 subtract_convert_fusion.1
  91.4 0.1 pad_maximum_fusion.1
  91.6 4.5 %all_gather.19 = bf16[128,512]{1,0:T(8,128)(2,1)S(1)} all-gather(bf16[64,512]{1,0:T(8,128)(2,1)S(1)} %bitcast.18), channel_id=1, replica_groups=mesh['zl'=2,'y'=8,'x'=8,'zh'=4,'c'=2] {'c'}, dimensions={0}, use_global_device_ids=true | all-gather | bytes 196608 | tf_op jit(solution)/shard_map/all_gather | solution.py:124
  96.1 0.0 collective-permute-done.6.b_ref
  96.1 1.1 %grad.1 = bf16[128,2048]{1,0:T(8,128)(2,1)} custom-call(bf16[128,256]{1,0:T(8,128)(2,1)S(1)} %get-tuple-element.35.kb_ref, bf16[256,2048]{1,0:T(8,128)(2,1)S(1)} %reshape.91.w_ref, bf16[128,1024]{1,0:T(8,128)(2,1)S(1)} %collective-permute-done.5.a_ref, bf16[128,1024]{1,0:T(8,128)(2,1)S(1)} %collective-permute-done.6.b_ref), custom_call_target="tpu_custom_call" | custom-call | tf_op jit(solution)/shard_map/grad/pallas_call | solution.py:126
  97.2 0.7 copy.14
  (11 shorter events, 0.2 us)
Async XLA Ops:
  0.6 16.0 %copy-start = (bf16[128,2048]{1,0:T(8,128)(2,1)S(1)}, bf16[128,2048]{1,0:T(8,128)(2,1)}, u32[]{:S(2)}) copy-start(bf16[128,2048]{1,0:T(8,128)(2,1)} %tok_ref.1) | copy-start | bytes 1572868
  0.6 0.8 copy-start.1
  1.4 20.1 %copy-start.2 = (bf16[128,512]{1,0:T(8,128)(2,1)S(1)}, bf16[128,512]{1,0:T(8,128)(2,1)}, u32[]{:S(2)}) copy-start(bf16[128,512]{1,0:T(8,128)(2,1)} %param.7) | copy-start | bytes 393220
  1.4 20.2 %copy-start.3 = (s32[1,128]{1,0:T(1,128)S(1)}, s32[1,128]{1,0:T(1,128)}, u32[]{:S(2)}) copy-start(s32[1,128]{1,0:T(1,128)} %param.5) | copy-start | bytes 1540
  2.5 37.6 %all-to-all-start = ((bf16[64,4,2048]{2,1,0:T(4,128)(2,1)}), bf16[64,4,2048]{2,1,0:T(4,128)(2,1)S(1)}, u32[]{:S(2)}, u32[]{:S(2)}) async-start(bf16[64,4,2048]{2,1,0:T(4,128)(2,1)} %spread.1), calls=%async_computation | async-start | bytes 2097152 | tf_op jit(solution)/shard_map/all_to_all | solution.py:83
  16.6 16.0 %collective-permute-start = (bf16[128,2048]{1,0:T(8,128)(2,1)S(1)}, bf16[128,2048]{1,0:T(8,128)(2,1)S(1)}, u32[]{:S(2)}, u32[]{:S(2)}) collective-permute-start(bf16[128,2048]{1,0:T(8,128)(2,1)S(1)} %copy-done), channel_id=1, source_target_pairs={{0,512},{512,0},{1,513},{513,1},{2,514},{514,2},{3,515},{515,3},{4... | collective-permute-start | bytes 1572872 | tf_op jit(solution)/shard_map/ppermute | solution.py:84
  22.7 9.9 %collective-permute-start.1 = (bf16[128,256]{1,0:T(8,128)(2,1)S(1)}, bf16[128,256]{1,0:T(8,128)(2,1)S(1)}, u32[]{:S(2)}, u32[]{:S(2)}) collective-permute-start(bf16[128,256]{1,0:T(8,128)(2,1)S(1)} %get-tuple-element.36), channel_id=1, source_target_pairs={{0,512},{512,0},{1,513},{513,1},{2,514},{514,2},{3,515},{515,3},{4... | collective-permute-start | bytes 196616 | tf_op jit(solution)/shard_map/ppermute | solution.py:89
  40.1 48.3 %all-to-all-start.1 = ((bf16[64,4,2048]{2,1,0:T(4,128)(2,1)}), bf16[64,4,2048]{2,1,0:T(4,128)(2,1)}, u32[]{:S(2)}, u32[]{:S(2)}) async-start(bf16[64,4,2048]{2,1,0:T(4,128)(2,1)} %reshape.92), calls=%async_computation.1 | async-start | bytes 2097152 | tf_op jit(solution)/shard_map/all_to_all | solution.py:105
  61.9 29.3 %collective-permute-start.5 = (bf16[128,1024]{1,0:T(8,128)(2,1)S(1)}, bf16[128,1024]{1,0:T(8,128)(2,1)S(1)}, u32[]{:S(2)}, u32[]{:S(2)}) collective-permute-start(bf16[128,1024]{1,0:T(8,128)(2,1)S(1)} %get-tuple-element.24), channel_id=1, source_target_pairs={{0,512},{512,0},{1,513},{513,1},{2,514},{514,2},{3,515},{515,3},{4... | collective-permute-start | bytes 786440 | tf_op jit(solution)/shard_map/ppermute | solution.py:111
  65.3 25.4 %collective-permute-start.4 = (bf16[64,512]{1,0:T(8,128)(2,1)S(1)}, bf16[64,512]{1,0:T(8,128)(2,1)S(1)}, u32[]{:S(2)}, u32[]{:S(2)}) collective-permute-start(bf16[64,512]{1,0:T(8,128)(2,1)S(1)} %maximum_select_fusion), channel_id=1, source_target_pairs={{0,4},{2,6},{4,0},{6,2},{1,5},{3,7},{5,1},{7,3},{8,12},{10,14},{12... | collective-permute-start | bytes 196616 | tf_op jit(solution)/shard_map/ppermute | solution.py:113
  78.7 12.0 %collective-permute-start.3 = (bf16[64,512]{1,0:T(8,128)(2,1)S(1)}, bf16[64,512]{1,0:T(8,128)(2,1)S(1)}, u32[]{:S(2)}, u32[]{:S(2)}) collective-permute-start(bf16[64,512]{1,0:T(8,128)(2,1)S(1)} %maximum_select_fusion), channel_id=1, source_target_pairs={{0,2},{2,4},{4,6},{6,0},{1,3},{3,5},{5,7},{7,1},{8,10},{10,12},{12... | collective-permute-start | bytes 196616 | tf_op jit(solution)/shard_map/ppermute | solution.py:113
  84.5 6.6 %collective-permute-start.2 = (bf16[64,512]{1,0:T(8,128)(2,1)S(1)}, bf16[64,512]{1,0:T(8,128)(2,1)S(1)}, u32[]{:S(2)}, u32[]{:S(2)}) collective-permute-start(bf16[64,512]{1,0:T(8,128)(2,1)S(1)} %maximum_select_fusion), channel_id=1, source_target_pairs={{0,6},{2,0},{4,2},{6,4},{1,7},{3,1},{5,3},{7,5},{8,14},{10,8},{12,... | collective-permute-start | bytes 196616 | tf_op jit(solution)/shard_map/ppermute | solution.py:113
  86.5 9.6 %collective-permute-start.6 = (bf16[128,1024]{1,0:T(8,128)(2,1)S(1)}, bf16[128,1024]{1,0:T(8,128)(2,1)S(1)}, u32[]{:S(2)}, u32[]{:S(2)}) collective-permute-start(bf16[128,1024]{1,0:T(8,128)(2,1)S(1)} %get-tuple-element.29), channel_id=1, source_target_pairs={{0,512},{512,0},{1,513},{513,1},{2,514},{514,2},{3,515},{515,3},{4... | collective-permute-start | bytes 786440 | tf_op jit(solution)/shard_map/ppermute | solution.py:111
